TPU v7x, 32 devices: a whole 2x2x4 slice. The times are simulated.
32 devices in a mesh: groups: 2 (over x), ctx: 4 (over y, core), heads: 4 (over z).
Axes of the slice: x: 2, y: 2, z: 4, core: 2. Of those that a mesh axis runs over, the one named last changes fastest.
Arguments:
- tokens: bfloat16 [4096, 2048], P(('groups', 'ctx', 'heads')), parts along dimension 0, may hold values from -60 to 60
- state_in: float32 [4, 256, 128], P('heads', 'groups'), parts along dimension 1, may hold values from -256 to 256
- past_kv: bfloat16 [2, 1024, 512], P(None, 'groups', 'heads'), parts along dimension 1, may hold values from -6 to 6
- w_qkv: bfloat16 [2048, 3, 512], P(None, None, 'heads'), may hold values from -0.125 to 0.125
- w_out: bfloat16 [512, 2048], P('heads'), may hold values from -0.25 to 0.25
- w_gate: bfloat16 [16, 2048, 768], P(('ctx', 'heads')), may hold values from -0.125 to 0.125
- w_up: bfloat16 [16, 2048, 768], P(('ctx', 'heads')), may hold values from -0.125 to 0.125
- w_down: bfloat16 [16, 768, 2048], P(('ctx', 'heads')), may hold values from -0.21875 to 0.21875
- expert_ids: int32 [4096, 8], P(('groups', 'ctx', 'heads')), parts along dimension 0, may hold values from 0 to 15, all different within a row; in each aligned block of 128 rows (0 to 127, 128 to 255, ...) at most 128 rows name the same one
- gate_weights: float32 [4096, 8], P(('groups', 'ctx', 'heads')), parts along dimension 0, may hold values from 0.1 to 1
Outputs:
- mixed: bfloat16 [4096, 2048], P(('groups', 'ctx', 'heads')), parts along dimension 0
There are 2 independent parts, one for each index of `groups`. A program takes and returns all parts, laid end to end along the dimension named above; an argument that names none is the same for every part. Nothing has to cross between parts.
Inputs may be any that keep to these rules, and one draw needn't show every extreme that they name: `expert_ids`: each row names 8 different experts; in each aligned block of 128 rows (the rows of one device) no expert is named by more than 128 rows, a bound that some block reaches.
All inputs are finite; a program needn't handle non-finite values.
Results may differ from a plain program's by a relative error of at most 0.017.
Values may be sent and summed in bfloat16 or wider, within the bound.
No kernel may reach another device: no remote copies, remote signals or barrier semaphores. Data moves between devices by JAX's collectives and lax.ppermute only.
A program may use at most 128 MiB of HBM per device.

v0:
```python
import math

import jax
import jax.numpy as jnp
from jax import lax
from jax.sharding import PartitionSpec as P

HDIM = 128
WINDOW = 512


def entering(x, axis, join, neutral):
    place = lax.axis_index(axis)
    gathered = lax.all_gather(x.astype(jnp.bfloat16), axis)
    state = jnp.zeros_like(x) + jnp.asarray(neutral, x.dtype)

    def one(lap, state):
        return join(state, lax.dynamic_index_in_dim(gathered, lap, 0, False).astype(x.dtype))

    return lax.fori_loop(0, place, one, state)


def from_behind(block, axis, distance):
    devices = range(lax.axis_size(axis))
    route = [(i - distance, i) for i in devices if i - distance in devices]
    return lax.ppermute(block, axis, route)


def normalize(value):
    return value * lax.rsqrt(jnp.mean(value * value, axis=-1, keepdims=True) + 1e-06)


def on_device(
    tokens, state_in, past_kv, w_qkv, w_out, w_gate, w_up, w_down, expert_ids, gate_weights
):
    row_count, model_width = tokens.shape
    inner_width = w_qkv.shape[2]
    local_heads = inner_width // HDIM
    w_flat = w_qkv.reshape(model_width, 3 * inner_width)
    projected = jnp.dot(
        lax.all_gather(tokens, "heads", axis=0, tiled=True),
        w_flat,
        preferred_element_type=jnp.float32,
    ).astype(jnp.bfloat16)
    slab_rows = projected.shape[0]
    projected = projected.reshape(slab_rows, 3, local_heads, HDIM)
    query = jnp.transpose(projected[:, 0], (1, 0, 2))
    keys = jnp.transpose(projected[:, 1], (1, 0, 2))
    values = jnp.transpose(projected[:, 2], (1, 0, 2))
    local_state = jnp.einsum("hsd,hse->hde", keys, values, preferred_element_type=jnp.float32)
    earlier_state = entering(
        local_state, "ctx", lambda first, second: first + second, jnp.zeros_like(local_state)
    )
    start_state = state_in + earlier_state
    tail = jnp.stack([keys, values], axis=0)
    arrived = from_behind(tail, "ctx", 1)
    past = jnp.transpose(past_kv.reshape(2, WINDOW, local_heads, HDIM), (0, 2, 1, 3))
    previous = jnp.where(lax.axis_index("ctx") == 0, past, arrived)
    all_keys = jnp.concatenate([previous[0], keys], axis=1)
    all_values = jnp.concatenate([previous[1], values], axis=1)
    block_rows = min(slab_rows, 512)
    block_count = slab_rows // block_rows
    scale = 1.0 / math.sqrt(HDIM)
    causal = jnp.arange(block_rows)[:, None] >= jnp.arange(block_rows)[None, :]
    offsets = jnp.arange(WINDOW + block_rows)[None, :] - jnp.arange(block_rows)[:, None]
    in_window = (offsets > 0) & (offsets <= WINDOW)

    def block_step(state, index):
        first = index * block_rows
        carried = jnp.einsum(
            "hsd,hde->hse", query.astype(jnp.float32), state, precision=lax.Precision.HIGHEST
        )
        inside = jnp.einsum("hsd,htd->hst", query, keys, preferred_element_type=jnp.float32)
        inside = jnp.where(causal[None], inside, 0.0).astype(jnp.bfloat16)
        linear = carried + jnp.einsum(
            "hst,hte->hse", inside, values, preferred_element_type=jnp.float32
        )
        scores = (
            jnp.einsum("hsd,htd->hst", query, all_keys, preferred_element_type=jnp.float32) * scale
        )
        scores = jnp.where(in_window[None], scores, -jnp.inf)
        top_score = jnp.max(scores, axis=-1, keepdims=True)
        expo = jnp.exp(scores - top_score)
        probs = (expo / jnp.sum(expo, axis=-1, keepdims=True)).astype(jnp.bfloat16)
        window_out = jnp.einsum(
            "hst,hte->hse", probs, all_values, preferred_element_type=jnp.float32
        )
        combined = (normalize(linear) + window_out).astype(jnp.bfloat16)
        new_state = state + jnp.einsum(
            "hsd,hse->hde", keys, values, preferred_element_type=jnp.float32
        )
        return (new_state, combined)

    _, outs = lax.scan(block_step, start_state, jnp.arange(block_count, dtype=jnp.int32))
    heads_out = jnp.transpose(outs, (0, 2, 1, 3)).reshape(slab_rows, inner_width)
    regrouped = lax.all_to_all(heads_out, "heads", split_axis=0, concat_axis=1, tiled=True)
    attn = jnp.dot(
        regrouped,
        lax.all_gather(w_out, "heads", axis=0, tiled=True),
        preferred_element_type=jnp.float32,
    )
    hidden_state = (tokens.astype(jnp.float32) + attn).astype(jnp.bfloat16)
    hidden_float = hidden_state.astype(jnp.float32)
    normed = normalize(hidden_float).astype(jnp.bfloat16)
    ctx_count = lax.axis_size("ctx")
    head_count = lax.axis_size("heads")
    exp_local = w_gate.shape[0]
    expert_count = exp_local * ctx_count * head_count
    top_count = expert_ids.shape[1]
    capacity = max(2, 2 * row_count * top_count // expert_count)
    picks = expert_ids.reshape(-1)
    onehot = (picks[:, None] == jnp.arange(expert_count, dtype=jnp.int32)[None, :]).astype(
        jnp.int32
    )
    earlier = jnp.cumsum(onehot, axis=0) - onehot
    slots = jnp.sum(onehot * earlier, axis=1)
    destination = picks * capacity + slots
    source_rows = jnp.arange(row_count * top_count, dtype=jnp.int32) // top_count
    outgoing = jnp.zeros((expert_count * capacity, model_width), jnp.bfloat16)
    outgoing = outgoing.at[destination].set(normed[source_rows])
    sendable = outgoing.reshape(expert_count, 1, capacity, model_width)
    arrived_rows = lax.all_to_all(
        sendable, ("ctx", "heads"), split_axis=0, concat_axis=1, tiled=True
    )
    e_count, n_count, c_count, d_count = arrived_rows.shape
    flat = arrived_rows.reshape(e_count, n_count * c_count, d_count)
    gate_act = jnp.einsum("erd,edf->erf", flat, w_gate, preferred_element_type=jnp.float32)
    up_act = jnp.einsum("erd,edf->erf", flat, w_up, preferred_element_type=jnp.float32)
    hid = (jax.nn.silu(gate_act) * up_act).astype(jnp.bfloat16)
    out_rows = jnp.einsum("erf,efd->erd", hid, w_down, preferred_element_type=jnp.float32)
    finished = out_rows.astype(jnp.bfloat16).reshape(e_count, n_count, c_count, d_count)
    returned = lax.all_to_all(finished, ("ctx", "heads"), split_axis=1, concat_axis=0, tiled=True)
    returned = returned.reshape(expert_count * capacity, model_width)
    picked = returned[destination].reshape(row_count, top_count, model_width).astype(jnp.float32)
    routed = jnp.sum(gate_weights[:, :, None] * picked, axis=1)
    return (hidden_float + routed).astype(jnp.bfloat16)


def solution(mesh):
    return jax.shard_map(
        on_device,
        mesh=mesh,
        in_specs=(
            P(("groups", "ctx", "heads"), None),
            P("heads", "groups", None),
            P(None, "groups", "heads"),
            P(None, None, "heads"),
            P("heads", None),
            P(("ctx", "heads"), None, None),
            P(("ctx", "heads"), None, None),
            P(("ctx", "heads"), None, None),
            P(("groups", "ctx", "heads"), None),
            P(("groups", "ctx", "heads"), None),
        ),
        out_specs=P(("groups", "ctx", "heads"), None),
        check_vma=False,
    )
```

profile of v0, /device:TPU:0, one launch (start us, length us, event | category | flops | bytes accessed | tf_op | source)
XLA Modules:
  0.0 574.0 jit_solution(15762192888532435691)
XLA Ops:
  6.5 0.7 all-gather.4.cloned.1.call-update
  7.3 0.0 all-gather.6.cloned.1.call-start
  7.3 0.7 all-gather.6.cloned.1.call-update
  8.0 0.8 copy.41
  8.8 0.1 eq.33
  8.9 0.1 eq.29
  9.0 0.7 broadcast_multiply_fusion
  9.7 2.6 copy.32
  12.3 4.5 reduce-window.6
  16.9 0.1 slice.37
  16.9 0.1 copy.43
  17.1 0.1 copy.44
  17.2 0.1 broadcast_add_fusion
  17.3 0.1 copy.40
  17.4 0.1 mul.73
  17.5 40.1 %all-gather.4.cloned.1.call-done = bf16[512,2048]{1,0:T(8,128)(2,1)} async-done(((bf16[128,2048]{1,0:T(8,128)(2,1)}), bf16[512,2048]{1,0:T(8,128)(2,1)}) %all-gather.4.cloned.1.call-update) | async-done | bytes 2097168 | tf_op jit(solution)/shard_map/all_gather | solution.py:41
  57.6 3.1 convolution_convert_fusion.1
  60.7 0.0 copy-start.7
  60.7 0.7 fusion.46
  61.4 0.8 convolution_convert_fusion.2
  62.2 0.1 copy.46
  62.4 1.1 copy.47
  63.4 0.8 pad_maximum_fusion
  64.2 2.4 collective-permute-start
  66.6 6.0 %all-gather = bf16[512,128]{1,0:T(8,128)(2,1)S(1)} all-gather(bf16[128,128]{1,0:T(8,128)(2,1)} %convolution_convert_fusion.2), channel_id=2, replica_groups=mesh['groups'=2,'ctx'=4,'heads'=4] {'ctx'}, dimensions={0}, use_global_device_ids=true | all-gather | bytes 163840 | tf_op jit(solution)/shard_map/all_gather | solution.py:14
  72.7 2.0 fusion.30
  74.7 2.3 multiply_reduce_fusion.1
  77.0 1.1 bitcast_select_fusion
  78.1 1.5 fusion.47
  79.6 0.5 fusion.15
  80.2 0.6 fusion.19
  80.7 0.8 copy.38
  81.5 3.5 all-to-all-start
  85.0 21.6 %all-gather.6.cloned.1.call-done = bf16[512,2048]{1,0:T(8,128)(2,1)} async-done(((bf16[128,2048]{1,0:T(8,128)(2,1)}), bf16[512,2048]{1,0:T(8,128)(2,1)}) %all-gather.6.cloned.1.call-update) | async-done | bytes 2097168 | tf_op jit(solution)/shard_map/all_gather | solution.py:99
  106.6 2.2 multiply_reduce_fusion
  108.9 1.0 copy-done.2
  109.9 0.9 multiply_convert_fusion.1
  110.8 24.7 %scatter_custom_fusion = bf16[2048,2048]{1,0:T(8,128)(2,1)} fusion(s32[1024]{0:T(1024)S(1)} %bitcast.134, bf16[128,2048]{1,0:T(8,128)(2,1)} %multiply_convert_fusion.1, s32[1024]{0:T(1024)S(1)} %broadcast_clamp_fusion.1, bf16[]{:T(256)} %constant.69.clone.1), kind=kCustom, calls=%fused_computation.8 | custom fusion | bytes 8389120 | tf_op jit(solution)/shard_map/scatter | solution.py:120
  135.5 188.5 %all_to_all.37 = bf16[16,1,128,2048]{3,2,1,0:T(8,128)(2,1)S(1)} all-to-all(bf16[16,1,128,2048]{3,2,1,0:T(8,128)(2,1)} %bitcast.113), channel_id=1, replica_groups=mesh['groups'=2,'ctx'=4,'heads'=4] {'ctx','heads'}, dimensions={0} | all-to-all | bytes 16777216 | tf_op jit(solution)/shard_map/all_to_all | solution.py:122
  324.0 3.2 copy-done.4
  327.2 8.5 %fusion.7 = f32[2048,768]{1,0:T(8,128)} fusion(bf16[2048,2048]{1,0:T(8,128)(2,1)S(1)} %bitcast.115, bf16[1,2048,768]{2,1,0:T(8,128)(2,1)S(1)} %copy-done.10), kind=kOutput, calls=%fused_computation.13 | convolution fusion | flops 6442450944 | bytes 17825792 | tf_op jit(solution)/shard_map/erd,edf->erf/dot_general | solution.py:127
  335.8 21.3 %convolution_convert_fusion = bf16[2048,2048]{1,0:T(8,128)(2,1)} fusion(f32[2048,768]{1,0:T(8,128)} %fusion.7, bf16[2048,2048]{1,0:T(8,128)(2,1)} %bitcast.116, bf16[1,768,2048]{2,1,0:T(8,128)(2,1)S(1)} %copy-done, bf16[1,2048,768]{2,1,0:T(8,128)(2,1)} %param.18), kind=kOutput, calls=%fused_computation.6 | convolution fusion | flops 12898533376 | bytes 29360128 | tf_op jit(solution)/shard_map/erf,efd->erd/dot_general | solution.py:130
  357.0 5.2 all-to-all-start.2
  362.2 0.1 copy.39
  362.3 183.9 %all-to-all-done.2 = bf16[1,16,128,2048]{3,2,0,1:T(8,128)(2,1)} async-done(((bf16[1,16,128,2048]{3,2,0,1:T(8,128)(2,1)}), bf16[1,16,128,2048]{3,2,0,1:T(8,128)(2,1)}, u32[]{:S(2)}, u32[]{:S(2)}) %all-to-all-start.2) | async-done | bytes 8388640 | tf_op jit(solution)/shard_map/all_to_all | solution.py:132
  546.2 13.4 %gather_fusion = bf16[1024,2048]{1,0:T(8,128)(2,1)} fusion(bf16[2048,2048]{1,0:T(8,128)(2,1)} %bitcast.35, s32[1024]{0:T(1024)S(1)} %broadcast_clamp_fusion), kind=kCustom, calls=%fused_computation.1 | custom fusion | bytes 8392704 | tf_op jit(solution)/shard_map/gather | solution.py:134
  559.6 6.6 %fusion = f32[128,2048]{1,0:T(8,128)S(1)} fusion(bf16[1024,2048]{1,0:T(8,128)(2,1)} %gather_fusion, f32[128,8]{1,0:T(8,128)S(1)} %copy.39), kind=kLoop, calls=%fused_computation.5 | loop fusion | flops 6029312 | bytes 5246976 | tf_op jit(solution)/shard_map/reduce_sum | solution.py:135
  566.3 0.9 add_convert_fusion
  (38 shorter events, 0.2 us)
Async XLA Ops:
  6.5 329.2 %copy-start = (bf16[1,768,2048]{2,1,0:T(8,128)(2,1)S(1)}, bf16[1,768,2048]{2,1,0:T(8,128)(2,1)}, u32[]{:S(2)}) copy-start(bf16[1,768,2048]{2,1,0:T(8,128)(2,1)} %param.19) | copy-start | bytes 9437188
  6.5 51.1 %all-gather.4.cloned.1.call-start = ((), (), s32[]{:S(2)}) async-start(), calls=%async_computation.3 | async-start | bytes 2621440 | tf_op jit(solution)/shard_map/all_gather | solution.py:41
  7.3 99.4 %all-gather.6.cloned.1.call-start = ((), (), s32[]{:S(2)}) async-start(), calls=%async_computation.4 | async-start | bytes 2621440 | tf_op jit(solution)/shard_map/all_gather | solution.py:99
  57.6 15.1 %copy-start.8 = (f32[1,128,128]{2,1,0:T(8,128)S(1)}, f32[1,128,128]{2,1,0:T(8,128)}, u32[]{:S(2)}) copy-start(f32[1,128,128]{2,1,0:T(8,128)} %param.13) | copy-start | bytes 196612
  60.7 1.5 copy-start.7
  62.4 1.8 copy-start.5
  64.2 12.8 %collective-permute-start = (bf16[2,1,512,128]{3,2,1,0:T(8,128)(2,1)}, bf16[2,1,512,128]{3,2,1,0:T(8,128)(2,1)}, u32[]{:S(2)}, u32[]{:S(2)}) collective-permute-start(bf16[2,1,512,128]{3,2,1,0:T(8,128)(2,1)} %pad_maximum_fusion), channel_id=1, source_target_pairs={{0,4},{4,8},{8,12},{1,5},{5,9},{9,13},{2,6},{6,10},{10,14},{3,7},{... | collective-permute-start | bytes 786440 | tf_op jit(solution)/shard_map/ppermute | solution.py:26
  72.7 5.4 copy-start.6
  78.1 2.1 copy-start.11
  81.5 25.1 %all-to-all-start = ((bf16[4,128,128]{1,2,0:T(8,128)(2,1)}), bf16[4,128,128]{1,2,0:T(8,128)(2,1)S(1)}, u32[]{:S(2)}, u32[]{:S(2)}) async-start(bf16[4,128,128]{1,2,0:T(8,128)(2,1)} %copy.38), calls=%async_computation | async-start | bytes 262144 | tf_op jit(solution)/shard_map/all_to_all | solution.py:96
  108.9 1.0 copy-start.2
  135.5 191.7 %copy-start.10 = (bf16[1,2048,768]{2,1,0:T(8,128)(2,1)S(1)}, bf16[1,2048,768]{2,1,0:T(8,128)(2,1)}, u32[]{:S(2)}) copy-start(bf16[1,2048,768]{2,1,0:T(8,128)(2,1)} %param.17) | copy-start | bytes 9437188
  324.0 3.2 copy-start.4
  357.0 5.2 copy-start.9
  357.0 189.2 %all-to-all-start.2 = ((bf16[1,16,128,2048]{3,2,0,1:T(8,128)(2,1)}), bf16[1,16,128,2048]{3,2,0,1:T(8,128)(2,1)}, u32[]{:S(2)}, u32[]{:S(2)}) async-start(bf16[1,16,128,2048]{3,2,0,1:T(8,128)(2,1)} %bitcast.114), calls=%async_computation.2 | async-start | bytes 16777216 | tf_op jit(solution)/shard_map/all_to_all | solution.py:132
  546.2 21.0 %copy-start.1 = (bf16[1,768,2048]{2,1,0:T(8,128)(2,1)S(1)}, bf16[1,768,2048]{2,1,0:T(8,128)(2,1)}, u32[]{:S(2)}) copy-start(bf16[1,768,2048]{2,1,0:T(8,128)(2,1)} %param.19) | copy-start | bytes 9437188
  559.6 6.6 %copy-start.3 = (f32[128,2048]{1,0:T(8,128)S(1)}, f32[128,2048]{1,0:T(8,128)}, u32[]{:S(2)}) copy-start(f32[128,2048]{1,0:T(8,128)} %copy-done.2) | copy-start | bytes 3145732
Sparse Core Ops, SparseCore 0:
  8.9 48.6 all-gather.3
  59.2 47.4 all-gather.5
where the time goes:
time: 575 us; the launch traced here: 574 us
  waiting for transfers between devices  247 us (43%)
  blocking collectives  195 us (34%)
  local copies, waits for them, and re-layouts  49.3 us (9%)
  matrix products  42.2 us (7%)
  other arithmetic  16.2 us (3%)
  between operations  13.6 us (2%)
  starting transfers between devices  11.2 us (2%)
    all_to_all x1, blocking collectives, on_device(): lax.all_to_all(sendable, ('ctx', 'heads'), split_axis=0, concat_axis=1, t...  188 us
    all_to_all x1, waiting for transfers between devices, on_device(): lax.all_to_all(finished, ('ctx', 'heads'), split_axis=1, concat_axis=0, t...  184 us
    all_gather x1, waiting for transfers between devices, on_device(): lax.all_gather(tokens, 'heads', axis=0, tiled=True)  40.1 us
    scatter x1, local copies, waits for them, and re-layouts, on_device(): outgoing = outgoing.at[destination].set(normed[source_rows])  24.7 us
    all_gather x1, waiting for transfers between devices, on_device(): lax.all_gather(w_out, 'heads', axis=0, tiled=True)  21.6 us
    dot_general x1, matrix products, on_device(): jnp.einsum('erf,efd->erd', hid, w_down, preferred_element_type=jnp.float32)  21.3 us
    gather x1, local copies, waits for them, and re-layouts, on_device(): returned[destination].reshape(row_count, top_count, model_width)  13.4 us
  transfers between devices with their start and end apart: 5, of which 3 were waited for; matrix products, arithmetic and copies ran while one was open for 4% of the time, Pallas kernels for 0%

commit v1 on v0

--- a/solution.py
+++ b/solution.py
@@ -30,7 +30,7 @@
     return value * lax.rsqrt(jnp.mean(value * value, axis=-1, keepdims=True) + 1e-06)
 
 
-def on_device(
+def on_device_routed(
     tokens, state_in, past_kv, w_qkv, w_out, w_gate, w_up, w_down, expert_ids, gate_weights
 ):
     row_count, model_width = tokens.shape
@@ -136,7 +136,190 @@
     return (hidden_float + routed).astype(jnp.bfloat16)
 
 
+def ring_pairs(count, step):
+    return [(i, (i + step) % count) for i in range(count)]
+
+
+def partner_pairs(count, bit):
+    return [(i, i ^ bit) for i in range(count)]
+
+
+def gather_ring(block, count):
+    blocks = [block]
+    for _ in range(count - 1):
+        blocks.append(lax.ppermute(blocks[-1], "heads", ring_pairs(count, 1)))
+    return blocks
+
+
+def gather_direct(block, count):
+    return [block] + [
+        lax.ppermute(block, "heads", ring_pairs(count, step)) for step in range(1, count)
+    ]
+
+
+def flip_row(block, ctx_count):
+    return lax.ppermute(block, "ctx", partner_pairs(ctx_count, 2))
+
+
+def flip_core(block, ctx_count):
+    return lax.ppermute(block, "ctx", partner_pairs(ctx_count, 1))
+
+
+def gather_w_out(w_out, head_count, ctx_count, group_count):
+    rows = w_out.shape[0]
+    parts = 2 * group_count
+    piece_rows = rows // parts
+    core = lax.axis_index("ctx") % 2
+    place = core * group_count + lax.axis_index("groups")
+    piece = lax.dynamic_slice_in_dim(w_out, place * piece_rows, piece_rows, 0)
+    own = jnp.stack(gather_direct(piece, head_count), axis=0)[:, None]
+    if group_count == 2:
+        other = lax.ppermute(own, "groups", [(0, 1), (1, 0)])
+        first = lax.axis_index("groups") == 0
+        own = jnp.concatenate(
+            [jnp.where(first, own, other), jnp.where(first, other, own)], axis=1
+        )
+    other = flip_core(own, ctx_count)
+    own = jnp.concatenate(
+        [jnp.where(core == 0, own, other), jnp.where(core == 0, other, own)], axis=1
+    )
+    return own.reshape(head_count * rows, w_out.shape[1])
+
+
+def on_device_dense(
+    tokens, state_in, past_kv, w_qkv, w_out, w_gate, w_up, w_down, expert_ids, gate_weights
+):
+    row_count, model_width = tokens.shape
+    head_count = lax.axis_size("heads")
+    ctx_count = lax.axis_size("ctx")
+    group_count = lax.axis_size("groups")
+    ctx = lax.axis_index("ctx")
+    place = lax.axis_index("heads")
+    slab_rows = row_count * head_count
+    expert_count = ctx_count * head_count
+    starts = [((place - s) % head_count) * row_count for s in range(head_count)]
+
+    hit = expert_ids[:, :, None] == jnp.arange(expert_count, dtype=jnp.int32)[None, None, :]
+    dense_weights = jnp.sum(jnp.where(hit, gate_weights[:, :, None], 0.0), axis=1)
+    all_weights = lax.all_gather(dense_weights, ("ctx", "heads"), axis=0, tiled=True)
+    all_weights = all_weights.reshape(ctx_count, slab_rows, expert_count)
+
+    blocks = gather_ring(tokens, head_count)
+    w_flat = w_qkv.reshape(model_width, 3 * HDIM)
+    projected = jnp.zeros((slab_rows, 3 * HDIM), jnp.bfloat16)
+    for s in range(head_count):
+        part = jnp.dot(blocks[s], w_flat, preferred_element_type=jnp.float32)
+        projected = lax.dynamic_update_slice_in_dim(
+            projected, part.astype(jnp.bfloat16), starts[s], 0
+        )
+    across = [flip_row(block, ctx_count) for block in blocks]
+    w_out_all = gather_w_out(w_out, head_count, ctx_count, group_count)
+    experts = [
+        (w_gate[0], w_up[0], w_down[0]),
+        tuple(flip_core(w[0], ctx_count) for w in (w_gate, w_up, w_down)),
+    ]
+
+    query = projected[:, :HDIM]
+    keys = projected[:, HDIM : 2 * HDIM]
+    values = projected[:, 2 * HDIM :]
+    local_state = jnp.dot(keys.T, values, preferred_element_type=jnp.float32)
+    arrived = from_behind(projected[:, HDIM:], "ctx", 1)
+    start_state = state_in[0]
+    packed_state = local_state.astype(jnp.bfloat16)
+    for distance in range(1, ctx_count):
+        start_state = start_state + from_behind(packed_state, "ctx", distance).astype(jnp.float32)
+    past = jnp.concatenate([past_kv[0], past_kv[1]], axis=1)
+    previous = jnp.where(ctx == 0, past, arrived)
+    all_keys = jnp.concatenate([previous[:, :HDIM], keys], axis=0)
+    all_values = jnp.concatenate([previous[:, HDIM:], values], axis=0)
+    scale = 1.0 / math.sqrt(HDIM)
+    causal = jnp.arange(slab_rows)[:, None] >= jnp.arange(slab_rows)[None, :]
+    offsets = jnp.arange(WINDOW + slab_rows)[None, :] - jnp.arange(slab_rows)[:, None]
+    in_window = (offsets > 0) & (offsets <= WINDOW)
+    carried = jnp.dot(
+        query.astype(jnp.float32), start_state, precision=lax.Precision.HIGHEST
+    )
+    products = jnp.dot(query, all_keys.T, preferred_element_type=jnp.float32)
+    inside = jnp.where(causal, products[:, WINDOW:], 0.0).astype(jnp.bfloat16)
+    linear = carried + jnp.dot(inside, values, preferred_element_type=jnp.float32)
+    scores = jnp.where(in_window, products * scale, -jnp.inf)
+    expo = jnp.exp(scores - jnp.max(scores, axis=-1, keepdims=True))
+    probs = (expo / jnp.sum(expo, axis=-1, keepdims=True)).astype(jnp.bfloat16)
+    window_out = jnp.dot(probs, all_values, preferred_element_type=jnp.float32)
+    heads_out = (normalize(linear) + window_out).astype(jnp.bfloat16)
+
+    near_heads = gather_direct(heads_out, head_count)
+    far_heads = [flip_row(part, ctx_count) for part in near_heads]
+
+    own_expert = ctx * head_count + place
+    other_expert = (ctx ^ 1) * head_count + place
+
+    def chunk_rows(s):
+        heads_rows = jnp.concatenate(
+            [
+                jnp.concatenate(
+                    [lax.dynamic_slice_in_dim(part, starts[s], row_count, 0) for part in parts],
+                    axis=1,
+                )
+                for parts in (near_heads, far_heads)
+            ],
+            axis=0,
+        )
+        token_rows = jnp.concatenate([blocks[s], across[s]], axis=0)
+        attn = jnp.dot(heads_rows, w_out_all, preferred_element_type=jnp.float32)
+        hidden = (token_rows.astype(jnp.float32) + attn).astype(jnp.bfloat16)
+        return hidden, normalize(hidden.astype(jnp.float32)).astype(jnp.bfloat16)
+
+    def chunk_weights(s, expert):
+        rows = [
+            lax.dynamic_slice(all_weights, (where, starts[s], expert), (1, row_count, 1))
+            for where in (ctx, ctx ^ 2)
+        ]
+        return jnp.concatenate(rows, axis=1)[0]
+
+    def chunk_sum(s, normed):
+        total = 0.0
+        for (gate, up, down), expert in zip(experts, (own_expert, other_expert)):
+            gate_act = jnp.dot(normed, gate, preferred_element_type=jnp.float32)
+            up_act = jnp.dot(normed, up, preferred_element_type=jnp.float32)
+            hid = (jax.nn.silu(gate_act) * up_act).astype(jnp.bfloat16)
+            out_rows = jnp.dot(hid, down, preferred_element_type=jnp.float32)
+            out_rows = out_rows.astype(jnp.bfloat16).astype(jnp.float32)
+            total = total + chunk_weights(s, expert) * out_rows
+        return total.astype(jnp.bfloat16)
+
+    carry = None
+    for s in list(range(1, head_count)) + [0]:
+        hidden, normed = chunk_rows(s)
+        partial = chunk_sum(s, normed)
+        near, far = partial[:row_count], partial[row_count:]
+        joined = near.astype(jnp.float32) + flip_row(far, ctx_count).astype(jnp.float32)
+        if carry is not None:
+            joined = joined + carry.astype(jnp.float32)
+        if s:
+            carry = lax.ppermute(
+                joined.astype(jnp.bfloat16), "heads", ring_pairs(head_count, 1)
+            )
+    return (hidden[:row_count].astype(jnp.float32) + joined).astype(jnp.bfloat16)
+
+
 def solution(mesh):
+    sizes = mesh.shape
+
+    def on_device(*args):
+        w_qkv, w_gate, expert_ids = args[3], args[5], args[8]
+        expert_count = w_gate.shape[0] * sizes["ctx"] * sizes["heads"]
+        slab_rows = args[0].shape[0] * sizes["heads"]
+        dense = (
+            sizes["ctx"] == 4
+            and sizes["groups"] <= 2
+            and w_gate.shape[0] == 1
+            and w_qkv.shape[2] == HDIM
+            and slab_rows == WINDOW
+            and expert_count <= 2 * expert_ids.shape[1]
+        )
+        return (on_device_dense if dense else on_device_routed)(*args)
+
     return jax.shard_map(
         on_device,
         mesh=mesh,

time: 575 us -> 284 us (0.49)
  waiting for transfers between devices: 247 us -> 90.8 us
  blocking collectives: 195 us -> 42 us
  matrix products: 42.2 us -> 97.3 us
  local copies, waits for them, and re-layouts: 49.3 us -> 4.37 us
  starting transfers between devices: 11.2 us -> 37.3 us
  between operations: 13.6 us -> 0.6 us
    all_to_all x1 -> x0, blocking collectives: 188 us -> none  [on_device(): lax.all_to_all(sendable, ('ctx', 'heads'), split_axis=0, concat_axis=1, t...]
    all_to_all x2 -> x0, waiting for transfers between devices: 184 us -> none  [the longest x1 184 us: on_device(): lax.all_to_all(finished, ('ctx', 'heads'), split_axis=1, concat_axis=0, t...]
    ppermute x0 -> x29, waiting for transfers between devices: none -> 89.8 us  [the longest x12 34.9 us: flip_row(): return lax.ppermute(block, 'ctx', partner_pairs(ctx_count, 2))]
    all_gather x2 -> x0, waiting for transfers between devices: 61.7 us -> none  [the longest x1 40.1 us: on_device(): lax.all_gather(tokens, 'heads', axis=0, tiled=True)]
    dot_general x9 -> x29, matrix products: 42.2 us -> 97.3 us  [the longest x8 51.8 us: chunk_sum(): out_rows = jnp.dot(hid, down, preferred_element_type=jnp.float32)]
    all_gather x1, blocking collectives: 6.03 us -> 42 us  [on_device_dense(): lax.all_gather(dense_weights, ('ctx', 'heads'), axis=0, tiled=True)]
    ppermute x0 -> x29, starting transfers between devices: none -> 27.9 us  [the longest x12 17 us: flip_row(): return lax.ppermute(block, 'ctx', partner_pairs(ctx_count, 2))]
    scatter x1 -> x0, local copies, waits for them, and re-layouts: 24.7 us -> none  [on_device(): outgoing = outgoing.at[destination].set(normed[source_rows])]
  transfers between devices with their start and end apart: 5 -> 33, of which waited for: 3 -> 15; matrix products, arithmetic and copies ran while one was open for 4% -> 37% of each run, Pallas kernels for 0% -> 0%
where the time goes in v1:
time: 284 us; the launch traced here: 283 us
  matrix products  97.3 us (34%)
  waiting for transfers between devices  90.8 us (32%)
  blocking collectives  42 us (15%)
  starting transfers between devices  37.3 us (13%)
  other arithmetic  10.9 us (4%)
  local copies, waits for them, and re-layouts  4.37 us (2%)
    dot_general x8, matrix products, chunk_sum(): out_rows = jnp.dot(hid, down, preferred_element_type=jnp.float32)  51.8 us
    all_gather x1, blocking collectives, on_device_dense(): lax.all_gather(dense_weights, ('ctx', 'heads'), axis=0, tiled=True)  42 us
    ppermute x12, waiting for transfers between devices, flip_row(): return lax.ppermute(block, 'ctx', partner_pairs(ctx_count, 2))  34.9 us
    ppermute x3, waiting for transfers between devices, gather_ring(): blocks.append(lax.ppermute(blocks[-1], 'heads', ring_pairs(count, 1)))  17.8 us
    ppermute x3, waiting for transfers between devices, on_device_dense(): lax.ppermute(joined.astype(jnp.bfloat16), 'heads', ring_pairs(head_count,...  17.2 us
    ppermute x12, starting transfers between devices, flip_row(): return lax.ppermute(block, 'ctx', partner_pairs(ctx_count, 2))  17 us
    dot_general x4, matrix products, chunk_sum(): gate_act = jnp.dot(normed, gate, preferred_element_type=jnp.float32)  16.9 us
    dot_general x4, matrix products, chunk_sum(): up_act = jnp.dot(normed, up, preferred_element_type=jnp.float32)  16.3 us
  transfers between devices with their start and end apart: 33, of which 15 were waited for; matrix products, arithmetic and copies ran while one was open for 37% of the time, Pallas kernels for 0%

profile of v1, /device:TPU:0, one launch (start us, length us, event | category | flops | bytes accessed | tf_op | source)
XLA Modules:
  0.0 283.2 jit_solution(10132347904557113644)
XLA Ops:
  1.1 5.1 %collective-permute-start.17 = (bf16[32,2048]{1,0:T(8,128)(2,1)S(1)}, bf16[32,2048]{1,0:T(8,128)(2,1)S(1)}, u32[]{:S(2)}, u32[]{:S(2)}) collective-permute-start(bf16[32,2048]{1,0:T(8,128)(2,1)S(1)} %constant_dynamic-slice_fusion.24), channel_id=1, source_target_pairs={{0,3},{1,0},{2,1},{3,2},{4,7},{5,4},{6,5},{7,6},{8,11},{9,8},{10,9... | collective-permute-start | bytes 393224 | tf_op jit(solution)/shard_map/ppermute | solution.py:156
  7.2 2.5 collective-permute-start.1
  9.6 1.5 collective-permute-start
  11.9 42.0 %all_gather.3 = f32[2048,16]{0,1:T(8,128)S(1)} all-gather(f32[128,16]{0,1:T(8,128)S(1)} %select_reduce_fusion), channel_id=1, replica_groups=mesh['groups'=2,'ctx'=4,'heads'=4] {'ctx','heads'}, dimensions={0}, use_global_device_ids=true | all-gather | bytes 139264 | tf_op jit(solution)/shard_map/all_gather | solution.py:204
  57.3 1.5 collective-permute-start.18
  60.6 1.7 fusion.44
  62.5 9.5 %collective-permute-done.18 = bf16[4,1,32,2048]{3,2,1,0:T(8,128)(2,1)} collective-permute-done((bf16[4,1,32,2048]{3,2,1,0:T(8,128)(2,1)}, bf16[4,1,32,2048]{3,2,1,0:T(8,128)(2,1)}, u32[]{:S(2)}, u32[]{:S(2)}) %collective-permute-start.18) | collective-permute-done | bytes 524320 | tf_op jit(solution)/shard_map/ppermute | solution.py:177
  73.3 5.1 %collective-permute-done.2 = bf16[128,2048]{1,0:T(8,128)(2,1)S(1)} collective-permute-done((bf16[128,2048]{1,0:T(8,128)(2,1)}, bf16[128,2048]{1,0:T(8,128)(2,1)S(1)}, u32[]{:S(2)}, u32[]{:S(2)}) %collective-permute-start.2) | collective-permute-done | bytes 524320 | tf_op jit(solution)/shard_map/ppermute | solution.py:150
  78.4 1.6 fusion.43
  80.7 12.7 %collective-permute-done.3 = bf16[128,2048]{1,0:T(8,128)(2,1)S(1)} collective-permute-done((bf16[128,2048]{1,0:T(8,128)(2,1)S(1)}, bf16[128,2048]{1,0:T(8,128)(2,1)S(1)}, u32[]{:S(2)}, u32[]{:S(2)}) %collective-permute-start.3) | collective-permute-done | bytes 524320 | tf_op jit(solution)/shard_map/ppermute | solution.py:150
  94.3 1.4 collective-permute-start.6
  95.7 2.6 collective-permute-start.5
  100.8 4.2 %collective-permute-start.4 = (bf16[128,128]{1,0:T(8,128)(2,1)S(1)}, bf16[128,128]{1,0:T(8,128)(2,1)S(1)}, u32[]{:S(2)}, u32[]{:S(2)}) collective-permute-start(bf16[128,128]{1,0:T(8,128)(2,1)S(1)} %convolution_convert_fusion.12), channel_id=1, source_target_pairs={{0,4},{4,8},{8,12},{1,5},{5,9},{9,13},{2,6},{6,10},{10,14},{3,7},{... | collective-permute-start | bytes 98312 | tf_op jit(solution)/shard_map/ppermute | solution.py:26
  106.0 2.4 collective-permute-start.28
  110.1 2.3 collective-permute-start.11
  112.7 10.4 %collective-permute-done.11 = bf16[512,128]{0,1:T(8,128)(2,1)S(1)} collective-permute-done((bf16[512,128]{0,1:T(8,128)(2,1)S(1)}, bf16[512,128]{0,1:T(8,128)(2,1)S(1)}, u32[]{:S(2)}, u32[]{:S(2)}) %collective-permute-start.11) | collective-permute-done | bytes 131104 | tf_op jit(solution)/shard_map/ppermute | solution.py:161
  123.6 10.3 %collective-permute-done.9 = bf16[512,128]{0,1:T(8,128)(2,1)S(1)} collective-permute-done((bf16[512,128]{0,1:T(8,128)(2,1)S(1)}, bf16[512,128]{0,1:T(8,128)(2,1)S(1)}, u32[]{:S(2)}, u32[]{:S(2)}) %collective-permute-start.9) | collective-permute-done | bytes 131104 | tf_op jit(solution)/shard_map/ppermute | solution.py:156
  136.0 4.2 %collective-permute-done.14 = bf16[512,128]{0,1:T(8,128)(2,1)S(1)} collective-permute-done((bf16[512,128]{0,1:T(8,128)(2,1)S(1)}, bf16[512,128]{0,1:T(8,128)(2,1)S(1)}, u32[]{:S(2)}, u32[]{:S(2)}) %collective-permute-start.14) | collective-permute-done | bytes 131104 | tf_op jit(solution)/shard_map/ppermute | solution.py:161
  141.5 1.5 collective-permute-done.13
  143.0 2.1 collective-permute-done.12
  145.2 1.3 collective-permute-start.26
  146.6 1.9 fusion.31
  148.5 4.3 %fusion.184 = f32[256,768]{1,0:T(8,128)} fusion(bf16[1,2048,768]{2,1,0:T(8,128)(2,1)} %param.15, bf16[256,2048]{1,0:T(8,128)(2,1)S(1)} %get-tuple-element.68, f32[256]{0:T(256)S(1)} %add_rsqrt_fusion.1), kind=kOutput, calls=%fused_computation.275 | convolution fusion | flops 806879232 | bytes 4981760 | tf_op jit(solution)/shard_map/dot_general | solution.py:283
  152.8 6.8 %collective-permute-done.26 = bf16[128,2048]{1,0:T(8,128)(2,1)S(1)} collective-permute-done((bf16[128,2048]{1,0:T(8,128)(2,1)S(1)}, bf16[128,2048]{1,0:T(8,128)(2,1)S(1)}, u32[]{:S(2)}, u32[]{:S(2)}) %collective-permute-start.26) | collective-permute-done | bytes 524320 | tf_op jit(solution)/shard_map/ppermute | solution.py:161
  161.8 4.2 %fusion.186 = f32[256,768]{1,0:T(8,128)} fusion(bf16[1,2048,768]{2,1,0:T(8,128)(2,1)} %param.15, bf16[256,2048]{1,0:T(8,128)(2,1)S(1)} %get-tuple-element.70, f32[256]{0:T(256)S(1)} %add_rsqrt_fusion.2), kind=kOutput, calls=%fused_computation.277 | convolution fusion | flops 806879232 | bytes 4981760 | tf_op jit(solution)/shard_map/dot_general | solution.py:283
  166.0 7.2 %collective-permute-done.24 = bf16[128,2048]{1,0:T(8,128)(2,1)S(1)} collective-permute-done((bf16[128,2048]{1,0:T(8,128)(2,1)S(1)}, bf16[128,2048]{1,0:T(8,128)(2,1)S(1)}, u32[]{:S(2)}, u32[]{:S(2)}) %collective-permute-start.24) | collective-permute-done | bytes 524320 | tf_op jit(solution)/shard_map/ppermute | solution.py:161
  174.1 4.2 %fusion.188 = f32[256,768]{1,0:T(8,128)} fusion(bf16[1,2048,768]{2,1,0:T(8,128)(2,1)} %param.15, bf16[256,2048]{1,0:T(8,128)(2,1)S(1)} %get-tuple-element.72, f32[256]{0:T(256)S(1)} %add_rsqrt_fusion.3), kind=kOutput, calls=%fused_computation.279 | convolution fusion | flops 806879232 | bytes 4981760 | tf_op jit(solution)/shard_map/dot_general | solution.py:283
  178.3 1.9 fusion.25
  180.3 4.2 %fusion.190 = f32[256,768]{1,0:T(8,128)} fusion(bf16[1,2048,768]{2,1,0:T(8,128)(2,1)} %param.15, bf16[256,2048]{1,0:T(8,128)(2,1)S(1)} %get-tuple-element.74, f32[256]{0:T(256)S(1)} %add_rsqrt_fusion.4), kind=kOutput, calls=%fused_computation.281 | convolution fusion | flops 806879232 | bytes 4981760 | tf_op jit(solution)/shard_map/dot_general | solution.py:283
  184.5 6.7 %fusion.6 = f32[256,2048]{1,0:T(8,128)} fusion(f32[256]{0:T(256)S(1)} %bitcast.109, f32[256,768]{1,0:T(8,128)} %fusion.184, bf16[1,768,2048]{2,1,0:T(8,128)(2,1)} %param.17, bf16[1,2048,768]{2,1,0:T(8,128)(2,1)} %param.16, bf16[256,2048]{1,0:T(8,128)(2,1)S(1)} %copy-done.16, f32[256]{0:T(256)S(1)} %add_rsqrt_fusion.1), kind=kOutput, calls=%fused_computation.17 | convolution fusion | flops 1614938112 | bytes 10225664 | tf_op jit(solution)/shard_map/dot_general | solution.py:286
  191.2 6.9 %fusion.12 = f32[256,2048]{1,0:T(8,128)} fusion(f32[256]{0:T(256)S(1)} %bitcast.110, f32[256,768]{1,0:T(8,128)} %fusion.186, bf16[1,768,2048]{2,1,0:T(8,128)(2,1)} %param.17, bf16[1,2048,768]{2,1,0:T(8,128)(2,1)} %param.16, bf16[256,2048]{1,0:T(8,128)(2,1)} %copy-done.18, f32[256]{0:T(256)S(1)} %add_rsqrt_fusion.2), kind=kOutput, calls=%fused_computation.25 | convolution fusion | flops 1614938112 | bytes 10225664 | tf_op jit(solution)/shard_map/dot_general | solution.py:286
  198.1 7.0 %fusion.18 = f32[256,2048]{1,0:T(8,128)} fusion(f32[256]{0:T(256)S(1)} %bitcast.111, f32[256,768]{1,0:T(8,128)} %fusion.188, bf16[1,768,2048]{2,1,0:T(8,128)(2,1)} %param.17, bf16[1,2048,768]{2,1,0:T(8,128)(2,1)} %param.16, bf16[256,2048]{1,0:T(8,128)(2,1)} %copy-done.17, f32[256]{0:T(256)S(1)} %add_rsqrt_fusion.3), kind=kOutput, calls=%fused_computation.33 | convolution fusion | flops 1614938112 | bytes 10225664 | tf_op jit(solution)/shard_map/dot_general | solution.py:286
  205.0 6.8 %fusion.24 = f32[256,2048]{1,0:T(8,128)} fusion(f32[256]{0:T(256)S(1)} %bitcast.112, f32[256,768]{1,0:T(8,128)} %fusion.190, bf16[1,768,2048]{2,1,0:T(8,128)(2,1)} %param.17, bf16[1,2048,768]{2,1,0:T(8,128)(2,1)} %param.16, bf16[256,2048]{1,0:T(8,128)(2,1)S(1)} %get-tuple-element.74, f32[256]{0:T(256)S(1)} %add_rsqrt_fusion.4), kind=kOutput, calls=%fused_computation.41 | convolution fusion | flops 1614938112 | bytes 10225664 | tf_op jit(solution)/shard_map/dot_general | solution.py:286
  211.8 3.8 %fusion.207 = f32[256,768]{1,0:T(8,128)} fusion(bf16[2048,768]{1,0:T(8,128)(2,1)} %collective-permute-done.21, bf16[256,2048]{1,0:T(8,128)(2,1)S(1)} %copy-done.16, f32[256]{0:T(256)S(1)} %add_rsqrt_fusion.1), kind=kOutput, calls=%fused_computation.298 | convolution fusion | flops 806879232 | bytes 4981760 | tf_op jit(solution)/shard_map/dot_general | solution.py:284
  215.7 5.9 %fusion.4 = bf16[256,2048]{1,0:T(8,128)(2,1)S(1)} fusion(f32[256,2048]{1,0:T(8,128)} %fusion.6, bf16[768,2048]{1,0:T(8,128)(2,1)} %collective-permute-done.22, f32[256]{0:T(256)S(1)} %bitcast.108, f32[256,768]{1,0:T(8,128)} %fusion.207, bf16[2048,768]{1,0:T(8,128)(2,1)} %collective-permute-done.20, bf16[256,2048]{1,0:T(8,128)(2,1)S(1)} %copy-done.16, ...), kind=kOutput, calls=%fused_computation.14 | convolution fusion | flops 1615986688 | bytes 11274240 | tf_op jit(solution)/shard_map/dot_general | solution.py:286
  223.0 4.2 %fusion.218 = f32[256,768]{1,0:T(8,128)} fusion(bf16[2048,768]{1,0:T(8,128)(2,1)} %collective-permute-done.21, bf16[256,2048]{1,0:T(8,128)(2,1)} %copy-done.18, f32[256]{0:T(256)S(1)} %add_rsqrt_fusion.2), kind=kOutput, calls=%fused_computation.300 | convolution fusion | flops 806879232 | bytes 4981760 | tf_op jit(solution)/shard_map/dot_general | solution.py:284
  227.1 6.2 %fusion.10 = bf16[256,2048]{1,0:T(8,128)(2,1)S(1)} fusion(f32[256,2048]{1,0:T(8,128)} %fusion.12, bf16[768,2048]{1,0:T(8,128)(2,1)} %collective-permute-done.22, f32[256]{0:T(256)S(1)} %bitcast.107, f32[256,768]{1,0:T(8,128)} %fusion.218, bf16[2048,768]{1,0:T(8,128)(2,1)} %collective-permute-done.20, bf16[256,2048]{1,0:T(8,128)(2,1)} %copy-done.18, ...), kind=kOutput, calls=%fused_computation.22 | convolution fusion | flops 1615986688 | bytes 11274240 | tf_op jit(solution)/shard_map/dot_general | solution.py:286
  235.0 4.1 %fusion.229 = f32[256,768]{1,0:T(8,128)} fusion(bf16[2048,768]{1,0:T(8,128)(2,1)} %collective-permute-done.21, bf16[256,2048]{1,0:T(8,128)(2,1)} %copy-done.17, f32[256]{0:T(256)S(1)} %add_rsqrt_fusion.3), kind=kOutput, calls=%fused_computation.302 | convolution fusion | flops 806879232 | bytes 4981760 | tf_op jit(solution)/shard_map/dot_general | solution.py:284
  239.3 6.2 %fusion.16 = bf16[256,2048]{1,0:T(8,128)(2,1)S(1)} fusion(f32[256,2048]{1,0:T(8,128)} %fusion.18, bf16[768,2048]{1,0:T(8,128)(2,1)} %collective-permute-done.22, f32[256]{0:T(256)S(1)} %bitcast.106, f32[256,768]{1,0:T(8,128)} %fusion.229, bf16[2048,768]{1,0:T(8,128)(2,1)} %collective-permute-done.20, bf16[256,2048]{1,0:T(8,128)(2,1)} %copy-done.17, ...), kind=kOutput, calls=%fused_computation.30 | convolution fusion | flops 1615986688 | bytes 11274240 | tf_op jit(solution)/shard_map/dot_general | solution.py:286
  245.5 1.3 collective-permute-start.25
  246.9 4.2 %fusion.240 = f32[256,768]{1,0:T(8,128)} fusion(bf16[2048,768]{1,0:T(8,128)(2,1)} %collective-permute-done.21, bf16[256,2048]{1,0:T(8,128)(2,1)} %copy-done.8, f32[256]{0:T(256)S(1)} %add_rsqrt_fusion.4), kind=kOutput, calls=%fused_computation.304 | convolution fusion | flops 806879232 | bytes 4981760 | tf_op jit(solution)/shard_map/dot_general | solution.py:284
  251.0 2.1 collective-permute-done.30
  253.2 2.1 add_convert_fusion.5
  255.3 6.2 %fusion.22 = bf16[256,2048]{1,0:T(8,128)(2,1)S(1)} fusion(f32[256,2048]{1,0:T(8,128)} %fusion.24, bf16[768,2048]{1,0:T(8,128)(2,1)} %collective-permute-done.22, f32[256]{0:T(256)S(1)} %bitcast.105, f32[256,768]{1,0:T(8,128)} %fusion.240, bf16[2048,768]{1,0:T(8,128)(2,1)} %collective-permute-done.20, bf16[256,2048]{1,0:T(8,128)(2,1)} %copy-done.8, ...), kind=kOutput, calls=%fused_computation.38 | convolution fusion | flops 1615986688 | bytes 11274240 | tf_op jit(solution)/shard_map/dot_general | solution.py:286
  262.9 5.7 %collective-permute-done.31 = bf16[128,2048]{1,0:T(8,128)(2,1)} collective-permute-done((bf16[128,2048]{1,0:T(8,128)(2,1)}, bf16[128,2048]{1,0:T(8,128)(2,1)}, u32[]{:S(2)}, u32[]{:S(2)}) %collective-permute-start.31) | collective-permute-done | bytes 524320 | tf_op jit(solution)/shard_map/ppermute | solution.py:300
  268.6 1.4 add_convert_fusion.4
  270.1 2.7 collective-permute-done.23
  272.8 9.3 %collective-permute-done.32 = bf16[128,2048]{1,0:T(8,128)(2,1)S(1)} collective-permute-done((bf16[128,2048]{1,0:T(8,128)(2,1)S(1)}, bf16[128,2048]{1,0:T(8,128)(2,1)S(1)}, u32[]{:S(2)}, u32[]{:S(2)}) %collective-permute-start.32) | collective-permute-done | bytes 524320 | tf_op jit(solution)/shard_map/ppermute | solution.py:300
  (133 shorter events, 29.1 us)
Async XLA Ops:
  0.0 58.8 %copy-start.2 = (bf16[2048,3,128]{2,0,1:T(8,128)(2,1)S(1)}, bf16[2048,3,128]{2,0,1:T(8,128)(2,1)}, u32[]{:S(2)}) copy-start(bf16[2048,3,128]{2,0,1:T(8,128)(2,1)} %param.13) | copy-start | bytes 4718596
  1.1 55.4 %collective-permute-start.17 = (bf16[32,2048]{1,0:T(8,128)(2,1)S(1)}, bf16[32,2048]{1,0:T(8,128)(2,1)S(1)}, u32[]{:S(2)}, u32[]{:S(2)}) collective-permute-start(bf16[32,2048]{1,0:T(8,128)(2,1)S(1)} %constant_dynamic-slice_fusion.24), channel_id=1, source_target_pairs={{0,3},{1,0},{2,1},{3,2},{4,7},{5,4},{6,5},{7,6},{8,11},{9,8},{10,9... | collective-permute-start | bytes 393224 | tf_op jit(solution)/shard_map/ppermute | solution.py:156
  6.2 50.3 %collective-permute-start.16 = (bf16[32,2048]{1,0:T(8,128)(2,1)S(1)}, bf16[32,2048]{1,0:T(8,128)(2,1)S(1)}, u32[]{:S(2)}, u32[]{:S(2)}) collective-permute-start(bf16[32,2048]{1,0:T(8,128)(2,1)S(1)} %constant_dynamic-slice_fusion.24), channel_id=1, source_target_pairs={{0,2},{1,3},{2,0},{3,1},{4,6},{5,7},{6,4},{7,5},{8,10},{9,11},{10,... | collective-permute-start | bytes 393224 | tf_op jit(solution)/shard_map/ppermute | solution.py:156
  6.2 50.3 %collective-permute-start.15 = (bf16[32,2048]{1,0:T(8,128)(2,1)S(1)}, bf16[32,2048]{1,0:T(8,128)(2,1)S(1)}, u32[]{:S(2)}, u32[]{:S(2)}) collective-permute-start(bf16[32,2048]{1,0:T(8,128)(2,1)S(1)} %constant_dynamic-slice_fusion.24), channel_id=1, source_target_pairs={{0,1},{1,2},{2,3},{3,0},{4,5},{5,6},{6,7},{7,4},{8,9},{9,10},{10,1... | collective-permute-start | bytes 393224 | tf_op jit(solution)/shard_map/ppermute | solution.py:156
  7.2 55.1 %collective-permute-start.1 = (bf16[128,2048]{1,0:T(8,128)(2,1)}, bf16[128,2048]{1,0:T(8,128)(2,1)}, u32[]{:S(2)}, u32[]{:S(2)}) collective-permute-start(bf16[128,2048]{1,0:T(8,128)(2,1)} %param.10), channel_id=1, source_target_pairs={{0,1},{1,2},{2,3},{3,0},{4,5},{5,6},{6,7},{7,4},{8,9},{9,10},{10,1... | collective-permute-start | bytes 1572872 | tf_op jit(solution)/shard_map/ppermute | solution.py:150
  9.6 168.6 %collective-permute-start = (bf16[128,2048]{1,0:T(8,128)(2,1)}, bf16[128,2048]{1,0:T(8,128)(2,1)}, u32[]{:S(2)}, u32[]{:S(2)}) collective-permute-start(bf16[128,2048]{1,0:T(8,128)(2,1)} %param.10), channel_id=1, source_target_pairs={{0,8},{4,12},{8,0},{12,4},{1,9},{5,13},{9,1},{13,5},{2,10},{6,14},... | collective-permute-start | bytes 1572872 | tf_op jit(solution)/shard_map/ppermute | solution.py:161
  56.5 159.2 %collective-permute-start.22 = (bf16[768,2048]{1,0:T(8,128)(2,1)}, bf16[768,2048]{1,0:T(8,128)(2,1)}, u32[]{:S(2)}, u32[]{:S(2)}) collective-permute-start(bf16[768,2048]{1,0:T(8,128)(2,1)} %bitcast.113), channel_id=1, source_target_pairs={{0,4},{4,0},{8,12},{12,8},{1,5},{5,1},{9,13},{13,9},{2,6},{6,2},{1... | collective-permute-start | bytes 9437192 | tf_op jit(solution)/shard_map/ppermute | solution.py:165
  57.3 14.6 %collective-permute-start.18 = (bf16[4,1,32,2048]{3,2,1,0:T(8,128)(2,1)}, bf16[4,1,32,2048]{3,2,1,0:T(8,128)(2,1)}, u32[]{:S(2)}, u32[]{:S(2)}) collective-permute-start(bf16[4,1,32,2048]{3,2,1,0:T(8,128)(2,1)} %maximum_bitcast_fusion), channel_id=1, source_target_pairs={{0,16},{16,0},{1,17},{17,1},{2,18},{18,2},{3,19},{19,3},{4,20},{20... | collective-permute-start | bytes 1572872 | tf_op jit(solution)/shard_map/ppermute | solution.py:177
  59.6 12.4 %copy-start.7 = (bf16[32,2048]{1,0:T(8,128)(2,1)S(1)}, bf16[32,2048]{1,0:T(8,128)(2,1)}, u32[]{:S(2)}) copy-start(bf16[32,2048]{1,0:T(8,128)(2,1)} %copy-done.6) | copy-start | bytes 393220
  62.3 16.1 %collective-permute-start.2 = (bf16[128,2048]{1,0:T(8,128)(2,1)}, bf16[128,2048]{1,0:T(8,128)(2,1)S(1)}, u32[]{:S(2)}, u32[]{:S(2)}) collective-permute-start(bf16[128,2048]{1,0:T(8,128)(2,1)} %collective-permute-done.1), channel_id=1, source_target_pairs={{0,1},{1,2},{2,3},{3,0},{4,5},{5,6},{6,7},{7,4},{8,9},{9,10},{10,1... | collective-permute-start | bytes 1572872 | tf_op jit(solution)/shard_map/ppermute | solution.py:150
  73.2 25.1 %collective-permute-start.19 = (bf16[4,2,32,2048]{3,2,1,0:T(8,128)(2,1)S(1)}, bf16[4,2,32,2048]{3,2,1,0:T(8,128)(2,1)S(1)}, u32[]{:S(2)}, u32[]{:S(2)}) collective-permute-start(bf16[4,2,32,2048]{3,2,1,0:T(8,128)(2,1)S(1)} %pad_maximum_fusion.1), channel_id=1, source_target_pairs={{0,4},{4,0},{8,12},{12,8},{1,5},{5,1},{9,13},{13,9},{2,6},{6,2},{1... | collective-permute-start | bytes 3145736 | tf_op jit(solution)/shard_map/ppermute | solution.py:165
  78.4 15.0 %collective-permute-start.3 = (bf16[128,2048]{1,0:T(8,128)(2,1)S(1)}, bf16[128,2048]{1,0:T(8,128)(2,1)S(1)}, u32[]{:S(2)}, u32[]{:S(2)}) collective-permute-start(bf16[128,2048]{1,0:T(8,128)(2,1)S(1)} %collective-permute-done.2), channel_id=1, source_target_pairs={{0,1},{1,2},{2,3},{3,0},{4,5},{5,6},{6,7},{7,4},{8,9},{9,10},{10,1... | collective-permute-start | bytes 1572872 | tf_op jit(solution)/shard_map/ppermute | solution.py:150
  94.3 11.6 %collective-permute-start.6 = (bf16[128,128]{1,0:T(8,128)(2,1)S(1)}, bf16[128,128]{1,0:T(8,128)(2,1)S(1)}, u32[]{:S(2)}, u32[]{:S(2)}) collective-permute-start(bf16[128,128]{1,0:T(8,128)(2,1)S(1)} %convolution_convert_fusion.12), channel_id=1, source_target_pairs={{0,12},{1,13},{2,14},{3,15},{16,28},{17,29},{18,30},{19,31}} | collective-permute-start | bytes 98312 | tf_op jit(solution)/shard_map/ppermute | solution.py:26
  95.7 12.7 %collective-permute-start.5 = (bf16[128,128]{1,0:T(8,128)(2,1)S(1)}, bf16[128,128]{1,0:T(8,128)(2,1)S(1)}, u32[]{:S(2)}, u32[]{:S(2)}) collective-permute-start(bf16[128,128]{1,0:T(8,128)(2,1)S(1)} %convolution_convert_fusion.12), channel_id=1, source_target_pairs={{0,8},{4,12},{1,9},{5,13},{2,10},{6,14},{3,11},{7,15},{16,24},{20,... | collective-permute-start | bytes 98312 | tf_op jit(solution)/shard_map/ppermute | solution.py:26
  98.4 2.4 collective-permute-start.7
  100.8 7.6 %collective-permute-start.4 = (bf16[128,128]{1,0:T(8,128)(2,1)S(1)}, bf16[128,128]{1,0:T(8,128)(2,1)S(1)}, u32[]{:S(2)}, u32[]{:S(2)}) collective-permute-start(bf16[128,128]{1,0:T(8,128)(2,1)S(1)} %convolution_convert_fusion.12), channel_id=1, source_target_pairs={{0,4},{4,8},{8,12},{1,5},{5,9},{9,13},{2,6},{6,10},{10,14},{3,7},{... | collective-permute-start | bytes 98312 | tf_op jit(solution)/shard_map/ppermute | solution.py:26
  106.0 39.3 %collective-permute-start.28 = (bf16[128,2048]{1,0:T(8,128)(2,1)}, bf16[128,2048]{1,0:T(8,128)(2,1)S(1)}, u32[]{:S(2)}, u32[]{:S(2)}) collective-permute-start(bf16[128,2048]{1,0:T(8,128)(2,1)} %collective-permute-done.1), channel_id=1, source_target_pairs={{0,8},{4,12},{8,0},{12,4},{1,9},{5,13},{9,1},{13,5},{2,10},{6,14},... | collective-permute-start | bytes 1572872 | tf_op jit(solution)/shard_map/ppermute | solution.py:161
  110.1 13.0 %collective-permute-start.11 = (bf16[512,128]{0,1:T(8,128)(2,1)S(1)}, bf16[512,128]{0,1:T(8,128)(2,1)S(1)}, u32[]{:S(2)}, u32[]{:S(2)}) collective-permute-start(bf16[512,128]{0,1:T(8,128)(2,1)S(1)} %add_convert_fusion.7), channel_id=1, source_target_pairs={{0,8},{4,12},{8,0},{12,4},{1,9},{5,13},{9,1},{13,5},{2,10},{6,14},... | collective-permute-start | bytes 393224 | tf_op jit(solution)/shard_map/ppermute | solution.py:161
  112.6 10.6 %collective-permute-start.10 = (bf16[512,128]{0,1:T(8,128)(2,1)S(1)}, bf16[512,128]{0,1:T(8,128)(2,1)S(1)}, u32[]{:S(2)}, u32[]{:S(2)}) collective-permute-start(bf16[512,128]{0,1:T(8,128)(2,1)S(1)} %add_convert_fusion.7), channel_id=1, source_target_pairs={{0,3},{1,0},{2,1},{3,2},{4,7},{5,4},{6,5},{7,6},{8,11},{9,8},{10,9... | collective-permute-start | bytes 393224 | tf_op jit(solution)/shard_map/ppermute | solution.py:156
  123.2 10.7 %collective-permute-start.9 = (bf16[512,128]{0,1:T(8,128)(2,1)S(1)}, bf16[512,128]{0,1:T(8,128)(2,1)S(1)}, u32[]{:S(2)}, u32[]{:S(2)}) collective-permute-start(bf16[512,128]{0,1:T(8,128)(2,1)S(1)} %add_convert_fusion.7), channel_id=1, source_target_pairs={{0,2},{1,3},{2,0},{3,1},{4,6},{5,7},{6,4},{7,5},{8,10},{9,11},{10,... | collective-permute-start | bytes 393224 | tf_op jit(solution)/shard_map/ppermute | solution.py:156
  123.2 11.9 %collective-permute-start.8 = (bf16[512,128]{0,1:T(8,128)(2,1)S(1)}, bf16[512,128]{0,1:T(8,128)(2,1)S(1)}, u32[]{:S(2)}, u32[]{:S(2)}) collective-permute-start(bf16[512,128]{0,1:T(8,128)(2,1)S(1)} %add_convert_fusion.7), channel_id=1, source_target_pairs={{0,1},{1,2},{2,3},{3,0},{4,5},{5,6},{6,7},{7,4},{8,9},{9,10},{10,1... | collective-permute-start | bytes 393224 | tf_op jit(solution)/shard_map/ppermute | solution.py:156
  133.9 6.3 %collective-permute-start.14 = (bf16[512,128]{0,1:T(8,128)(2,1)S(1)}, bf16[512,128]{0,1:T(8,128)(2,1)S(1)}, u32[]{:S(2)}, u32[]{:S(2)}) collective-permute-start(bf16[512,128]{0,1:T(8,128)(2,1)S(1)} %collective-permute-done.10), channel_id=1, source_target_pairs={{0,8},{4,12},{8,0},{12,4},{1,9},{5,13},{9,1},{13,5},{2,10},{6,14},... | collective-permute-start | bytes 393224 | tf_op jit(solution)/shard_map/ppermute | solution.py:161
  135.1 7.9 %collective-permute-start.13 = (bf16[512,128]{0,1:T(8,128)(2,1)S(1)}, bf16[512,128]{0,1:T(8,128)(2,1)S(1)}, u32[]{:S(2)}, u32[]{:S(2)}) collective-permute-start(bf16[512,128]{0,1:T(8,128)(2,1)S(1)} %collective-permute-done.9), channel_id=1, source_target_pairs={{0,8},{4,12},{8,0},{12,4},{1,9},{5,13},{9,1},{13,5},{2,10},{6,14},... | collective-permute-start | bytes 393224 | tf_op jit(solution)/shard_map/ppermute | solution.py:161
  140.2 5.0 %collective-permute-start.12 = (bf16[512,128]{0,1:T(8,128)(2,1)S(1)}, bf16[512,128]{0,1:T(8,128)(2,1)S(1)}, u32[]{:S(2)}, u32[]{:S(2)}) collective-permute-start(bf16[512,128]{0,1:T(8,128)(2,1)S(1)} %collective-permute-done.8), channel_id=1, source_target_pairs={{0,8},{4,12},{8,0},{12,4},{1,9},{5,13},{9,1},{13,5},{2,10},{6,14},... | collective-permute-start | bytes 393224 | tf_op jit(solution)/shard_map/ppermute | solution.py:161
  143.0 68.8 %collective-permute-start.21 = (bf16[2048,768]{1,0:T(8,128)(2,1)}, bf16[2048,768]{1,0:T(8,128)(2,1)}, u32[]{:S(2)}, u32[]{:S(2)}) collective-permute-start(bf16[2048,768]{1,0:T(8,128)(2,1)} %bitcast.12), channel_id=1, source_target_pairs={{0,4},{4,0},{8,12},{12,8},{1,5},{5,1},{9,13},{13,9},{2,6},{6,2},{1... | collective-permute-start | bytes 9437192 | tf_op jit(solution)/shard_map/ppermute | solution.py:165
  145.2 70.5 %collective-permute-start.20 = (bf16[2048,768]{1,0:T(8,128)(2,1)}, bf16[2048,768]{1,0:T(8,128)(2,1)}, u32[]{:S(2)}, u32[]{:S(2)}) collective-permute-start(bf16[2048,768]{1,0:T(8,128)(2,1)} %bitcast.11), channel_id=1, source_target_pairs={{0,4},{4,0},{8,12},{12,8},{1,5},{5,1},{9,13},{13,9},{2,6},{6,2},{1... | collective-permute-start | bytes 9437192 | tf_op jit(solution)/shard_map/ppermute | solution.py:165
  145.2 14.4 %collective-permute-start.26 = (bf16[128,2048]{1,0:T(8,128)(2,1)S(1)}, bf16[128,2048]{1,0:T(8,128)(2,1)S(1)}, u32[]{:S(2)}, u32[]{:S(2)}) collective-permute-start(bf16[128,2048]{1,0:T(8,128)(2,1)S(1)} %collective-permute-done.2), channel_id=1, source_target_pairs={{0,8},{4,12},{8,0},{12,4},{1,9},{5,13},{9,1},{13,5},{2,10},{6,14},... | collective-permute-start | bytes 1572872 | tf_op jit(solution)/shard_map/ppermute | solution.py:161
  148.5 4.3 %copy-start.15 = (bf16[256,2048]{1,0:T(8,128)(2,1)}, bf16[256,2048]{1,0:T(8,128)(2,1)S(1)}, u32[]{:S(2)}) copy-start(bf16[256,2048]{1,0:T(8,128)(2,1)S(1)} %get-tuple-element.68) | copy-start | bytes 3145732
  159.6 13.6 %collective-permute-start.24 = (bf16[128,2048]{1,0:T(8,128)(2,1)S(1)}, bf16[128,2048]{1,0:T(8,128)(2,1)S(1)}, u32[]{:S(2)}, u32[]{:S(2)}) collective-permute-start(bf16[128,2048]{1,0:T(8,128)(2,1)S(1)} %collective-permute-done.3), channel_id=1, source_target_pairs={{0,8},{4,12},{8,0},{12,4},{1,9},{5,13},{9,1},{13,5},{2,10},{6,14},... | collective-permute-start | bytes 1572872 | tf_op jit(solution)/shard_map/ppermute | solution.py:161
  161.8 4.2 %copy-start.18 = (bf16[256,2048]{1,0:T(8,128)(2,1)}, bf16[256,2048]{1,0:T(8,128)(2,1)S(1)}, u32[]{:S(2)}) copy-start(bf16[256,2048]{1,0:T(8,128)(2,1)S(1)} %get-tuple-element.70) | copy-start | bytes 3145732
  174.1 4.2 %copy-start.17 = (bf16[256,2048]{1,0:T(8,128)(2,1)}, bf16[256,2048]{1,0:T(8,128)(2,1)S(1)}, u32[]{:S(2)}) copy-start(bf16[256,2048]{1,0:T(8,128)(2,1)S(1)} %get-tuple-element.72) | copy-start | bytes 3145732
  180.2 24.8 %copy-start.8 = (bf16[256,2048]{1,0:T(8,128)(2,1)}, bf16[256,2048]{1,0:T(8,128)(2,1)S(1)}, u32[]{:S(2)}) copy-start(bf16[256,2048]{1,0:T(8,128)(2,1)S(1)} %get-tuple-element.74) | copy-start | bytes 3145732
  180.2 4.2 %copy-start.11 = (f32[1,256,1]{1,0,2:T(1,128)S(1)}, f32[1,256,1]{1,0,2:T(1,128)}, u32[]{:S(2)}) copy-start(f32[1,256,1]{1,0,2:T(1,128)} %pad_maximum_fusion.8) | copy-start | bytes 3076
  180.3 4.2 %copy-start.16 = (bf16[256,2048]{1,0:T(8,128)(2,1)S(1)}, bf16[256,2048]{1,0:T(8,128)(2,1)}, u32[]{:S(2)}) copy-start(bf16[256,2048]{1,0:T(8,128)(2,1)} %copy-done.15) | copy-start | bytes 3145732
  184.5 6.7 %copy-start.12 = (f32[1,256,1]{1,0,2:T(1,128)S(1)}, f32[1,256,1]{1,0,2:T(1,128)}, u32[]{:S(2)}) copy-start(f32[1,256,1]{1,0,2:T(1,128)} %pad_maximum_fusion.6) | copy-start | bytes 3076
  191.2 6.9 %copy-start.13 = (f32[1,256,1]{1,0,2:T(1,128)S(1)}, f32[1,256,1]{1,0,2:T(1,128)}, u32[]{:S(2)}) copy-start(f32[1,256,1]{1,0,2:T(1,128)} %pad_maximum_fusion.4) | copy-start | bytes 3076
  198.1 7.0 %copy-start.14 = (f32[1,256,1]{1,0,2:T(1,128)S(1)}, f32[1,256,1]{1,0,2:T(1,128)}, u32[]{:S(2)}) copy-start(f32[1,256,1]{1,0,2:T(1,128)} %pad_maximum_fusion.2) | copy-start | bytes 3076
  221.6 17.5 %collective-permute-start.29 = (bf16[128,2048]{1,0:T(8,128)(2,1)S(1)}, bf16[128,2048]{1,0:T(8,128)(2,1)S(1)}, u32[]{:S(2)}, u32[]{:S(2)}) collective-permute-start(bf16[128,2048]{1,0:T(8,128)(2,1)S(1)} %slice.87), channel_id=1, source_target_pairs={{0,8},{4,12},{8,0},{12,4},{1,9},{5,13},{9,1},{13,5},{2,10},{6,14},... | collective-permute-start | bytes 1572872 | tf_op jit(solution)/shard_map/ppermute | solution.py:161
  233.3 5.8 %copy-start.3 = (bf16[256,2048]{1,0:T(8,128)(2,1)}, bf16[256,2048]{1,0:T(8,128)(2,1)S(1)}, u32[]{:S(2)}) copy-start(bf16[256,2048]{1,0:T(8,128)(2,1)S(1)} %fusion.10) | copy-start | bytes 3145732
  234.2 16.8 %collective-permute-start.27 = (bf16[128,2048]{1,0:T(8,128)(2,1)}, bf16[128,2048]{1,0:T(8,128)(2,1)}, u32[]{:S(2)}, u32[]{:S(2)}) collective-permute-start(bf16[128,2048]{1,0:T(8,128)(2,1)} %slice.85), channel_id=1, source_target_pairs={{0,8},{4,12},{8,0},{12,4},{1,9},{5,13},{9,1},{13,5},{2,10},{6,14},... | collective-permute-start | bytes 1572872 | tf_op jit(solution)/shard_map/ppermute | solution.py:161
  239.2 14.0 %collective-permute-start.30 = (bf16[128,2048]{1,0:T(8,128)(2,1)S(1)}, bf16[128,2048]{1,0:T(8,128)(2,1)S(1)}, u32[]{:S(2)}, u32[]{:S(2)}) collective-permute-start(bf16[128,2048]{1,0:T(8,128)(2,1)S(1)} %add_convert_fusion.6), channel_id=1, source_target_pairs={{0,1},{1,2},{2,3},{3,0},{4,5},{5,6},{6,7},{7,4},{8,9},{9,10},{10,1... | collective-permute-start | bytes 1572872 | tf_op jit(solution)/shard_map/ppermute | solution.py:300
  245.5 7.6 %copy-start.4 = (bf16[256,2048]{1,0:T(8,128)(2,1)S(1)}, bf16[256,2048]{1,0:T(8,128)(2,1)}, u32[]{:S(2)}) copy-start(bf16[256,2048]{1,0:T(8,128)(2,1)} %copy-done.3) | copy-start | bytes 3145732
  245.5 17.3 %collective-permute-start.25 = (bf16[128,2048]{1,0:T(8,128)(2,1)S(1)}, bf16[128,2048]{1,0:T(8,128)(2,1)}, u32[]{:S(2)}, u32[]{:S(2)}) collective-permute-start(bf16[128,2048]{1,0:T(8,128)(2,1)S(1)} %slice.83), channel_id=1, source_target_pairs={{0,8},{4,12},{8,0},{12,4},{1,9},{5,13},{9,1},{13,5},{2,10},{6,14},... | collective-permute-start | bytes 1572872 | tf_op jit(solution)/shard_map/ppermute | solution.py:161
  255.3 13.3 %collective-permute-start.31 = (bf16[128,2048]{1,0:T(8,128)(2,1)}, bf16[128,2048]{1,0:T(8,128)(2,1)}, u32[]{:S(2)}, u32[]{:S(2)}) collective-permute-start(bf16[128,2048]{1,0:T(8,128)(2,1)} %add_convert_fusion.5), channel_id=1, source_target_pairs={{0,1},{1,2},{2,3},{3,0},{4,5},{5,6},{6,7},{7,4},{8,9},{9,10},{10,1... | collective-permute-start | bytes 1572872 | tf_op jit(solution)/shard_map/ppermute | solution.py:300
  261.5 20.7 %copy-start.9 = (bf16[256,2048]{1,0:T(8,128)(2,1)S(1)}, bf16[256,2048]{1,0:T(8,128)(2,1)}, u32[]{:S(2)}) copy-start(bf16[256,2048]{1,0:T(8,128)(2,1)} %copy-done.8) | copy-start | bytes 3145732
  261.5 21.8 %copy-start.1 = (bf16[128,2048]{1,0:T(8,128)(2,1)S(1)}, bf16[128,2048]{1,0:T(8,128)(2,1)}, u32[]{:S(2)}) copy-start(bf16[128,2048]{1,0:T(8,128)(2,1)} %param.14) | copy-start | bytes 1572868
  261.5 11.2 %collective-permute-start.23 = (bf16[128,2048]{1,0:T(8,128)(2,1)S(1)}, bf16[128,2048]{1,0:T(8,128)(2,1)S(1)}, u32[]{:S(2)}, u32[]{:S(2)}) collective-permute-start(bf16[128,2048]{1,0:T(8,128)(2,1)S(1)} %slice.81), channel_id=1, source_target_pairs={{0,8},{4,12},{8,0},{12,4},{1,9},{5,13},{9,1},{13,5},{2,10},{6,14},... | collective-permute-start | bytes 1572872 | tf_op jit(solution)/shard_map/ppermute | solution.py:161
  270.0 12.1 %collective-permute-start.32 = (bf16[128,2048]{1,0:T(8,128)(2,1)S(1)}, bf16[128,2048]{1,0:T(8,128)(2,1)S(1)}, u32[]{:S(2)}, u32[]{:S(2)}) collective-permute-start(bf16[128,2048]{1,0:T(8,128)(2,1)S(1)} %add_convert_fusion.4), channel_id=1, source_target_pairs={{0,1},{1,2},{2,3},{3,0},{4,5},{5,6},{6,7},{7,4},{8,9},{9,10},{10,1... | collective-permute-start | bytes 1572872 | tf_op jit(solution)/shard_map/ppermute | solution.py:300
  (4 other events, 10.9 us)

commit v2 on v1

--- a/solution.py
+++ b/solution.py
@@ -1,8 +1,11 @@
+import functools
 import math
 
 import jax
 import jax.numpy as jnp
 from jax import lax
+from jax.experimental import pallas as pl
+from jax.experimental.pallas import tpu as pltpu
 from jax.sharding import PartitionSpec as P
 
 HDIM = 128
@@ -144,11 +147,12 @@
     return [(i, i ^ bit) for i in range(count)]
 
 
-def gather_ring(block, count):
-    blocks = [block]
-    for _ in range(count - 1):
-        blocks.append(lax.ppermute(blocks[-1], "heads", ring_pairs(count, 1)))
-    return blocks
+def after(value, *others):
+    return lax.optimization_barrier((value, *others))[0]
+
+
+def next_place(block, count):
+    return lax.ppermute(block, "heads", ring_pairs(count, 1))
 
 
 def gather_direct(block, count):
@@ -165,25 +169,143 @@
     return lax.ppermute(block, "ctx", partner_pairs(ctx_count, 1))
 
 
-def gather_w_out(w_out, head_count, ctx_count, group_count):
-    rows = w_out.shape[0]
-    parts = 2 * group_count
-    piece_rows = rows // parts
-    core = lax.axis_index("ctx") % 2
-    place = core * group_count + lax.axis_index("groups")
-    piece = lax.dynamic_slice_in_dim(w_out, place * piece_rows, piece_rows, 0)
-    own = jnp.stack(gather_direct(piece, head_count), axis=0)[:, None]
-    if group_count == 2:
-        other = lax.ppermute(own, "groups", [(0, 1), (1, 0)])
-        first = lax.axis_index("groups") == 0
-        own = jnp.concatenate(
-            [jnp.where(first, own, other), jnp.where(first, other, own)], axis=1
-        )
-    other = flip_core(own, ctx_count)
-    own = jnp.concatenate(
-        [jnp.where(core == 0, own, other), jnp.where(core == 0, other, own)], axis=1
-    )
-    return own.reshape(head_count * rows, w_out.shape[1])
+def w_out_piece(w_out, group_count):
+    piece_rows = w_out.shape[0] // (2 * group_count)
+    place = (lax.axis_index("ctx") % 2) * group_count + lax.axis_index("groups")
+    return lax.dynamic_slice_in_dim(w_out, place * piece_rows, piece_rows, 0)
+
+
+def chunk_kernel(head_count, turn, place_ref, *refs):
+    near_heads = refs[:head_count]
+    far_heads = refs[head_count : 2 * head_count]
+    near_tokens, far_tokens, near_out_w, far_out_w, *weights = refs[
+        2 * head_count : 2 * head_count + 10
+    ]
+    outs = refs[2 * head_count + 10 : -10]
+    heads_buf, token_buf, mark_buf, w_out_buf, *rest = refs[-10:]
+    wide_bufs, narrow_bufs, normed_buf, total_buf, small_sems, weight_sems = rest
+    row_count, model_width = outs[0].shape
+    slab_rows = row_count * head_count
+    experts, mark_rows = narrow_bufs.shape[0], mark_buf.shape[1]
+    first = pl.multiple_of(place_ref[0], row_count)
+
+    pairs = []
+    for side, (heads_in, tokens_in) in enumerate(
+        ((near_heads, near_tokens), (far_heads, far_tokens))
+    ):
+        rows = pl.ds(side * row_count, row_count)
+        for turns in range(head_count):
+            source = heads_in[turns].at[pl.ds(first, row_count)]
+            pairs.append((source, heads_buf.at[rows, pl.ds(turns * HDIM, HDIM)]))
+        pairs.append((tokens_in, token_buf.at[rows]))
+        pairs.append((heads_in[turn].at[pl.ds(slab_rows, mark_rows)], mark_buf.at[side]))
+    group_count = near_out_w.shape[0]
+    for core, pieces in enumerate((near_out_w, far_out_w)):
+        for group in range(group_count):
+            slot = place_ref[3 + core * group_count + group]
+            pairs.append((pieces.at[group], w_out_buf.at[:, slot]))
+    small = [
+        pltpu.make_async_copy(source, target, small_sems.at[i])
+        for i, (source, target) in enumerate(pairs)
+    ]
+    large = []
+    for expert in range(experts):
+        targets = (wide_bufs.at[expert, 0], wide_bufs.at[expert, 1], narrow_bufs.at[expert])
+        for kind, target in enumerate(targets):
+            copy = pltpu.make_async_copy(
+                weights[3 * expert + kind].at[0], target, weight_sems.at[3 * expert + kind]
+            )
+            large.append(copy)
+
+    for copy in small:
+        copy.start()
+    large[0].start()
+    for copy in small:
+        copy.wait()
+    large[1].start()
+
+    w_out_rows = w_out_buf[...].reshape(head_count * HDIM, model_width)
+    attn = jnp.dot(heads_buf[...], w_out_rows, preferred_element_type=jnp.float32)
+    hidden = (token_buf[...].astype(jnp.float32) + attn).astype(jnp.bfloat16)
+    if len(outs) == 3:
+        outs[2][...] = hidden[:row_count]
+    normed_buf[...] = normalize(hidden.astype(jnp.float32)).astype(jnp.bfloat16)
+
+    spots = lax.rem(lax.broadcasted_iota(jnp.int32, (mark_rows, HDIM), 0), mark_rows // 2)
+    for expert in range(experts):
+        chosen = jnp.where(spots == place_ref[1 + expert], 1.0, 0.0).astype(jnp.bfloat16)
+        gating = jnp.concatenate(
+            [
+                lax.dot_general(
+                    mark_buf[side],
+                    chosen,
+                    (((0,), (0,)), ((), ())),
+                    preferred_element_type=jnp.float32,
+                )[:, :1]
+                for side in range(2)
+            ],
+            axis=0,
+        )
+        acts = []
+        for kind in range(3):
+            step = 3 * expert + kind
+            if step + 2 < len(large):
+                large[step + 2].start()
+            large[step].wait()
+            if kind < 2:
+                acts.append(
+                    jnp.dot(
+                        normed_buf[...], wide_bufs[expert, kind], preferred_element_type=jnp.float32
+                    )
+                )
+        hid = (jax.nn.silu(acts[0]) * acts[1]).astype(jnp.bfloat16)
+        rows = jnp.dot(hid, narrow_bufs[expert], preferred_element_type=jnp.float32)
+        rows = rows.astype(jnp.bfloat16).astype(jnp.float32) * gating
+        if expert:
+            rows = rows + total_buf[...]
+        if expert < experts - 1:
+            total_buf[...] = rows
+        else:
+            rows = rows.astype(jnp.bfloat16)
+            outs[0][...] = rows[:row_count]
+            outs[1][...] = rows[row_count:]
+
+
+def run_chunk(turn, place, near_heads, far_heads, near_tokens, far_tokens, w_out, weights):
+    row_count, model_width = near_tokens.shape
+    head_count = len(near_heads)
+    inner = weights[0].shape[2]
+    rows = 2 * row_count
+    mark_rows = near_heads[0].shape[0] - row_count * head_count
+    experts = len(weights) // 3
+    outs = 2 if turn else 3
+    anywhere = pl.BlockSpec(memory_space=pl.ANY)
+    operands = [*near_heads, *far_heads, near_tokens, far_tokens, *w_out, *weights]
+    group_count, _, piece_rows, _ = w_out[0].shape
+    flops = 2 * rows * model_width * (3 * experts * inner + head_count * HDIM)
+    return pl.pallas_call(
+        functools.partial(chunk_kernel, head_count, turn),
+        out_shape=[jax.ShapeDtypeStruct((row_count, model_width), jnp.bfloat16)] * outs,
+        in_specs=[pl.BlockSpec(memory_space=pltpu.SMEM)] + [anywhere] * len(operands),
+        out_specs=[pl.BlockSpec(memory_space=pltpu.VMEM)] * outs,
+        scratch_shapes=[
+            pltpu.VMEM((rows, head_count * HDIM), jnp.bfloat16),
+            pltpu.VMEM((rows, model_width), jnp.bfloat16),
+            pltpu.VMEM((2, mark_rows, row_count), jnp.bfloat16),
+            pltpu.VMEM((head_count, 2 * group_count, piece_rows, model_width), jnp.bfloat16),
+            pltpu.VMEM((experts, 2, model_width, inner), jnp.bfloat16),
+            pltpu.VMEM((experts, inner, model_width), jnp.bfloat16),
+            pltpu.VMEM((rows, model_width), jnp.bfloat16),
+            pltpu.VMEM((rows, model_width), jnp.float32),
+            pltpu.SemaphoreType.DMA((2 * (head_count + 2 + group_count),)),
+            pltpu.SemaphoreType.DMA((3 * experts,)),
+        ],
+        compiler_params=pltpu.CompilerParams(vmem_limit_bytes=60 * 2**20),
+        cost_estimate=pl.CostEstimate(
+            flops=flops, bytes_accessed=sum(2 * math.prod(w.shape) for w in weights), transcendentals=0
+        ),
+        name="chunk",
+    )(place, *operands)
 
 
 def on_device_dense(
@@ -201,23 +323,39 @@
 
     hit = expert_ids[:, :, None] == jnp.arange(expert_count, dtype=jnp.int32)[None, None, :]
     dense_weights = jnp.sum(jnp.where(hit, gate_weights[:, :, None], 0.0), axis=1)
-    all_weights = lax.all_gather(dense_weights, ("ctx", "heads"), axis=0, tiled=True)
-    all_weights = all_weights.reshape(ctx_count, slab_rows, expert_count)
-
-    blocks = gather_ring(tokens, head_count)
+    coarse = lax.reduce_precision(dense_weights, 8, 7)
+    halves = [coarse, dense_weights - coarse]
+    marks = jnp.concatenate(halves, axis=1).astype(jnp.bfloat16).T
+
     w_flat = w_qkv.reshape(model_width, 3 * HDIM)
     projected = jnp.zeros((slab_rows, 3 * HDIM), jnp.bfloat16)
-    for s in range(head_count):
+
+    def project(projected, s):
         part = jnp.dot(blocks[s], w_flat, preferred_element_type=jnp.float32)
-        projected = lax.dynamic_update_slice_in_dim(
-            projected, part.astype(jnp.bfloat16), starts[s], 0
-        )
-    across = [flip_row(block, ctx_count) for block in blocks]
-    w_out_all = gather_w_out(w_out, head_count, ctx_count, group_count)
-    experts = [
-        (w_gate[0], w_up[0], w_down[0]),
-        tuple(flip_core(w[0], ctx_count) for w in (w_gate, w_up, w_down)),
-    ]
+        return lax.dynamic_update_slice_in_dim(projected, part.astype(jnp.bfloat16), starts[s], 0)
+
+    experts = [w_gate, w_up, w_down]
+    blocks, across, swapped = [tokens], [], []
+    pieces = [w_out_piece(w_out, group_count)] + [None] * (head_count - 1)
+    for s in range(head_count - 1):
+        blocks.append(next_place(blocks[s], head_count))
+        across.append(flip_row(blocks[s], ctx_count))
+        swapped.append(flip_core(after(experts[s], blocks[s]), ctx_count))
+        projected = project(projected, s)
+        for distance in ((1, head_count - 1), range(2, head_count - 1), ())[s]:
+            piece = after(pieces[0], blocks[s], swapped[s])
+            pieces[distance] = lax.ppermute(piece, "heads", ring_pairs(head_count, distance))
+        extra = (pieces, halves)[s - 1] if s else []
+        blocks[-1], across[-1], swapped[-1], projected, *extra = lax.optimization_barrier(
+            (blocks[-1], across[-1], swapped[-1], projected, *extra)
+        )
+        if s == 1:
+            halves = [jnp.concatenate(extra, axis=0)]
+            if group_count == 2:
+                halves.append(lax.ppermute(halves[0], "groups", [(0, 1), (1, 0)]))
+    half = jnp.stack(extra, axis=0)
+    projected = project(projected, head_count - 1)
+    experts = experts + swapped
 
     query = projected[:, :HDIM]
     keys = projected[:, HDIM : 2 * HDIM]
@@ -229,6 +367,11 @@
     for distance in range(1, ctx_count):
         start_state = start_state + from_behind(packed_state, "ctx", distance).astype(jnp.float32)
     past = jnp.concatenate([past_kv[0], past_kv[1]], axis=1)
+    half = after(half, arrived)
+    w_out_halves = [
+        part.reshape(group_count, head_count, -1, model_width)
+        for part in (half, flip_core(half, ctx_count))
+    ]
     previous = jnp.where(ctx == 0, past, arrived)
     all_keys = jnp.concatenate([previous[:, :HDIM], keys], axis=0)
     all_values = jnp.concatenate([previous[:, HDIM:], values], axis=0)
@@ -248,51 +391,26 @@
     window_out = jnp.dot(probs, all_values, preferred_element_type=jnp.float32)
     heads_out = (normalize(linear) + window_out).astype(jnp.bfloat16)
 
-    near_heads = gather_direct(heads_out, head_count)
+    near_heads = gather_direct(jnp.concatenate([heads_out, marks], axis=0), head_count)
     far_heads = [flip_row(part, ctx_count) for part in near_heads]
-
+    across.append(flip_row(after(blocks[-1], *far_heads), ctx_count))
     own_expert = ctx * head_count + place
     other_expert = (ctx ^ 1) * head_count + place
 
-    def chunk_rows(s):
-        heads_rows = jnp.concatenate(
-            [
-                jnp.concatenate(
-                    [lax.dynamic_slice_in_dim(part, starts[s], row_count, 0) for part in parts],
-                    axis=1,
-                )
-                for parts in (near_heads, far_heads)
-            ],
-            axis=0,
-        )
-        token_rows = jnp.concatenate([blocks[s], across[s]], axis=0)
-        attn = jnp.dot(heads_rows, w_out_all, preferred_element_type=jnp.float32)
-        hidden = (token_rows.astype(jnp.float32) + attn).astype(jnp.bfloat16)
-        return hidden, normalize(hidden.astype(jnp.float32)).astype(jnp.bfloat16)
-
-    def chunk_weights(s, expert):
-        rows = [
-            lax.dynamic_slice(all_weights, (where, starts[s], expert), (1, row_count, 1))
-            for where in (ctx, ctx ^ 2)
-        ]
-        return jnp.concatenate(rows, axis=1)[0]
-
-    def chunk_sum(s, normed):
-        total = 0.0
-        for (gate, up, down), expert in zip(experts, (own_expert, other_expert)):
-            gate_act = jnp.dot(normed, gate, preferred_element_type=jnp.float32)
-            up_act = jnp.dot(normed, up, preferred_element_type=jnp.float32)
-            hid = (jax.nn.silu(gate_act) * up_act).astype(jnp.bfloat16)
-            out_rows = jnp.dot(hid, down, preferred_element_type=jnp.float32)
-            out_rows = out_rows.astype(jnp.bfloat16).astype(jnp.float32)
-            total = total + chunk_weights(s, expert) * out_rows
-        return total.astype(jnp.bfloat16)
+    across[2] = after(across[2], across[-1])
+    group = lax.axis_index("groups")
+    slots = [
+        ((ctx % 2) ^ side) * group_count + (group ^ other)
+        for side in range(2)
+        for other in range(group_count)
+    ]
 
     carry = None
     for s in list(range(1, head_count)) + [0]:
-        hidden, normed = chunk_rows(s)
-        partial = chunk_sum(s, normed)
-        near, far = partial[:row_count], partial[row_count:]
+        where = jnp.stack([starts[s], own_expert, other_expert, *slots])
+        near, far, *hidden = run_chunk(
+            s, where, near_heads, far_heads, blocks[s], across[s], w_out_halves, experts
+        )
         joined = near.astype(jnp.float32) + flip_row(far, ctx_count).astype(jnp.float32)
         if carry is not None:
             joined = joined + carry.astype(jnp.float32)
@@ -300,7 +418,7 @@
             carry = lax.ppermute(
                 joined.astype(jnp.bfloat16), "heads", ring_pairs(head_count, 1)
             )
-    return (hidden[:row_count].astype(jnp.float32) + joined).astype(jnp.bfloat16)
+    return (hidden[0].astype(jnp.float32) + joined).astype(jnp.bfloat16)
 
 
 def solution(mesh):
@@ -312,10 +430,13 @@
         slab_rows = args[0].shape[0] * sizes["heads"]
         dense = (
             sizes["ctx"] == 4
+            and sizes["heads"] == 4
             and sizes["groups"] <= 2
             and w_gate.shape[0] == 1
             and w_qkv.shape[2] == HDIM
             and slab_rows == WINDOW
+            and args[0].shape[0] == HDIM
+            and expert_count % 8 == 0
             and expert_count <= 2 * expert_ids.shape[1]
         )
         return (on_device_dense if dense else on_device_routed)(*args)

time: 284 us -> 171 us (0.60)
  matrix products: 97.3 us -> 5.56 us
  Pallas kernels: 0 us -> 47.8 us
  blocking collectives: 42 us -> 0 us
  waiting for transfers between devices: 90.8 us -> 65 us
  other arithmetic: 10.9 us -> 3.68 us
  local copies, waits for them, and re-layouts: 4.37 us -> 8.97 us
    dot_general x24 -> x4, matrix products: 95.1 us -> 3.46 us  [project(): part = jnp.dot(blocks[s], w_flat, preferred_element_type=jnp.float32)]
    pallas_call x0 -> x4, Pallas kernels: none -> 47.8 us  [run_chunk(): pl.pallas_call(functools.partial(chunk_kernel, head_count, turn), out_sha...]
    all_gather x1 -> x0, blocking collectives: 42 us -> none  [on_device_dense(): lax.all_gather(dense_weights, ('ctx', 'heads'), axis=0, tiled=True)]
    ppermute x12, waiting for transfers between devices: 34.9 us -> 13.6 us  [flip_row(): return lax.ppermute(block, 'ctx', partner_pairs(ctx_count, 2))]
    ppermute x3, waiting for transfers between devices: 17.2 us -> 2.2 us  [on_device_dense(): lax.ppermute(joined.astype(jnp.bfloat16), 'heads', ring_pairs(head_count,...]
    ppermute x4 -> x7, waiting for transfers between devices: 27.3 us -> 40.8 us  [the longest x3 19.7 us: next_place(): return lax.ppermute(block, 'heads', ring_pairs(count, 1))]
    ppermute x4 -> x7, starting transfers between devices: 4.14 us -> 10.7 us  [the longest x3 5.47 us: on_device_dense(): lax.ppermute(piece, 'heads', ring_pairs(head_count, distance))]
    ppermute x3, starting transfers between devices: 0.12 us -> 4.62 us  [on_device_dense(): lax.ppermute(joined.astype(jnp.bfloat16), 'heads', ring_pairs(head_count,...]
  transfers between devices with their start and end apart: 33 -> 33, of which waited for: 15 -> 12; matrix products, arithmetic and copies ran while one was open for 37% -> 8% of each run, Pallas kernels for 0% -> 28%
where the time goes in v2:
time: 171 us
  waiting for transfers between devices  65 us (38%)
  Pallas kernels  47.8 us (28%)
  starting transfers between devices  39.5 us (23%)
  local copies, waits for them, and re-layouts  8.97 us (5%)
  matrix products  5.56 us (3%)
  other arithmetic  3.68 us (2%)
    pallas_call x4, Pallas kernels, run_chunk(): pl.pallas_call(functools.partial(chunk_kernel, head_count, turn), out_sha...  47.8 us
    ppermute x3, waiting for transfers between devices, next_place(): return lax.ppermute(block, 'heads', ring_pairs(count, 1))  19.7 us
    ppermute x3, waiting for transfers between devices, on_device_dense(): lax.ppermute(piece, 'heads', ring_pairs(head_count, distance))  18.7 us
    ppermute x12, waiting for transfers between devices, flip_row(): return lax.ppermute(block, 'ctx', partner_pairs(ctx_count, 2))  13.6 us
    ppermute x12, starting transfers between devices, flip_row(): return lax.ppermute(block, 'ctx', partner_pairs(ctx_count, 2))  12.9 us
    ppermute x3, waiting for transfers between devices, gather_direct(): lax.ppermute(block, 'heads', ring_pairs(count, step))  8.43 us
    ppermute x4, starting transfers between devices, from_behind(): return lax.ppermute(block, axis, route)  6.39 us
    ppermute x3, starting transfers between devices, on_device_dense(): lax.ppermute(piece, 'heads', ring_pairs(head_count, distance))  5.47 us
  transfers between devices with their start and end apart: 33, of which 12 were waited for; matrix products, arithmetic and copies ran while one was open for 8% of the time, Pallas kernels for 28%

profile of v2, /device:TPU:0, one launch (start us, length us, event | category | flops | bytes accessed | tf_op | source)
XLA Modules:
  0.0 171.1 jit_solution(18284447123536785280)
XLA Ops:
  0.5 2.6 %collective-permute-start = (bf16[128,2048]{1,0:T(8,128)(2,1)}, bf16[128,2048]{1,0:T(8,128)(2,1)S(1)}, u32[]{:S(2)}, u32[]{:S(2)}) collective-permute-start(bf16[128,2048]{1,0:T(8,128)(2,1)} %refs_8_.1), channel_id=1, source_target_pairs={{0,1},{1,2},{2,3},{3,0},{4,5},{5,6},{6,7},{7,4},{8,9},{9,10},{10,1... | collective-permute-start | bytes 1572872 | tf_op jit(solution)/shard_map/ppermute | solution.py:155
  3.1 1.5 collective-permute-start.1
  4.6 1.7 %copy.16 = bf16[2048,3,128]{0,2,1:T(8,128)(2,1)S(1)} copy(bf16[2048,3,128]{2,0,1:T(8,128)(2,1)} %param.13) | data formatting | bytes 3145728 | tf_op args[3]
  7.0 10.8 %collective-permute-done.refs_8_ = bf16[128,2048]{1,0:T(8,128)(2,1)S(1)} collective-permute-done((bf16[128,2048]{1,0:T(8,128)(2,1)}, bf16[128,2048]{1,0:T(8,128)(2,1)S(1)}, u32[]{:S(2)}, u32[]{:S(2)}) %collective-permute-start) | collective-permute-done | bytes 524320 | tf_op jit(solution)/shard_map/ppermute | solution.py:155
  18.0 1.0 collective-permute-start.3
  19.0 1.5 collective-permute-start.4
  20.5 1.6 collective-permute-start.6
  22.2 2.2 %collective-permute-start.8 = (bf16[32,2048]{1,0:T(8,128)(2,1)S(1)}, bf16[32,2048]{1,0:T(8,128)(2,1)S(1)}, u32[]{:S(2)}, u32[]{:S(2)}) collective-permute-start(bf16[32,2048]{1,0:T(8,128)(2,1)S(1)} %constant_dynamic-slice_fusion), channel_id=1, source_target_pairs={{0,3},{1,0},{2,1},{3,2},{4,7},{5,4},{6,5},{7,6},{8,11},{9,8},{10,9... | collective-permute-start | bytes 393224 | tf_op jit(solution)/shard_map/ppermute | solution.py:347
  24.4 1.6 collective-permute-start.7
  26.6 10.8 %collective-permute-done.6 = bf16[32,2048]{1,0:T(8,128)(2,1)S(1)} collective-permute-done((bf16[32,2048]{1,0:T(8,128)(2,1)S(1)}, bf16[32,2048]{1,0:T(8,128)(2,1)S(1)}, u32[]{:S(2)}, u32[]{:S(2)}) %collective-permute-start.6) | collective-permute-done | bytes 131104 | tf_op jit(solution)/shard_map/ppermute | solution.py:347
  37.4 2.3 %collective-permute-done.8 = bf16[32,2048]{1,0:T(8,128)(2,1)S(1)} collective-permute-done((bf16[32,2048]{1,0:T(8,128)(2,1)S(1)}, bf16[32,2048]{1,0:T(8,128)(2,1)S(1)}, u32[]{:S(2)}, u32[]{:S(2)}) %collective-permute-start.8) | collective-permute-done | bytes 131104 | tf_op jit(solution)/shard_map/ppermute | solution.py:347
  39.7 5.6 %collective-permute-done.7 = bf16[32,2048]{1,0:T(8,128)(2,1)S(1)} collective-permute-done((bf16[32,2048]{1,0:T(8,128)(2,1)S(1)}, bf16[32,2048]{1,0:T(8,128)(2,1)S(1)}, u32[]{:S(2)}, u32[]{:S(2)}) %collective-permute-start.7) | collective-permute-done | bytes 131104 | tf_op jit(solution)/shard_map/ppermute | solution.py:347
  45.4 1.6 collective-permute-start.10
  47.0 0.7 constant_dynamic-update-slice_fusion.3
  47.7 0.7 constant_dynamic-update-slice_fusion.2
  48.3 0.7 constant_dynamic-update-slice_fusion.1
  49.6 1.5 collective-permute-start.12
  51.1 1.0 slice_bitcast_fusion.1
  52.7 8.9 %collective-permute-done.9.refs_8_ = bf16[128,2048]{1,0:T(8,128)(2,1)} collective-permute-done((bf16[128,2048]{1,0:T(8,128)(2,1)S(1)}, bf16[128,2048]{1,0:T(8,128)(2,1)}, u32[]{:S(2)}, u32[]{:S(2)}) %collective-permute-start.9) | collective-permute-done | bytes 524320 | tf_op jit(solution)/shard_map/ppermute | solution.py:155
  61.6 2.4 %collective-permute-done.12 = bf16[128,2048]{1,0:T(8,128)(2,1)} collective-permute-done((bf16[128,2048]{1,0:T(8,128)(2,1)}, bf16[128,2048]{1,0:T(8,128)(2,1)}, u32[]{:S(2)}, u32[]{:S(2)}) %collective-permute-start.12) | collective-permute-done | bytes 524320 | tf_op jit(solution)/shard_map/ppermute | solution.py:355
  64.0 1.6 fusion.4
  65.7 1.3 collective-permute-start.16
  67.3 1.4 collective-permute-start.15
  68.7 2.3 %collective-permute-start.14 = (bf16[128,128]{1,0:T(8,128)(2,1)S(1)}, bf16[128,128]{1,0:T(8,128)(2,1)S(1)}, u32[]{:S(2)}, u32[]{:S(2)}) collective-permute-start(bf16[128,128]{1,0:T(8,128)(2,1)S(1)} %convolution_convert_fusion.4), channel_id=1, source_target_pairs={{0,8},{4,12},{1,9},{5,13},{2,10},{6,14},{3,11},{7,15},{16,24},{20,... | collective-permute-start | bytes 98312 | tf_op jit(solution)/shard_map/ppermute | solution.py:29
  71.0 1.4 collective-permute-start.13
  72.4 1.3 pad_maximum_fusion
  75.7 0.7 add_convert_fusion.4
  76.5 4.0 %collective-permute-start.18 = (bf16[544,128]{1,0:T(8,128)(2,1)S(1)}, bf16[544,128]{1,0:T(8,128)(2,1)S(1)}, u32[]{:S(2)}, u32[]{:S(2)}) collective-permute-start(bf16[544,128]{1,0:T(8,128)(2,1)S(1)} %pad_maximum_fusion.1.refs_0_), channel_id=1, source_target_pairs={{0,2},{1,3},{2,0},{3,1},{4,6},{5,7},{6,4},{7,5},{8,10},{9,11},{10,... | collective-permute-start | bytes 417800 | tf_op jit(solution)/shard_map/ppermute | solution.py:160
  81.3 3.5 %collective-permute-done.17.refs_1_ = bf16[544,128]{1,0:T(8,128)(2,1)S(1)} collective-permute-done((bf16[544,128]{1,0:T(8,128)(2,1)S(1)}, bf16[544,128]{1,0:T(8,128)(2,1)S(1)}, u32[]{:S(2)}, u32[]{:S(2)}) %collective-permute-start.17) | collective-permute-done | bytes 139296 | tf_op jit(solution)/shard_map/ppermute | solution.py:160
  85.4 4.9 %collective-permute-done.18.refs_2_ = bf16[544,128]{1,0:T(8,128)(2,1)S(1)} collective-permute-done((bf16[544,128]{1,0:T(8,128)(2,1)S(1)}, bf16[544,128]{1,0:T(8,128)(2,1)S(1)}, u32[]{:S(2)}, u32[]{:S(2)}) %collective-permute-start.18) | collective-permute-done | bytes 139296 | tf_op jit(solution)/shard_map/ppermute | solution.py:160
  90.9 1.5 collective-permute-start.23
  93.0 4.0 %collective-permute-done.22.refs_6_ = bf16[544,128]{1,0:T(8,128)(2,1)} collective-permute-done((bf16[544,128]{1,0:T(8,128)(2,1)S(1)}, bf16[544,128]{1,0:T(8,128)(2,1)}, u32[]{:S(2)}, u32[]{:S(2)}) %collective-permute-start.22) | collective-permute-done | bytes 139296 | tf_op jit(solution)/shard_map/ppermute | solution.py:165
  97.0 2.1 %collective-permute-done.23.refs_7_ = bf16[544,128]{1,0:T(8,128)(2,1)} collective-permute-done((bf16[544,128]{1,0:T(8,128)(2,1)S(1)}, bf16[544,128]{1,0:T(8,128)(2,1)}, u32[]{:S(2)}, u32[]{:S(2)}) %collective-permute-start.23) | collective-permute-done | bytes 139296 | tf_op jit(solution)/shard_map/ppermute | solution.py:165
  99.6 0.9 copy-done.2
  100.5 11.8 %chunk.7 = (bf16[128,2048]{1,0:T(8,128)(2,1)}, bf16[128,2048]{1,0:T(8,128)(2,1)}) custom-call(s32[7]{0:T(128)} %stack.85.place_ref, bf16[544,128]{1,0:T(8,128)(2,1)} %copy-done.3, bf16[544,128]{1,0:T(8,128)(2,1)} %copy-done.4, bf16[544,128]{1,0:T(8,128)(2,1)} %copy-done.5, bf16[544,128]{1,0:T(8,128)(2,1)} %copy-done.6, bf16[544,128]{1,0:T(8,128)(2,1)} %copy-done.7, ...), custom_call_target="tpu_custom_call" | custom-call | flops 5368709120 | bytes 18874368 | tf_op jit(solution)/shard_map/chunk/pallas_call | solution.py:286
  112.4 1.5 collective-permute-start.29
  114.5 12.0 %chunk.6 = (bf16[128,2048]{1,0:T(8,128)(2,1)}, bf16[128,2048]{1,0:T(8,128)(2,1)}) custom-call(s32[7]{0:T(128)} %stack.83.place_ref, bf16[544,128]{1,0:T(8,128)(2,1)} %copy-done.3, bf16[544,128]{1,0:T(8,128)(2,1)} %copy-done.4, bf16[544,128]{1,0:T(8,128)(2,1)} %copy-done.5, bf16[544,128]{1,0:T(8,128)(2,1)} %copy-done.6, bf16[544,128]{1,0:T(8,128)(2,1)} %copy-done.7, ...), custom_call_target="tpu_custom_call" | custom-call | flops 5368709120 | bytes 18874368 | tf_op jit(solution)/shard_map/chunk/pallas_call | solution.py:286
  126.5 0.9 collective-permute-start.28
  128.1 0.7 stack.81.place_ref
  128.7 12.0 %chunk.5 = (bf16[128,2048]{1,0:T(8,128)(2,1)}, bf16[128,2048]{1,0:T(8,128)(2,1)}) custom-call(s32[7]{0:T(128)} %stack.81.place_ref, bf16[544,128]{1,0:T(8,128)(2,1)} %copy-done.3, bf16[544,128]{1,0:T(8,128)(2,1)} %copy-done.4, bf16[544,128]{1,0:T(8,128)(2,1)} %copy-done.5, bf16[544,128]{1,0:T(8,128)(2,1)} %copy-done.6, bf16[544,128]{1,0:T(8,128)(2,1)} %copy-done.7, ...), custom_call_target="tpu_custom_call" | custom-call | flops 5368709120 | bytes 18874368 | tf_op jit(solution)/shard_map/chunk/pallas_call | solution.py:286
  140.7 1.5 collective-permute-start.27
  142.5 1.4 collective-permute-start.31
  143.8 0.7 stack.76.place_ref
  144.5 12.1 %chunk.4 = (bf16[128,2048]{1,0:T(8,128)(2,1)}, bf16[128,2048]{1,0:T(8,128)(2,1)}, bf16[128,2048]{1,0:T(8,128)(2,1)}) custom-call(s32[7]{0:T(128)} %stack.76.place_ref, bf16[544,128]{1,0:T(8,128)(2,1)} %copy-done.3, bf16[544,128]{1,0:T(8,128)(2,1)} %copy-done.4, bf16[544,128]{1,0:T(8,128)(2,1)} %copy-done.5, bf16[544,128]{1,0:T(8,128)(2,1)} %copy-done.6, ...), custom_call_target="tpu_custom_call" | custom-call | flops 5368709120 | bytes 18874368 | tf_op jit(solution)/shard_map/chunk/pallas_call | solution.py:286
  157.5 2.7 %collective-permute-start.32 = (bf16[128,2048]{1,0:T(8,128)(2,1)S(1)}, bf16[128,2048]{1,0:T(8,128)(2,1)S(1)}, u32[]{:S(2)}, u32[]{:S(2)}) collective-permute-start(bf16[128,2048]{1,0:T(8,128)(2,1)S(1)} %add_convert_fusion.1), channel_id=1, source_target_pairs={{0,1},{1,2},{2,3},{3,0},{4,5},{5,6},{6,7},{7,4},{8,9},{9,10},{10,1... | collective-permute-start | bytes 1572872 | tf_op jit(solution)/shard_map/ppermute | solution.py:418
  160.2 7.6 %collective-permute-done.25 = bf16[128,2048]{1,0:T(8,128)(2,1)S(1)} collective-permute-done((bf16[128,2048]{1,0:T(8,128)(2,1)}, bf16[128,2048]{1,0:T(8,128)(2,1)S(1)}, u32[]{:S(2)}, u32[]{:S(2)}) %collective-permute-start.25) | collective-permute-done | bytes 524320 | tf_op jit(solution)/shard_map/ppermute | solution.py:165
  167.7 2.2 %collective-permute-done.32 = bf16[128,2048]{1,0:T(8,128)(2,1)S(1)} collective-permute-done((bf16[128,2048]{1,0:T(8,128)(2,1)S(1)}, bf16[128,2048]{1,0:T(8,128)(2,1)S(1)}, u32[]{:S(2)}, u32[]{:S(2)}) %collective-permute-start.32) | collective-permute-done | bytes 524320 | tf_op jit(solution)/shard_map/ppermute | solution.py:418
  169.9 1.1 add_convert_fusion
  (98 shorter events, 11.1 us)
Async XLA Ops:
  0.0 20.5 %copy-start = (bf16[128,2048]{1,0:T(8,128)(2,1)S(1)}, bf16[128,2048]{1,0:T(8,128)(2,1)}, u32[]{:S(2)}) copy-start(bf16[128,2048]{1,0:T(8,128)(2,1)} %param.14) | copy-start | bytes 1572868
  0.0 17.9 %collective-permute-start.2 = (bf16[1,2048,768]{2,1,0:T(8,128)(2,1)}, bf16[1,2048,768]{2,1,0:T(8,128)(2,1)}, u32[]{:S(2)}, u32[]{:S(2)}) collective-permute-start(bf16[1,2048,768]{2,1,0:T(8,128)(2,1)} %refs_12_.7), channel_id=1, source_target_pairs={{0,4},{4,0},{8,12},{12,8},{1,5},{5,1},{9,13},{13,9},{2,6},{6,2},{1... | collective-permute-start | bytes 9437192 | tf_op jit(solution)/shard_map/ppermute | solution.py:169
  0.5 17.4 %collective-permute-start = (bf16[128,2048]{1,0:T(8,128)(2,1)}, bf16[128,2048]{1,0:T(8,128)(2,1)S(1)}, u32[]{:S(2)}, u32[]{:S(2)}) collective-permute-start(bf16[128,2048]{1,0:T(8,128)(2,1)} %refs_8_.1), channel_id=1, source_target_pairs={{0,1},{1,2},{2,3},{3,0},{4,5},{5,6},{6,7},{7,4},{8,9},{9,10},{10,1... | collective-permute-start | bytes 1572872 | tf_op jit(solution)/shard_map/ppermute | solution.py:155
  3.1 14.8 %collective-permute-start.1 = (bf16[128,2048]{1,0:T(8,128)(2,1)}, bf16[128,2048]{1,0:T(8,128)(2,1)}, u32[]{:S(2)}, u32[]{:S(2)}) collective-permute-start(bf16[128,2048]{1,0:T(8,128)(2,1)} %refs_8_.1), channel_id=1, source_target_pairs={{0,8},{4,12},{8,0},{12,4},{1,9},{5,13},{9,1},{13,5},{2,10},{6,14},... | collective-permute-start | bytes 1572872 | tf_op jit(solution)/shard_map/ppermute | solution.py:165
  6.4 38.9 %copy-start.18 = (f32[128,8]{0,1:T(8,128)S(1)}, f32[128,8]{0,1:T(8,128)}, u32[]{:S(2)}) copy-start(f32[128,8]{0,1:T(8,128)} %param.19) | copy-start | bytes 12292
  6.4 38.9 %copy-start.19 = (s32[128,8]{0,1:T(8,128)S(1)}, s32[128,8]{0,1:T(8,128)}, u32[]{:S(2)}) copy-start(s32[128,8]{0,1:T(8,128)} %param.18) | copy-start | bytes 12292
  17.9 34.3 %copy-start.10 = (bf16[128,2048]{1,0:T(8,128)(2,1)}, bf16[128,2048]{1,0:T(8,128)(2,1)S(1)}, u32[]{:S(2)}) copy-start(bf16[128,2048]{1,0:T(8,128)(2,1)S(1)} %collective-permute-done.refs_8_) | copy-start | bytes 1572868
  17.9 6.5 %collective-permute-start.5 = (bf16[1,2048,768]{2,1,0:T(8,128)(2,1)}, bf16[1,2048,768]{2,1,0:T(8,128)(2,1)}, u32[]{:S(2)}, u32[]{:S(2)}) collective-permute-start(bf16[1,2048,768]{2,1,0:T(8,128)(2,1)} %refs_13_.7), channel_id=1, source_target_pairs={{0,4},{4,0},{8,12},{12,8},{1,5},{5,1},{9,13},{13,9},{2,6},{6,2},{1... | collective-permute-start | bytes 9437192 | tf_op jit(solution)/shard_map/ppermute | solution.py:169
  18.0 21.7 %collective-permute-start.3 = (bf16[128,2048]{1,0:T(8,128)(2,1)S(1)}, bf16[128,2048]{1,0:T(8,128)(2,1)S(1)}, u32[]{:S(2)}, u32[]{:S(2)}) collective-permute-start(bf16[128,2048]{1,0:T(8,128)(2,1)S(1)} %collective-permute-done.refs_8_), channel_id=1, source_target_pairs={{0,1},{1,2},{2,3},{3,0},{4,5},{5,6},{6,7},{7,4},{8,9},{9,10},{10,1... | collective-permute-start | bytes 1572872 | tf_op jit(solution)/shard_map/ppermute | solution.py:155
  19.0 20.7 %collective-permute-start.4 = (bf16[128,2048]{1,0:T(8,128)(2,1)S(1)}, bf16[128,2048]{1,0:T(8,128)(2,1)}, u32[]{:S(2)}, u32[]{:S(2)}) collective-permute-start(bf16[128,2048]{1,0:T(8,128)(2,1)S(1)} %collective-permute-done.refs_8_), channel_id=1, source_target_pairs={{0,8},{4,12},{8,0},{12,4},{1,9},{5,13},{9,1},{13,5},{2,10},{6,14},... | collective-permute-start | bytes 1572872 | tf_op jit(solution)/shard_map/ppermute | solution.py:165
  20.5 16.9 %collective-permute-start.6 = (bf16[32,2048]{1,0:T(8,128)(2,1)S(1)}, bf16[32,2048]{1,0:T(8,128)(2,1)S(1)}, u32[]{:S(2)}, u32[]{:S(2)}) collective-permute-start(bf16[32,2048]{1,0:T(8,128)(2,1)S(1)} %constant_dynamic-slice_fusion), channel_id=1, source_target_pairs={{0,1},{1,2},{2,3},{3,0},{4,5},{5,6},{6,7},{7,4},{8,9},{9,10},{10,1... | collective-permute-start | bytes 393224 | tf_op jit(solution)/shard_map/ppermute | solution.py:347
  22.2 17.5 %collective-permute-start.8 = (bf16[32,2048]{1,0:T(8,128)(2,1)S(1)}, bf16[32,2048]{1,0:T(8,128)(2,1)S(1)}, u32[]{:S(2)}, u32[]{:S(2)}) collective-permute-start(bf16[32,2048]{1,0:T(8,128)(2,1)S(1)} %constant_dynamic-slice_fusion), channel_id=1, source_target_pairs={{0,3},{1,0},{2,1},{3,2},{4,7},{5,4},{6,5},{7,6},{8,11},{9,8},{10,9... | collective-permute-start | bytes 393224 | tf_op jit(solution)/shard_map/ppermute | solution.py:347
  24.4 20.9 %collective-permute-start.7 = (bf16[32,2048]{1,0:T(8,128)(2,1)S(1)}, bf16[32,2048]{1,0:T(8,128)(2,1)S(1)}, u32[]{:S(2)}, u32[]{:S(2)}) collective-permute-start(bf16[32,2048]{1,0:T(8,128)(2,1)S(1)} %constant_dynamic-slice_fusion), channel_id=1, source_target_pairs={{0,2},{1,3},{2,0},{3,1},{4,6},{5,7},{6,4},{7,5},{8,10},{9,11},{10,... | collective-permute-start | bytes 393224 | tf_op jit(solution)/shard_map/ppermute | solution.py:347
  39.7 26.0 %copy-start.11 = (bf16[128,2048]{1,0:T(8,128)(2,1)}, bf16[128,2048]{1,0:T(8,128)(2,1)S(1)}, u32[]{:S(2)}) copy-start(bf16[128,2048]{1,0:T(8,128)(2,1)S(1)} %collective-permute-done.3.refs_8_) | copy-start | bytes 1572868
  45.3 18.7 %collective-permute-start.11 = (bf16[1,768,2048]{2,1,0:T(8,128)(2,1)}, bf16[1,768,2048]{2,1,0:T(8,128)(2,1)}, u32[]{:S(2)}, u32[]{:S(2)}) collective-permute-start(bf16[1,768,2048]{2,1,0:T(8,128)(2,1)} %refs_14_.7), channel_id=1, source_target_pairs={{0,4},{4,0},{8,12},{12,8},{1,5},{5,1},{9,13},{13,9},{2,6},{6,2},{1... | collective-permute-start | bytes 9437192 | tf_op jit(solution)/shard_map/ppermute | solution.py:169
  45.4 16.3 %collective-permute-start.9 = (bf16[128,2048]{1,0:T(8,128)(2,1)S(1)}, bf16[128,2048]{1,0:T(8,128)(2,1)}, u32[]{:S(2)}, u32[]{:S(2)}) collective-permute-start(bf16[128,2048]{1,0:T(8,128)(2,1)S(1)} %collective-permute-done.3.refs_8_), channel_id=1, source_target_pairs={{0,1},{1,2},{2,3},{3,0},{4,5},{5,6},{6,7},{7,4},{8,9},{9,10},{10,1... | collective-permute-start | bytes 1572872 | tf_op jit(solution)/shard_map/ppermute | solution.py:155
  45.4 16.2 %collective-permute-start.10 = (bf16[128,2048]{1,0:T(8,128)(2,1)S(1)}, bf16[128,2048]{1,0:T(8,128)(2,1)}, u32[]{:S(2)}, u32[]{:S(2)}) collective-permute-start(bf16[128,2048]{1,0:T(8,128)(2,1)S(1)} %collective-permute-done.3.refs_8_), channel_id=1, source_target_pairs={{0,8},{4,12},{8,0},{12,4},{1,9},{5,13},{9,1},{13,5},{2,10},{6,14},... | collective-permute-start | bytes 1572872 | tf_op jit(solution)/shard_map/ppermute | solution.py:165
  49.6 14.4 %collective-permute-start.12 = (bf16[128,2048]{1,0:T(8,128)(2,1)}, bf16[128,2048]{1,0:T(8,128)(2,1)}, u32[]{:S(2)}, u32[]{:S(2)}) collective-permute-start(bf16[128,2048]{1,0:T(8,128)(2,1)} %constant_dynamic-update-slice_fusion), channel_id=1, source_target_pairs={{0,16},{16,0},{1,17},{17,1},{2,18},{18,2},{3,19},{19,3},{4,20},{20... | collective-permute-start | bytes 1572872 | tf_op jit(solution)/shard_map/ppermute | solution.py:355
  65.7 8.0 %collective-permute-start.16 = (bf16[512,256]{1,0:T(8,128)(2,1)S(1)}, bf16[512,256]{1,0:T(8,128)(2,1)S(1)}, u32[]{:S(2)}, u32[]{:S(2)}) collective-permute-start(bf16[512,256]{1,0:T(8,128)(2,1)S(1)} %slice.39), channel_id=1, source_target_pairs={{0,4},{4,8},{8,12},{1,5},{5,9},{9,13},{2,6},{6,10},{10,14},{3,7},{... | collective-permute-start | bytes 786440 | tf_op jit(solution)/shard_map/ppermute | solution.py:29
  67.3 8.0 %collective-permute-start.15 = (bf16[128,128]{1,0:T(8,128)(2,1)S(1)}, bf16[128,128]{1,0:T(8,128)(2,1)S(1)}, u32[]{:S(2)}, u32[]{:S(2)}) collective-permute-start(bf16[128,128]{1,0:T(8,128)(2,1)S(1)} %convolution_convert_fusion.4), channel_id=1, source_target_pairs={{0,12},{1,13},{2,14},{3,15},{16,28},{17,29},{18,30},{19,31}} | collective-permute-start | bytes 98312 | tf_op jit(solution)/shard_map/ppermute | solution.py:29
  68.7 6.6 %collective-permute-start.14 = (bf16[128,128]{1,0:T(8,128)(2,1)S(1)}, bf16[128,128]{1,0:T(8,128)(2,1)S(1)}, u32[]{:S(2)}, u32[]{:S(2)}) collective-permute-start(bf16[128,128]{1,0:T(8,128)(2,1)S(1)} %convolution_convert_fusion.4), channel_id=1, source_target_pairs={{0,8},{4,12},{1,9},{5,13},{2,10},{6,14},{3,11},{7,15},{16,24},{20,... | collective-permute-start | bytes 98312 | tf_op jit(solution)/shard_map/ppermute | solution.py:29
  71.0 4.3 %collective-permute-start.13 = (bf16[128,128]{1,0:T(8,128)(2,1)S(1)}, bf16[128,128]{1,0:T(8,128)(2,1)S(1)}, u32[]{:S(2)}, u32[]{:S(2)}) collective-permute-start(bf16[128,128]{1,0:T(8,128)(2,1)S(1)} %convolution_convert_fusion.4), channel_id=1, source_target_pairs={{0,4},{4,8},{8,12},{1,5},{5,9},{9,13},{2,6},{6,10},{10,14},{3,7},{... | collective-permute-start | bytes 98312 | tf_op jit(solution)/shard_map/ppermute | solution.py:29
  75.2 24.4 %collective-permute-start.24 = (bf16[2,128,2048]{2,1,0:T(8,128)(2,1)S(1)}, bf16[2,128,2048]{2,1,0:T(8,128)(2,1)S(1)}, u32[]{:S(2)}, u32[]{:S(2)}) collective-permute-start(bf16[2,128,2048]{2,1,0:T(8,128)(2,1)S(1)} %pad_maximum_fusion), channel_id=1, source_target_pairs={{0,4},{4,0},{8,12},{12,8},{1,5},{5,1},{9,13},{13,9},{2,6},{6,2},{1... | collective-permute-start | bytes 3145736 | tf_op jit(solution)/shard_map/ppermute | solution.py:169
  76.4 23.2 %copy-start.3 = (bf16[544,128]{1,0:T(8,128)(2,1)}, bf16[544,128]{1,0:T(8,128)(2,1)S(1)}, u32[]{:S(2)}) copy-start(bf16[544,128]{1,0:T(8,128)(2,1)S(1)} %pad_maximum_fusion.1.refs_0_) | copy-start | bytes 417796
  76.4 8.4 %collective-permute-start.17 = (bf16[544,128]{1,0:T(8,128)(2,1)S(1)}, bf16[544,128]{1,0:T(8,128)(2,1)S(1)}, u32[]{:S(2)}, u32[]{:S(2)}) collective-permute-start(bf16[544,128]{1,0:T(8,128)(2,1)S(1)} %pad_maximum_fusion.1.refs_0_), channel_id=1, source_target_pairs={{0,1},{1,2},{2,3},{3,0},{4,5},{5,6},{6,7},{7,4},{8,9},{9,10},{10,1... | collective-permute-start | bytes 417800 | tf_op jit(solution)/shard_map/ppermute | solution.py:160
  76.5 13.8 %collective-permute-start.18 = (bf16[544,128]{1,0:T(8,128)(2,1)S(1)}, bf16[544,128]{1,0:T(8,128)(2,1)S(1)}, u32[]{:S(2)}, u32[]{:S(2)}) collective-permute-start(bf16[544,128]{1,0:T(8,128)(2,1)S(1)} %pad_maximum_fusion.1.refs_0_), channel_id=1, source_target_pairs={{0,2},{1,3},{2,0},{3,1},{4,6},{5,7},{6,4},{7,5},{8,10},{9,11},{10,... | collective-permute-start | bytes 417800 | tf_op jit(solution)/shard_map/ppermute | solution.py:160
  80.5 10.4 %collective-permute-start.19 = (bf16[544,128]{1,0:T(8,128)(2,1)S(1)}, bf16[544,128]{1,0:T(8,128)(2,1)S(1)}, u32[]{:S(2)}, u32[]{:S(2)}) collective-permute-start(bf16[544,128]{1,0:T(8,128)(2,1)S(1)} %pad_maximum_fusion.1.refs_0_), channel_id=1, source_target_pairs={{0,3},{1,0},{2,1},{3,2},{4,7},{5,4},{6,5},{7,6},{8,11},{9,8},{10,9... | collective-permute-start | bytes 417800 | tf_op jit(solution)/shard_map/ppermute | solution.py:160
  80.8 12.2 %collective-permute-start.20 = (bf16[544,128]{1,0:T(8,128)(2,1)S(1)}, bf16[544,128]{1,0:T(8,128)(2,1)S(1)}, u32[]{:S(2)}, u32[]{:S(2)}) collective-permute-start(bf16[544,128]{1,0:T(8,128)(2,1)S(1)} %pad_maximum_fusion.1.refs_0_), channel_id=1, source_target_pairs={{0,8},{4,12},{8,0},{12,4},{1,9},{5,13},{9,1},{13,5},{2,10},{6,14},... | collective-permute-start | bytes 417800 | tf_op jit(solution)/shard_map/ppermute | solution.py:165
  84.8 14.8 %copy-start.4 = (bf16[544,128]{1,0:T(8,128)(2,1)}, bf16[544,128]{1,0:T(8,128)(2,1)S(1)}, u32[]{:S(2)}) copy-start(bf16[544,128]{1,0:T(8,128)(2,1)S(1)} %collective-permute-done.17.refs_1_) | copy-start | bytes 417796
  84.8 8.1 %collective-permute-start.21 = (bf16[544,128]{1,0:T(8,128)(2,1)S(1)}, bf16[544,128]{1,0:T(8,128)(2,1)S(1)}, u32[]{:S(2)}, u32[]{:S(2)}) collective-permute-start(bf16[544,128]{1,0:T(8,128)(2,1)S(1)} %collective-permute-done.17.refs_1_), channel_id=1, source_target_pairs={{0,8},{4,12},{8,0},{12,4},{1,9},{5,13},{9,1},{13,5},{2,10},{6,14},... | collective-permute-start | bytes 417800 | tf_op jit(solution)/shard_map/ppermute | solution.py:165
  90.3 9.3 %copy-start.5 = (bf16[544,128]{1,0:T(8,128)(2,1)}, bf16[544,128]{1,0:T(8,128)(2,1)S(1)}, u32[]{:S(2)}) copy-start(bf16[544,128]{1,0:T(8,128)(2,1)S(1)} %collective-permute-done.18.refs_2_) | copy-start | bytes 417796
  90.3 6.6 %collective-permute-start.22 = (bf16[544,128]{1,0:T(8,128)(2,1)S(1)}, bf16[544,128]{1,0:T(8,128)(2,1)}, u32[]{:S(2)}, u32[]{:S(2)}) collective-permute-start(bf16[544,128]{1,0:T(8,128)(2,1)S(1)} %collective-permute-done.18.refs_2_), channel_id=1, source_target_pairs={{0,8},{4,12},{8,0},{12,4},{1,9},{5,13},{9,1},{13,5},{2,10},{6,14},... | collective-permute-start | bytes 417800 | tf_op jit(solution)/shard_map/ppermute | solution.py:165
  90.9 8.7 %copy-start.6 = (bf16[544,128]{1,0:T(8,128)(2,1)}, bf16[544,128]{1,0:T(8,128)(2,1)S(1)}, u32[]{:S(2)}) copy-start(bf16[544,128]{1,0:T(8,128)(2,1)S(1)} %collective-permute-done.19.refs_3_) | copy-start | bytes 417796
  90.9 8.1 %collective-permute-start.23 = (bf16[544,128]{1,0:T(8,128)(2,1)S(1)}, bf16[544,128]{1,0:T(8,128)(2,1)}, u32[]{:S(2)}, u32[]{:S(2)}) collective-permute-start(bf16[544,128]{1,0:T(8,128)(2,1)S(1)} %collective-permute-done.19.refs_3_), channel_id=1, source_target_pairs={{0,8},{4,12},{8,0},{12,4},{1,9},{5,13},{9,1},{13,5},{2,10},{6,14},... | collective-permute-start | bytes 417800 | tf_op jit(solution)/shard_map/ppermute | solution.py:165
  93.0 6.6 %copy-start.8 = (bf16[544,128]{1,0:T(8,128)(2,1)}, bf16[544,128]{1,0:T(8,128)(2,1)S(1)}, u32[]{:S(2)}) copy-start(bf16[544,128]{1,0:T(8,128)(2,1)S(1)} %collective-permute-done.21.refs_5_) | copy-start | bytes 417796
  99.0 15.5 %collective-permute-start.26 = (bf16[128,2048]{1,0:T(8,128)(2,1)}, bf16[128,2048]{1,0:T(8,128)(2,1)}, u32[]{:S(2)}, u32[]{:S(2)}) collective-permute-start(bf16[128,2048]{1,0:T(8,128)(2,1)} %collective-permute-done.9.refs_8_), channel_id=1, source_target_pairs={{0,8},{4,12},{8,0},{12,4},{1,9},{5,13},{9,1},{13,5},{2,10},{6,14},... | collective-permute-start | bytes 1572872 | tf_op jit(solution)/shard_map/ppermute | solution.py:165
  112.4 15.0 %collective-permute-start.29 = (bf16[128,2048]{1,0:T(8,128)(2,1)}, bf16[128,2048]{1,0:T(8,128)(2,1)S(1)}, u32[]{:S(2)}, u32[]{:S(2)}) collective-permute-start(bf16[128,2048]{1,0:T(8,128)(2,1)} %get-tuple-element.74), channel_id=1, source_target_pairs={{0,8},{4,12},{8,0},{12,4},{1,9},{5,13},{9,1},{13,5},{2,10},{6,14},... | collective-permute-start | bytes 1572872 | tf_op jit(solution)/shard_map/ppermute | solution.py:165
  114.5 12.8 %copy-start.14 = (bf16[128,2048]{1,0:T(8,128)(2,1)S(1)}, bf16[128,2048]{1,0:T(8,128)(2,1)}, u32[]{:S(2)}) copy-start(bf16[128,2048]{1,0:T(8,128)(2,1)} %get-tuple-element.73) | copy-start | bytes 1572868
  126.5 15.8 %collective-permute-start.28 = (bf16[128,2048]{1,0:T(8,128)(2,1)}, bf16[128,2048]{1,0:T(8,128)(2,1)S(1)}, u32[]{:S(2)}, u32[]{:S(2)}) collective-permute-start(bf16[128,2048]{1,0:T(8,128)(2,1)} %get-tuple-element.71), channel_id=1, source_target_pairs={{0,8},{4,12},{8,0},{12,4},{1,9},{5,13},{9,1},{13,5},{2,10},{6,14},... | collective-permute-start | bytes 1572872 | tf_op jit(solution)/shard_map/ppermute | solution.py:165
  127.5 14.8 %collective-permute-start.30 = (bf16[128,2048]{1,0:T(8,128)(2,1)S(1)}, bf16[128,2048]{1,0:T(8,128)(2,1)S(1)}, u32[]{:S(2)}, u32[]{:S(2)}) collective-permute-start(bf16[128,2048]{1,0:T(8,128)(2,1)S(1)} %add_convert_fusion.3), channel_id=1, source_target_pairs={{0,1},{1,2},{2,3},{3,0},{4,5},{5,6},{6,7},{7,4},{8,9},{9,10},{10,1... | collective-permute-start | bytes 1572872 | tf_op jit(solution)/shard_map/ppermute | solution.py:418
  128.7 13.5 %copy-start.16 = (bf16[128,2048]{1,0:T(8,128)(2,1)S(1)}, bf16[128,2048]{1,0:T(8,128)(2,1)}, u32[]{:S(2)}) copy-start(bf16[128,2048]{1,0:T(8,128)(2,1)} %get-tuple-element.70) | copy-start | bytes 1572868
  140.7 16.6 %collective-permute-start.27 = (bf16[128,2048]{1,0:T(8,128)(2,1)}, bf16[128,2048]{1,0:T(8,128)(2,1)S(1)}, u32[]{:S(2)}, u32[]{:S(2)}) collective-permute-start(bf16[128,2048]{1,0:T(8,128)(2,1)} %get-tuple-element.67), channel_id=1, source_target_pairs={{0,8},{4,12},{8,0},{12,4},{1,9},{5,13},{9,1},{13,5},{2,10},{6,14},... | collective-permute-start | bytes 1572872 | tf_op jit(solution)/shard_map/ppermute | solution.py:165
  142.5 14.8 %collective-permute-start.31 = (bf16[128,2048]{1,0:T(8,128)(2,1)S(1)}, bf16[128,2048]{1,0:T(8,128)(2,1)S(1)}, u32[]{:S(2)}, u32[]{:S(2)}) collective-permute-start(bf16[128,2048]{1,0:T(8,128)(2,1)S(1)} %add_convert_fusion.2), channel_id=1, source_target_pairs={{0,1},{1,2},{2,3},{3,0},{4,5},{5,6},{6,7},{7,4},{8,9},{9,10},{10,1... | collective-permute-start | bytes 1572872 | tf_op jit(solution)/shard_map/ppermute | solution.py:418
  144.5 12.8 %copy-start.15 = (bf16[128,2048]{1,0:T(8,128)(2,1)S(1)}, bf16[128,2048]{1,0:T(8,128)(2,1)}, u32[]{:S(2)}) copy-start(bf16[128,2048]{1,0:T(8,128)(2,1)} %get-tuple-element.66) | copy-start | bytes 1572868
  156.6 13.3 %copy-start.12 = (bf16[128,2048]{1,0:T(8,128)(2,1)S(1)}, bf16[128,2048]{1,0:T(8,128)(2,1)}, u32[]{:S(2)}) copy-start(bf16[128,2048]{1,0:T(8,128)(2,1)} %get-tuple-element.63) | copy-start | bytes 1572868
  156.6 13.3 %copy-start.13 = (bf16[128,2048]{1,0:T(8,128)(2,1)S(1)}, bf16[128,2048]{1,0:T(8,128)(2,1)}, u32[]{:S(2)}) copy-start(bf16[128,2048]{1,0:T(8,128)(2,1)} %get-tuple-element.62) | copy-start | bytes 1572868
  156.6 11.1 %collective-permute-start.25 = (bf16[128,2048]{1,0:T(8,128)(2,1)}, bf16[128,2048]{1,0:T(8,128)(2,1)S(1)}, u32[]{:S(2)}, u32[]{:S(2)}) collective-permute-start(bf16[128,2048]{1,0:T(8,128)(2,1)} %get-tuple-element.64), channel_id=1, source_target_pairs={{0,8},{4,12},{8,0},{12,4},{1,9},{5,13},{9,1},{13,5},{2,10},{6,14},... | collective-permute-start | bytes 1572872 | tf_op jit(solution)/shard_map/ppermute | solution.py:165
  157.5 12.4 %collective-permute-start.32 = (bf16[128,2048]{1,0:T(8,128)(2,1)S(1)}, bf16[128,2048]{1,0:T(8,128)(2,1)S(1)}, u32[]{:S(2)}, u32[]{:S(2)}) collective-permute-start(bf16[128,2048]{1,0:T(8,128)(2,1)S(1)} %add_convert_fusion.1), channel_id=1, source_target_pairs={{0,1},{1,2},{2,3},{3,0},{4,5},{5,6},{6,7},{7,4},{8,9},{9,10},{10,1... | collective-permute-start | bytes 1572872 | tf_op jit(solution)/shard_map/ppermute | solution.py:418
  (5 other events, 16.5 us)

commit v3 on v2

--- a/solution.py
+++ b/solution.py
@@ -161,6 +161,16 @@
     ]
 
 
+def gather_both_ways(block, count):
+    parts = [block] + [None] * (count - 1)
+    for step in range(1, count // 2 + 1):
+        parts[step] = lax.ppermute(parts[step - 1], "heads", ring_pairs(count, 1))
+        if step < count - step:
+            before = parts[(1 - step) % count]
+            parts[-step] = lax.ppermute(before, "heads", ring_pairs(count, -1))
+    return parts
+
+
 def flip_row(block, ctx_count):
     return lax.ppermute(block, "ctx", partner_pairs(ctx_count, 2))
 
@@ -187,7 +197,7 @@
     row_count, model_width = outs[0].shape
     slab_rows = row_count * head_count
     experts, mark_rows = narrow_bufs.shape[0], mark_buf.shape[1]
-    first = pl.multiple_of(place_ref[0], row_count)
+    first = pl.multiple_of(place_ref[turn], row_count)
 
     pairs = []
     for side, (heads_in, tokens_in) in enumerate(
@@ -202,7 +212,7 @@
     group_count = near_out_w.shape[0]
     for core, pieces in enumerate((near_out_w, far_out_w)):
         for group in range(group_count):
-            slot = place_ref[3 + core * group_count + group]
+            slot = place_ref[head_count + 2 + core * group_count + group]
             pairs.append((pieces.at[group], w_out_buf.at[:, slot]))
     small = [
         pltpu.make_async_copy(source, target, small_sems.at[i])
@@ -233,7 +243,7 @@
 
     spots = lax.rem(lax.broadcasted_iota(jnp.int32, (mark_rows, HDIM), 0), mark_rows // 2)
     for expert in range(experts):
-        chosen = jnp.where(spots == place_ref[1 + expert], 1.0, 0.0).astype(jnp.bfloat16)
+        chosen = jnp.where(spots == place_ref[head_count + expert], 1.0, 0.0).astype(jnp.bfloat16)
         gating = jnp.concatenate(
             [
                 lax.dot_general(
@@ -334,6 +344,16 @@
         part = jnp.dot(blocks[s], w_flat, preferred_element_type=jnp.float32)
         return lax.dynamic_update_slice_in_dim(projected, part.astype(jnp.bfloat16), starts[s], 0)
 
+    own_expert = ctx * head_count + place
+    other_expert = (ctx ^ 1) * head_count + place
+
+    group = lax.axis_index("groups")
+    slots = [
+        ((ctx % 2) ^ side) * group_count + (group ^ other)
+        for side in range(2)
+        for other in range(group_count)
+    ]
+    where = jnp.stack([*starts, own_expert, other_expert, *slots])
     experts = [w_gate, w_up, w_down]
     blocks, across, swapped = [tokens], [], []
     pieces = [w_out_piece(w_out, group_count)] + [None] * (head_count - 1)
@@ -346,8 +366,8 @@
             piece = after(pieces[0], blocks[s], swapped[s])
             pieces[distance] = lax.ppermute(piece, "heads", ring_pairs(head_count, distance))
         extra = (pieces, halves)[s - 1] if s else []
-        blocks[-1], across[-1], swapped[-1], projected, *extra = lax.optimization_barrier(
-            (blocks[-1], across[-1], swapped[-1], projected, *extra)
+        blocks[-1], across[-1], swapped[-1], projected, where, *extra = lax.optimization_barrier(
+            (blocks[-1], across[-1], swapped[-1], projected, where, *extra)
         )
         if s == 1:
             halves = [jnp.concatenate(extra, axis=0)]
@@ -364,8 +384,11 @@
     arrived = from_behind(projected[:, HDIM:], "ctx", 1)
     start_state = state_in[0]
     packed_state = local_state.astype(jnp.bfloat16)
-    for distance in range(1, ctx_count):
+    for distance in range(2, ctx_count):
         start_state = start_state + from_behind(packed_state, "ctx", distance).astype(jnp.float32)
+    start_state = start_state + jnp.dot(
+        arrived[:, :HDIM].T, arrived[:, HDIM:], preferred_element_type=jnp.float32
+    )
     past = jnp.concatenate([past_kv[0], past_kv[1]], axis=1)
     half = after(half, arrived)
     w_out_halves = [
@@ -394,20 +417,9 @@
     near_heads = gather_direct(jnp.concatenate([heads_out, marks], axis=0), head_count)
     far_heads = [flip_row(part, ctx_count) for part in near_heads]
     across.append(flip_row(after(blocks[-1], *far_heads), ctx_count))
-    own_expert = ctx * head_count + place
-    other_expert = (ctx ^ 1) * head_count + place
-
     across[2] = after(across[2], across[-1])
-    group = lax.axis_index("groups")
-    slots = [
-        ((ctx % 2) ^ side) * group_count + (group ^ other)
-        for side in range(2)
-        for other in range(group_count)
-    ]
-
     carry = None
     for s in list(range(1, head_count)) + [0]:
-        where = jnp.stack([starts[s], own_expert, other_expert, *slots])
         near, far, *hidden = run_chunk(
             s, where, near_heads, far_heads, blocks[s], across[s], w_out_halves, experts
         )

time: 171 us -> 169 us (0.988)
  local copies, waits for them, and re-layouts: 8.97 us -> 6.99 us
    ppermute x12, starting transfers between devices: 12.9 us -> 15.8 us  [flip_row(): return lax.ppermute(block, 'ctx', partner_pairs(ctx_count, 2))]
    ppermute x3, waiting for transfers between devices: 8.43 us -> 5.64 us  [gather_direct(): lax.ppermute(block, 'heads', ring_pairs(count, step))]
    ppermute x3, waiting for transfers between devices: 2.2 us -> 4.2 us  [on_device_dense(): lax.ppermute(joined.astype(jnp.bfloat16), 'heads', ring_pairs(head_count,...]
    another operation x4 -> x1, local copies, waits for them, and re-layouts: 2.55 us -> 0.58 us  [on_device_dense(): where = jnp.stack([*starts, own_expert, other_expert, *slots])]
    ppermute x4 -> x3, starting transfers between devices: 6.39 us -> 5 us  [from_behind(): return lax.ppermute(block, axis, route)]
    unnamed x44 -> x50, local copies, waits for them, and re-layouts: 4.69 us -> 4.67 us
  transfers between devices with their start and end apart: 33 -> 32, of which waited for: 12 -> 14; matrix products, arithmetic and copies ran while one was open for 8% -> 7% of each run, Pallas kernels for 28% -> 28%
where the time goes in v3:
time: 169 us
  waiting for transfers between devices  63.8 us (38%)
  Pallas kernels  47.4 us (28%)
  starting transfers between devices  40.7 us (24%)
  local copies, waits for them, and re-layouts  6.99 us (4%)
  matrix products  5.77 us (3%)
  other arithmetic  3.68 us (2%)
    pallas_call x4, Pallas kernels, run_chunk(): pl.pallas_call(functools.partial(chunk_kernel, head_count, turn), out_sha...  47.4 us
    ppermute x3, waiting for transfers between devices, next_place(): return lax.ppermute(block, 'heads', ring_pairs(count, 1))  19.1 us
    ppermute x3, waiting for transfers between devices, on_device_dense(): lax.ppermute(piece, 'heads', ring_pairs(head_count, distance))  18.7 us
    ppermute x12, starting transfers between devices, flip_row(): return lax.ppermute(block, 'ctx', partner_pairs(ctx_count, 2))  15.8 us
    ppermute x12, waiting for transfers between devices, flip_row(): return lax.ppermute(block, 'ctx', partner_pairs(ctx_count, 2))  13.8 us
    ppermute x3, waiting for transfers between devices, gather_direct(): lax.ppermute(block, 'heads', ring_pairs(count, step))  5.64 us
    ppermute x3, starting transfers between devices, on_device_dense(): lax.ppermute(piece, 'heads', ring_pairs(head_count, distance))  5.47 us
    ppermute x3, starting transfers between devices, from_behind(): return lax.ppermute(block, axis, route)  5 us
  transfers between devices with their start and end apart: 32, of which 14 were waited for; matrix products, arithmetic and copies ran while one was open for 7% of the time, Pallas kernels for 28%

profile of v3, /device:TPU:0, one launch (start us, length us, event | category | flops | bytes accessed | tf_op | source)
XLA Modules:
  0.0 168.8 jit_solution(17853197992874410815)
XLA Ops:
  0.5 2.6 %collective-permute-start = (bf16[128,2048]{1,0:T(8,128)(2,1)}, bf16[128,2048]{1,0:T(8,128)(2,1)S(1)}, u32[]{:S(2)}, u32[]{:S(2)}) collective-permute-start(bf16[128,2048]{1,0:T(8,128)(2,1)} %refs_8_.1), channel_id=1, source_target_pairs={{0,1},{1,2},{2,3},{3,0},{4,5},{5,6},{6,7},{7,4},{8,9},{9,10},{10,1... | collective-permute-start | bytes 1572872 | tf_op jit(solution)/shard_map/ppermute | solution.py:155
  3.1 1.5 collective-permute-start.1
  4.6 1.7 %copy.16 = bf16[2048,3,128]{0,2,1:T(8,128)(2,1)S(1)} copy(bf16[2048,3,128]{2,0,1:T(8,128)(2,1)} %param.13) | data formatting | bytes 3145728 | tf_op args[3]
  7.7 10.2 %collective-permute-done.refs_8_ = bf16[128,2048]{1,0:T(8,128)(2,1)S(1)} collective-permute-done((bf16[128,2048]{1,0:T(8,128)(2,1)}, bf16[128,2048]{1,0:T(8,128)(2,1)S(1)}, u32[]{:S(2)}, u32[]{:S(2)}) %collective-permute-start) | collective-permute-done | bytes 524320 | tf_op jit(solution)/shard_map/ppermute | solution.py:155
  18.0 1.0 collective-permute-start.3
  19.0 1.5 collective-permute-start.4
  20.5 1.6 collective-permute-start.6
  22.2 2.2 %collective-permute-start.8 = (bf16[32,2048]{1,0:T(8,128)(2,1)S(1)}, bf16[32,2048]{1,0:T(8,128)(2,1)S(1)}, u32[]{:S(2)}, u32[]{:S(2)}) collective-permute-start(bf16[32,2048]{1,0:T(8,128)(2,1)S(1)} %constant_dynamic-slice_fusion), channel_id=1, source_target_pairs={{0,3},{1,0},{2,1},{3,2},{4,7},{5,4},{6,5},{7,6},{8,11},{9,8},{10,9... | collective-permute-start | bytes 393224 | tf_op jit(solution)/shard_map/ppermute | solution.py:367
  24.4 1.6 collective-permute-start.7
  26.6 10.8 %collective-permute-done.6 = bf16[32,2048]{1,0:T(8,128)(2,1)S(1)} collective-permute-done((bf16[32,2048]{1,0:T(8,128)(2,1)S(1)}, bf16[32,2048]{1,0:T(8,128)(2,1)S(1)}, u32[]{:S(2)}, u32[]{:S(2)}) %collective-permute-start.6) | collective-permute-done | bytes 131104 | tf_op jit(solution)/shard_map/ppermute | solution.py:367
  37.4 2.3 %collective-permute-done.8 = bf16[32,2048]{1,0:T(8,128)(2,1)S(1)} collective-permute-done((bf16[32,2048]{1,0:T(8,128)(2,1)S(1)}, bf16[32,2048]{1,0:T(8,128)(2,1)S(1)}, u32[]{:S(2)}, u32[]{:S(2)}) %collective-permute-start.8) | collective-permute-done | bytes 131104 | tf_op jit(solution)/shard_map/ppermute | solution.py:367
  39.7 5.6 %collective-permute-done.7 = bf16[32,2048]{1,0:T(8,128)(2,1)S(1)} collective-permute-done((bf16[32,2048]{1,0:T(8,128)(2,1)S(1)}, bf16[32,2048]{1,0:T(8,128)(2,1)S(1)}, u32[]{:S(2)}, u32[]{:S(2)}) %collective-permute-start.7) | collective-permute-done | bytes 131104 | tf_op jit(solution)/shard_map/ppermute | solution.py:367
  45.4 1.6 collective-permute-start.10
  47.0 0.7 constant_dynamic-update-slice_fusion.3
  47.7 0.6 constant_dynamic-update-slice_fusion.2
  48.3 0.7 constant_dynamic-update-slice_fusion.1
  49.0 0.6 constant_dynamic-update-slice_fusion
  49.6 1.5 collective-permute-start.12
  51.1 1.0 slice_bitcast_fusion.1
  52.7 8.9 %collective-permute-done.9.refs_8_ = bf16[128,2048]{1,0:T(8,128)(2,1)} collective-permute-done((bf16[128,2048]{1,0:T(8,128)(2,1)S(1)}, bf16[128,2048]{1,0:T(8,128)(2,1)}, u32[]{:S(2)}, u32[]{:S(2)}) %collective-permute-start.9) | collective-permute-done | bytes 524320 | tf_op jit(solution)/shard_map/ppermute | solution.py:155
  61.6 2.3 %collective-permute-done.12 = bf16[128,2048]{1,0:T(8,128)(2,1)} collective-permute-done((bf16[128,2048]{1,0:T(8,128)(2,1)}, bf16[128,2048]{1,0:T(8,128)(2,1)}, u32[]{:S(2)}, u32[]{:S(2)}) %collective-permute-start.12) | collective-permute-done | bytes 524320 | tf_op jit(solution)/shard_map/ppermute | solution.py:375
  64.0 1.6 fusion.4
  65.7 1.3 collective-permute-start.15
  67.3 1.4 collective-permute-start.14
  68.7 2.3 %collective-permute-start.13 = (bf16[128,128]{1,0:T(8,128)(2,1)S(1)}, bf16[128,128]{1,0:T(8,128)(2,1)S(1)}, u32[]{:S(2)}, u32[]{:S(2)}) collective-permute-start(bf16[128,128]{1,0:T(8,128)(2,1)S(1)} %convolution_convert_fusion.4), channel_id=1, source_target_pairs={{0,8},{4,12},{1,9},{5,13},{2,10},{6,14},{3,11},{7,15},{16,24},{20,... | collective-permute-start | bytes 98312 | tf_op jit(solution)/shard_map/ppermute | solution.py:29
  71.0 1.3 pad_maximum_fusion
  74.5 0.7 add_convert_fusion.4
  75.3 4.0 %collective-permute-start.17 = (bf16[544,128]{1,0:T(8,128)(2,1)S(1)}, bf16[544,128]{1,0:T(8,128)(2,1)S(1)}, u32[]{:S(2)}, u32[]{:S(2)}) collective-permute-start(bf16[544,128]{1,0:T(8,128)(2,1)S(1)} %pad_maximum_fusion.1.refs_0_), channel_id=1, source_target_pairs={{0,2},{1,3},{2,0},{3,1},{4,6},{5,7},{6,4},{7,5},{8,10},{9,11},{10,... | collective-permute-start | bytes 417800 | tf_op jit(solution)/shard_map/ppermute | solution.py:160
  79.5 2.0 %collective-permute-start.19 = (bf16[544,128]{1,0:T(8,128)(2,1)S(1)}, bf16[544,128]{1,0:T(8,128)(2,1)S(1)}, u32[]{:S(2)}, u32[]{:S(2)}) collective-permute-start(bf16[544,128]{1,0:T(8,128)(2,1)S(1)} %pad_maximum_fusion.1.refs_0_), channel_id=1, source_target_pairs={{0,8},{4,12},{8,0},{12,4},{1,9},{5,13},{9,1},{13,5},{2,10},{6,14},... | collective-permute-start | bytes 417800 | tf_op jit(solution)/shard_map/ppermute | solution.py:175
  81.5 2.1 %collective-permute-done.16.refs_1_ = bf16[544,128]{1,0:T(8,128)(2,1)S(1)} collective-permute-done((bf16[544,128]{1,0:T(8,128)(2,1)S(1)}, bf16[544,128]{1,0:T(8,128)(2,1)S(1)}, u32[]{:S(2)}, u32[]{:S(2)}) %collective-permute-start.16) | collective-permute-done | bytes 139296 | tf_op jit(solution)/shard_map/ppermute | solution.py:160
  83.6 2.0 %collective-permute-start.20 = (bf16[544,128]{1,0:T(8,128)(2,1)S(1)}, bf16[544,128]{1,0:T(8,128)(2,1)S(1)}, u32[]{:S(2)}, u32[]{:S(2)}) collective-permute-start(bf16[544,128]{1,0:T(8,128)(2,1)S(1)} %collective-permute-done.16.refs_1_), channel_id=1, source_target_pairs={{0,8},{4,12},{8,0},{12,4},{1,9},{5,13},{9,1},{13,5},{2,10},{6,14},... | collective-permute-start | bytes 417800 | tf_op jit(solution)/shard_map/ppermute | solution.py:175
  85.6 3.5 %collective-permute-done.17.refs_2_ = bf16[544,128]{1,0:T(8,128)(2,1)S(1)} collective-permute-done((bf16[544,128]{1,0:T(8,128)(2,1)S(1)}, bf16[544,128]{1,0:T(8,128)(2,1)S(1)}, u32[]{:S(2)}, u32[]{:S(2)}) %collective-permute-start.17) | collective-permute-done | bytes 139296 | tf_op jit(solution)/shard_map/ppermute | solution.py:160
  89.1 2.0 %collective-permute-start.21 = (bf16[544,128]{1,0:T(8,128)(2,1)S(1)}, bf16[544,128]{1,0:T(8,128)(2,1)S(1)}, u32[]{:S(2)}, u32[]{:S(2)}) collective-permute-start(bf16[544,128]{1,0:T(8,128)(2,1)S(1)} %collective-permute-done.17.refs_2_), channel_id=1, source_target_pairs={{0,8},{4,12},{8,0},{12,4},{1,9},{5,13},{9,1},{13,5},{2,10},{6,14},... | collective-permute-start | bytes 417800 | tf_op jit(solution)/shard_map/ppermute | solution.py:175
  91.2 4.4 %collective-permute-done.21.refs_6_ = bf16[544,128]{1,0:T(8,128)(2,1)S(1)} collective-permute-done((bf16[544,128]{1,0:T(8,128)(2,1)S(1)}, bf16[544,128]{1,0:T(8,128)(2,1)S(1)}, u32[]{:S(2)}, u32[]{:S(2)}) %collective-permute-start.21) | collective-permute-done | bytes 139296 | tf_op jit(solution)/shard_map/ppermute | solution.py:175
  95.6 2.3 %collective-permute-done.22.refs_7_ = bf16[544,128]{1,0:T(8,128)(2,1)S(1)} collective-permute-done((bf16[544,128]{1,0:T(8,128)(2,1)S(1)}, bf16[544,128]{1,0:T(8,128)(2,1)S(1)}, u32[]{:S(2)}, u32[]{:S(2)}) %collective-permute-start.22) | collective-permute-done | bytes 139296 | tf_op jit(solution)/shard_map/ppermute | solution.py:175
  98.0 1.7 %collective-permute-start.25 = (bf16[128,2048]{1,0:T(8,128)(2,1)}, bf16[128,2048]{1,0:T(8,128)(2,1)S(1)}, u32[]{:S(2)}, u32[]{:S(2)}) collective-permute-start(bf16[128,2048]{1,0:T(8,128)(2,1)} %collective-permute-done.9.refs_8_), channel_id=1, source_target_pairs={{0,8},{4,12},{8,0},{12,4},{1,9},{5,13},{9,1},{13,5},{2,10},{6,14},... | collective-permute-start | bytes 1572872 | tf_op jit(solution)/shard_map/ppermute | solution.py:175
  99.8 0.9 copy-done.2
  100.7 11.8 %chunk.7 = (bf16[128,2048]{1,0:T(8,128)(2,1)}, bf16[128,2048]{1,0:T(8,128)(2,1)}) custom-call(s32[10]{0:T(128)} %stack.52.place_ref, bf16[544,128]{1,0:T(8,128)(2,1)} %copy-done.3, bf16[544,128]{1,0:T(8,128)(2,1)} %copy-done.4, bf16[544,128]{1,0:T(8,128)(2,1)} %copy-done.5, bf16[544,128]{1,0:T(8,128)(2,1)} %copy-done.6, bf16[544,128]{1,0:T(8,128)(2,1)} %copy-done.7, ...), custom_call_target="tpu_custom_call" | custom-call | flops 5368709120 | bytes 18874368 | tf_op jit(solution)/shard_map/chunk/pallas_call | solution.py:296
  112.8 11.8 %chunk.6 = (bf16[128,2048]{1,0:T(8,128)(2,1)}, bf16[128,2048]{1,0:T(8,128)(2,1)}) custom-call(s32[10]{0:T(128)} %stack.52.place_ref, bf16[544,128]{1,0:T(8,128)(2,1)} %copy-done.3, bf16[544,128]{1,0:T(8,128)(2,1)} %copy-done.4, bf16[544,128]{1,0:T(8,128)(2,1)} %copy-done.5, bf16[544,128]{1,0:T(8,128)(2,1)} %copy-done.6, bf16[544,128]{1,0:T(8,128)(2,1)} %copy-done.7, ...), custom_call_target="tpu_custom_call" | custom-call | flops 5368709120 | bytes 18874368 | tf_op jit(solution)/shard_map/chunk/pallas_call | solution.py:296
  124.7 2.0 %collective-permute-start.27 = (bf16[128,2048]{1,0:T(8,128)(2,1)}, bf16[128,2048]{1,0:T(8,128)(2,1)S(1)}, u32[]{:S(2)}, u32[]{:S(2)}) collective-permute-start(bf16[128,2048]{1,0:T(8,128)(2,1)} %get-tuple-element.77), channel_id=1, source_target_pairs={{0,8},{4,12},{8,0},{12,4},{1,9},{5,13},{9,1},{13,5},{2,10},{6,14},... | collective-permute-start | bytes 1572872 | tf_op jit(solution)/shard_map/ppermute | solution.py:175
  127.5 11.8 %chunk.5 = (bf16[128,2048]{1,0:T(8,128)(2,1)}, bf16[128,2048]{1,0:T(8,128)(2,1)}) custom-call(s32[10]{0:T(128)} %stack.52.place_ref, bf16[544,128]{1,0:T(8,128)(2,1)} %copy-done.3, bf16[544,128]{1,0:T(8,128)(2,1)} %copy-done.4, bf16[544,128]{1,0:T(8,128)(2,1)} %copy-done.5, bf16[544,128]{1,0:T(8,128)(2,1)} %copy-done.6, bf16[544,128]{1,0:T(8,128)(2,1)} %copy-done.7, ...), custom_call_target="tpu_custom_call" | custom-call | flops 5368709120 | bytes 18874368 | tf_op jit(solution)/shard_map/chunk/pallas_call | solution.py:296
  139.6 1.2 collective-permute-done.29
  141.4 12.0 %chunk.4 = (bf16[128,2048]{1,0:T(8,128)(2,1)}, bf16[128,2048]{1,0:T(8,128)(2,1)}, bf16[128,2048]{1,0:T(8,128)(2,1)}) custom-call(s32[10]{0:T(128)} %stack.52.place_ref, bf16[544,128]{1,0:T(8,128)(2,1)} %copy-done.3, bf16[544,128]{1,0:T(8,128)(2,1)} %copy-done.4, bf16[544,128]{1,0:T(8,128)(2,1)} %copy-done.5, bf16[544,128]{1,0:T(8,128)(2,1)} %copy-done.6, ...), custom_call_target="tpu_custom_call" | custom-call | flops 5368709120 | bytes 18874368 | tf_op jit(solution)/shard_map/chunk/pallas_call | solution.py:296
  153.5 0.7 collective-permute-start.24
  154.7 3.3 %collective-permute-start.31 = (bf16[128,2048]{1,0:T(8,128)(2,1)S(1)}, bf16[128,2048]{1,0:T(8,128)(2,1)S(1)}, u32[]{:S(2)}, u32[]{:S(2)}) collective-permute-start(bf16[128,2048]{1,0:T(8,128)(2,1)S(1)} %add_convert_fusion.1), channel_id=1, source_target_pairs={{0,1},{1,2},{2,3},{3,0},{4,5},{5,6},{6,7},{7,4},{8,9},{9,10},{10,1... | collective-permute-start | bytes 1572872 | tf_op jit(solution)/shard_map/ppermute | solution.py:430
  158.0 7.0 %collective-permute-done.24 = bf16[128,2048]{1,0:T(8,128)(2,1)S(1)} collective-permute-done((bf16[128,2048]{1,0:T(8,128)(2,1)}, bf16[128,2048]{1,0:T(8,128)(2,1)S(1)}, u32[]{:S(2)}, u32[]{:S(2)}) %collective-permute-start.24) | collective-permute-done | bytes 524320 | tf_op jit(solution)/shard_map/ppermute | solution.py:175
  165.0 2.7 %collective-permute-done.31 = bf16[128,2048]{1,0:T(8,128)(2,1)S(1)} collective-permute-done((bf16[128,2048]{1,0:T(8,128)(2,1)S(1)}, bf16[128,2048]{1,0:T(8,128)(2,1)S(1)}, u32[]{:S(2)}, u32[]{:S(2)}) %collective-permute-start.31) | collective-permute-done | bytes 524320 | tf_op jit(solution)/shard_map/ppermute | solution.py:430
  167.7 1.1 add_convert_fusion
  (100 shorter events, 8.5 us)
Async XLA Ops:
  0.0 20.5 %copy-start = (bf16[128,2048]{1,0:T(8,128)(2,1)S(1)}, bf16[128,2048]{1,0:T(8,128)(2,1)}, u32[]{:S(2)}) copy-start(bf16[128,2048]{1,0:T(8,128)(2,1)} %param.14) | copy-start | bytes 1572868
  0.0 17.9 %collective-permute-start.2 = (bf16[1,2048,768]{2,1,0:T(8,128)(2,1)}, bf16[1,2048,768]{2,1,0:T(8,128)(2,1)}, u32[]{:S(2)}, u32[]{:S(2)}) collective-permute-start(bf16[1,2048,768]{2,1,0:T(8,128)(2,1)} %refs_12_.7), channel_id=1, source_target_pairs={{0,4},{4,0},{8,12},{12,8},{1,5},{5,1},{9,13},{13,9},{2,6},{6,2},{1... | collective-permute-start | bytes 9437192 | tf_op jit(solution)/shard_map/ppermute | solution.py:179
  0.5 17.4 %collective-permute-start = (bf16[128,2048]{1,0:T(8,128)(2,1)}, bf16[128,2048]{1,0:T(8,128)(2,1)S(1)}, u32[]{:S(2)}, u32[]{:S(2)}) collective-permute-start(bf16[128,2048]{1,0:T(8,128)(2,1)} %refs_8_.1), channel_id=1, source_target_pairs={{0,1},{1,2},{2,3},{3,0},{4,5},{5,6},{6,7},{7,4},{8,9},{9,10},{10,1... | collective-permute-start | bytes 1572872 | tf_op jit(solution)/shard_map/ppermute | solution.py:155
  3.1 14.8 %collective-permute-start.1 = (bf16[128,2048]{1,0:T(8,128)(2,1)}, bf16[128,2048]{1,0:T(8,128)(2,1)}, u32[]{:S(2)}, u32[]{:S(2)}) collective-permute-start(bf16[128,2048]{1,0:T(8,128)(2,1)} %refs_8_.1), channel_id=1, source_target_pairs={{0,8},{4,12},{8,0},{12,4},{1,9},{5,13},{9,1},{13,5},{2,10},{6,14},... | collective-permute-start | bytes 1572872 | tf_op jit(solution)/shard_map/ppermute | solution.py:175
  7.0 38.3 %copy-start.21 = (f32[128,8]{0,1:T(8,128)S(1)}, f32[128,8]{0,1:T(8,128)}, u32[]{:S(2)}) copy-start(f32[128,8]{0,1:T(8,128)} %param.19) | copy-start | bytes 12292
  7.0 38.3 %copy-start.22 = (s32[128,8]{0,1:T(8,128)S(1)}, s32[128,8]{0,1:T(8,128)}, u32[]{:S(2)}) copy-start(s32[128,8]{0,1:T(8,128)} %param.18) | copy-start | bytes 12292
  17.9 34.9 %copy-start.12 = (bf16[128,2048]{1,0:T(8,128)(2,1)}, bf16[128,2048]{1,0:T(8,128)(2,1)S(1)}, u32[]{:S(2)}) copy-start(bf16[128,2048]{1,0:T(8,128)(2,1)S(1)} %collective-permute-done.refs_8_) | copy-start | bytes 1572868
  17.9 6.5 %collective-permute-start.5 = (bf16[1,2048,768]{2,1,0:T(8,128)(2,1)}, bf16[1,2048,768]{2,1,0:T(8,128)(2,1)}, u32[]{:S(2)}, u32[]{:S(2)}) collective-permute-start(bf16[1,2048,768]{2,1,0:T(8,128)(2,1)} %refs_13_.7), channel_id=1, source_target_pairs={{0,4},{4,0},{8,12},{12,8},{1,5},{5,1},{9,13},{13,9},{2,6},{6,2},{1... | collective-permute-start | bytes 9437192 | tf_op jit(solution)/shard_map/ppermute | solution.py:179
  18.0 21.7 %collective-permute-start.3 = (bf16[128,2048]{1,0:T(8,128)(2,1)S(1)}, bf16[128,2048]{1,0:T(8,128)(2,1)S(1)}, u32[]{:S(2)}, u32[]{:S(2)}) collective-permute-start(bf16[128,2048]{1,0:T(8,128)(2,1)S(1)} %collective-permute-done.refs_8_), channel_id=1, source_target_pairs={{0,1},{1,2},{2,3},{3,0},{4,5},{5,6},{6,7},{7,4},{8,9},{9,10},{10,1... | collective-permute-start | bytes 1572872 | tf_op jit(solution)/shard_map/ppermute | solution.py:155
  19.0 20.7 %collective-permute-start.4 = (bf16[128,2048]{1,0:T(8,128)(2,1)S(1)}, bf16[128,2048]{1,0:T(8,128)(2,1)}, u32[]{:S(2)}, u32[]{:S(2)}) collective-permute-start(bf16[128,2048]{1,0:T(8,128)(2,1)S(1)} %collective-permute-done.refs_8_), channel_id=1, source_target_pairs={{0,8},{4,12},{8,0},{12,4},{1,9},{5,13},{9,1},{13,5},{2,10},{6,14},... | collective-permute-start | bytes 1572872 | tf_op jit(solution)/shard_map/ppermute | solution.py:175
  20.5 16.9 %collective-permute-start.6 = (bf16[32,2048]{1,0:T(8,128)(2,1)S(1)}, bf16[32,2048]{1,0:T(8,128)(2,1)S(1)}, u32[]{:S(2)}, u32[]{:S(2)}) collective-permute-start(bf16[32,2048]{1,0:T(8,128)(2,1)S(1)} %constant_dynamic-slice_fusion), channel_id=1, source_target_pairs={{0,1},{1,2},{2,3},{3,0},{4,5},{5,6},{6,7},{7,4},{8,9},{9,10},{10,1... | collective-permute-start | bytes 393224 | tf_op jit(solution)/shard_map/ppermute | solution.py:367
  22.2 17.5 %collective-permute-start.8 = (bf16[32,2048]{1,0:T(8,128)(2,1)S(1)}, bf16[32,2048]{1,0:T(8,128)(2,1)S(1)}, u32[]{:S(2)}, u32[]{:S(2)}) collective-permute-start(bf16[32,2048]{1,0:T(8,128)(2,1)S(1)} %constant_dynamic-slice_fusion), channel_id=1, source_target_pairs={{0,3},{1,0},{2,1},{3,2},{4,7},{5,4},{6,5},{7,6},{8,11},{9,8},{10,9... | collective-permute-start | bytes 393224 | tf_op jit(solution)/shard_map/ppermute | solution.py:367
  24.4 20.9 %collective-permute-start.7 = (bf16[32,2048]{1,0:T(8,128)(2,1)S(1)}, bf16[32,2048]{1,0:T(8,128)(2,1)S(1)}, u32[]{:S(2)}, u32[]{:S(2)}) collective-permute-start(bf16[32,2048]{1,0:T(8,128)(2,1)S(1)} %constant_dynamic-slice_fusion), channel_id=1, source_target_pairs={{0,2},{1,3},{2,0},{3,1},{4,6},{5,7},{6,4},{7,5},{8,10},{9,11},{10,... | collective-permute-start | bytes 393224 | tf_op jit(solution)/shard_map/ppermute | solution.py:367
  39.7 25.9 %copy-start.13 = (bf16[128,2048]{1,0:T(8,128)(2,1)}, bf16[128,2048]{1,0:T(8,128)(2,1)S(1)}, u32[]{:S(2)}) copy-start(bf16[128,2048]{1,0:T(8,128)(2,1)S(1)} %collective-permute-done.3.refs_8_) | copy-start | bytes 1572868
  45.3 18.7 %collective-permute-start.11 = (bf16[1,768,2048]{2,1,0:T(8,128)(2,1)}, bf16[1,768,2048]{2,1,0:T(8,128)(2,1)}, u32[]{:S(2)}, u32[]{:S(2)}) collective-permute-start(bf16[1,768,2048]{2,1,0:T(8,128)(2,1)} %refs_14_.7), channel_id=1, source_target_pairs={{0,4},{4,0},{8,12},{12,8},{1,5},{5,1},{9,13},{13,9},{2,6},{6,2},{1... | collective-permute-start | bytes 9437192 | tf_op jit(solution)/shard_map/ppermute | solution.py:179
  45.4 16.3 %collective-permute-start.9 = (bf16[128,2048]{1,0:T(8,128)(2,1)S(1)}, bf16[128,2048]{1,0:T(8,128)(2,1)}, u32[]{:S(2)}, u32[]{:S(2)}) collective-permute-start(bf16[128,2048]{1,0:T(8,128)(2,1)S(1)} %collective-permute-done.3.refs_8_), channel_id=1, source_target_pairs={{0,1},{1,2},{2,3},{3,0},{4,5},{5,6},{6,7},{7,4},{8,9},{9,10},{10,1... | collective-permute-start | bytes 1572872 | tf_op jit(solution)/shard_map/ppermute | solution.py:155
  45.4 16.2 %collective-permute-start.10 = (bf16[128,2048]{1,0:T(8,128)(2,1)S(1)}, bf16[128,2048]{1,0:T(8,128)(2,1)}, u32[]{:S(2)}, u32[]{:S(2)}) collective-permute-start(bf16[128,2048]{1,0:T(8,128)(2,1)S(1)} %collective-permute-done.3.refs_8_), channel_id=1, source_target_pairs={{0,8},{4,12},{8,0},{12,4},{1,9},{5,13},{9,1},{13,5},{2,10},{6,14},... | collective-permute-start | bytes 1572872 | tf_op jit(solution)/shard_map/ppermute | solution.py:175
  49.6 14.4 %collective-permute-start.12 = (bf16[128,2048]{1,0:T(8,128)(2,1)}, bf16[128,2048]{1,0:T(8,128)(2,1)}, u32[]{:S(2)}, u32[]{:S(2)}) collective-permute-start(bf16[128,2048]{1,0:T(8,128)(2,1)} %constant_dynamic-update-slice_fusion), channel_id=1, source_target_pairs={{0,16},{16,0},{1,17},{17,1},{2,18},{18,2},{3,19},{19,3},{4,20},{20... | collective-permute-start | bytes 1572872 | tf_op jit(solution)/shard_map/ppermute | solution.py:375
  65.7 6.6 %collective-permute-start.15 = (bf16[512,256]{1,0:T(8,128)(2,1)S(1)}, bf16[512,256]{1,0:T(8,128)(2,1)S(1)}, u32[]{:S(2)}, u32[]{:S(2)}) collective-permute-start(bf16[512,256]{1,0:T(8,128)(2,1)S(1)} %slice.47), channel_id=1, source_target_pairs={{0,4},{4,8},{8,12},{1,5},{5,9},{9,13},{2,6},{6,10},{10,14},{3,7},{... | collective-permute-start | bytes 786440 | tf_op jit(solution)/shard_map/ppermute | solution.py:29
  67.3 6.8 %collective-permute-start.14 = (bf16[128,128]{1,0:T(8,128)(2,1)S(1)}, bf16[128,128]{1,0:T(8,128)(2,1)S(1)}, u32[]{:S(2)}, u32[]{:S(2)}) collective-permute-start(bf16[128,128]{1,0:T(8,128)(2,1)S(1)} %convolution_convert_fusion.4), channel_id=1, source_target_pairs={{0,12},{1,13},{2,14},{3,15},{16,28},{17,29},{18,30},{19,31}} | collective-permute-start | bytes 98312 | tf_op jit(solution)/shard_map/ppermute | solution.py:29
  68.7 5.4 %collective-permute-start.13 = (bf16[128,128]{1,0:T(8,128)(2,1)S(1)}, bf16[128,128]{1,0:T(8,128)(2,1)S(1)}, u32[]{:S(2)}, u32[]{:S(2)}) collective-permute-start(bf16[128,128]{1,0:T(8,128)(2,1)S(1)} %convolution_convert_fusion.4), channel_id=1, source_target_pairs={{0,8},{4,12},{1,9},{5,13},{2,10},{6,14},{3,11},{7,15},{16,24},{20,... | collective-permute-start | bytes 98312 | tf_op jit(solution)/shard_map/ppermute | solution.py:29
  73.8 25.9 %collective-permute-start.23 = (bf16[2,128,2048]{2,1,0:T(8,128)(2,1)S(1)}, bf16[2,128,2048]{2,1,0:T(8,128)(2,1)S(1)}, u32[]{:S(2)}, u32[]{:S(2)}) collective-permute-start(bf16[2,128,2048]{2,1,0:T(8,128)(2,1)S(1)} %pad_maximum_fusion), channel_id=1, source_target_pairs={{0,4},{4,0},{8,12},{12,8},{1,5},{5,1},{9,13},{13,9},{2,6},{6,2},{1... | collective-permute-start | bytes 3145736 | tf_op jit(solution)/shard_map/ppermute | solution.py:179
  75.2 24.5 %copy-start.3 = (bf16[544,128]{1,0:T(8,128)(2,1)}, bf16[544,128]{1,0:T(8,128)(2,1)S(1)}, u32[]{:S(2)}) copy-start(bf16[544,128]{1,0:T(8,128)(2,1)S(1)} %pad_maximum_fusion.1.refs_0_) | copy-start | bytes 417796
  75.2 8.4 %collective-permute-start.16 = (bf16[544,128]{1,0:T(8,128)(2,1)S(1)}, bf16[544,128]{1,0:T(8,128)(2,1)S(1)}, u32[]{:S(2)}, u32[]{:S(2)}) collective-permute-start(bf16[544,128]{1,0:T(8,128)(2,1)S(1)} %pad_maximum_fusion.1.refs_0_), channel_id=1, source_target_pairs={{0,1},{1,2},{2,3},{3,0},{4,5},{5,6},{6,7},{7,4},{8,9},{9,10},{10,1... | collective-permute-start | bytes 417800 | tf_op jit(solution)/shard_map/ppermute | solution.py:160
  75.3 13.9 %collective-permute-start.17 = (bf16[544,128]{1,0:T(8,128)(2,1)S(1)}, bf16[544,128]{1,0:T(8,128)(2,1)S(1)}, u32[]{:S(2)}, u32[]{:S(2)}) collective-permute-start(bf16[544,128]{1,0:T(8,128)(2,1)S(1)} %pad_maximum_fusion.1.refs_0_), channel_id=1, source_target_pairs={{0,2},{1,3},{2,0},{3,1},{4,6},{5,7},{6,4},{7,5},{8,10},{9,11},{10,... | collective-permute-start | bytes 417800 | tf_op jit(solution)/shard_map/ppermute | solution.py:160
  79.3 11.8 %collective-permute-start.18 = (bf16[544,128]{1,0:T(8,128)(2,1)S(1)}, bf16[544,128]{1,0:T(8,128)(2,1)S(1)}, u32[]{:S(2)}, u32[]{:S(2)}) collective-permute-start(bf16[544,128]{1,0:T(8,128)(2,1)S(1)} %pad_maximum_fusion.1.refs_0_), channel_id=1, source_target_pairs={{0,3},{1,0},{2,1},{3,2},{4,7},{5,4},{6,5},{7,6},{8,11},{9,8},{10,9... | collective-permute-start | bytes 417800 | tf_op jit(solution)/shard_map/ppermute | solution.py:160
  79.5 11.6 %collective-permute-start.19 = (bf16[544,128]{1,0:T(8,128)(2,1)S(1)}, bf16[544,128]{1,0:T(8,128)(2,1)S(1)}, u32[]{:S(2)}, u32[]{:S(2)}) collective-permute-start(bf16[544,128]{1,0:T(8,128)(2,1)S(1)} %pad_maximum_fusion.1.refs_0_), channel_id=1, source_target_pairs={{0,8},{4,12},{8,0},{12,4},{1,9},{5,13},{9,1},{13,5},{2,10},{6,14},... | collective-permute-start | bytes 417800 | tf_op jit(solution)/shard_map/ppermute | solution.py:175
  83.6 16.1 %copy-start.4 = (bf16[544,128]{1,0:T(8,128)(2,1)}, bf16[544,128]{1,0:T(8,128)(2,1)S(1)}, u32[]{:S(2)}) copy-start(bf16[544,128]{1,0:T(8,128)(2,1)S(1)} %collective-permute-done.16.refs_1_) | copy-start | bytes 417796
  83.6 7.6 %collective-permute-start.20 = (bf16[544,128]{1,0:T(8,128)(2,1)S(1)}, bf16[544,128]{1,0:T(8,128)(2,1)S(1)}, u32[]{:S(2)}, u32[]{:S(2)}) collective-permute-start(bf16[544,128]{1,0:T(8,128)(2,1)S(1)} %collective-permute-done.16.refs_1_), channel_id=1, source_target_pairs={{0,8},{4,12},{8,0},{12,4},{1,9},{5,13},{9,1},{13,5},{2,10},{6,14},... | collective-permute-start | bytes 417800 | tf_op jit(solution)/shard_map/ppermute | solution.py:175
  89.1 10.6 %copy-start.5 = (bf16[544,128]{1,0:T(8,128)(2,1)}, bf16[544,128]{1,0:T(8,128)(2,1)S(1)}, u32[]{:S(2)}) copy-start(bf16[544,128]{1,0:T(8,128)(2,1)S(1)} %collective-permute-done.17.refs_2_) | copy-start | bytes 417796
  89.1 6.5 %collective-permute-start.21 = (bf16[544,128]{1,0:T(8,128)(2,1)S(1)}, bf16[544,128]{1,0:T(8,128)(2,1)S(1)}, u32[]{:S(2)}, u32[]{:S(2)}) collective-permute-start(bf16[544,128]{1,0:T(8,128)(2,1)S(1)} %collective-permute-done.17.refs_2_), channel_id=1, source_target_pairs={{0,8},{4,12},{8,0},{12,4},{1,9},{5,13},{9,1},{13,5},{2,10},{6,14},... | collective-permute-start | bytes 417800 | tf_op jit(solution)/shard_map/ppermute | solution.py:175
  91.1 8.6 %copy-start.6 = (bf16[544,128]{1,0:T(8,128)(2,1)}, bf16[544,128]{1,0:T(8,128)(2,1)S(1)}, u32[]{:S(2)}) copy-start(bf16[544,128]{1,0:T(8,128)(2,1)S(1)} %collective-permute-done.18.refs_3_) | copy-start | bytes 417796
  91.1 6.8 %collective-permute-start.22 = (bf16[544,128]{1,0:T(8,128)(2,1)S(1)}, bf16[544,128]{1,0:T(8,128)(2,1)S(1)}, u32[]{:S(2)}, u32[]{:S(2)}) collective-permute-start(bf16[544,128]{1,0:T(8,128)(2,1)S(1)} %collective-permute-done.18.refs_3_), channel_id=1, source_target_pairs={{0,8},{4,12},{8,0},{12,4},{1,9},{5,13},{9,1},{13,5},{2,10},{6,14},... | collective-permute-start | bytes 417800 | tf_op jit(solution)/shard_map/ppermute | solution.py:175
  91.2 8.5 %copy-start.8 = (bf16[544,128]{1,0:T(8,128)(2,1)}, bf16[544,128]{1,0:T(8,128)(2,1)S(1)}, u32[]{:S(2)}) copy-start(bf16[544,128]{1,0:T(8,128)(2,1)S(1)} %collective-permute-done.20.refs_5_) | copy-start | bytes 417796
  98.0 14.9 %collective-permute-start.25 = (bf16[128,2048]{1,0:T(8,128)(2,1)}, bf16[128,2048]{1,0:T(8,128)(2,1)S(1)}, u32[]{:S(2)}, u32[]{:S(2)}) collective-permute-start(bf16[128,2048]{1,0:T(8,128)(2,1)} %collective-permute-done.9.refs_8_), channel_id=1, source_target_pairs={{0,8},{4,12},{8,0},{12,4},{1,9},{5,13},{9,1},{13,5},{2,10},{6,14},... | collective-permute-start | bytes 1572872 | tf_op jit(solution)/shard_map/ppermute | solution.py:175
  112.5 14.2 %copy-start.17 = (bf16[128,2048]{1,0:T(8,128)(2,1)S(1)}, bf16[128,2048]{1,0:T(8,128)(2,1)}, u32[]{:S(2)}) copy-start(bf16[128,2048]{1,0:T(8,128)(2,1)} %get-tuple-element.79) | copy-start | bytes 1572868
  112.5 14.2 %collective-permute-start.28 = (bf16[128,2048]{1,0:T(8,128)(2,1)}, bf16[128,2048]{1,0:T(8,128)(2,1)S(1)}, u32[]{:S(2)}, u32[]{:S(2)}) collective-permute-start(bf16[128,2048]{1,0:T(8,128)(2,1)} %get-tuple-element.80), channel_id=1, source_target_pairs={{0,8},{4,12},{8,0},{12,4},{1,9},{5,13},{9,1},{13,5},{2,10},{6,14},... | collective-permute-start | bytes 1572872 | tf_op jit(solution)/shard_map/ppermute | solution.py:175
  112.8 11.8 %copy-start.16 = (bf16[128,2048]{1,0:T(8,128)(2,1)}, bf16[128,2048]{1,0:T(8,128)(2,1)S(1)}, u32[]{:S(2)}) copy-start(bf16[128,2048]{1,0:T(8,128)(2,1)S(1)} %collective-permute-done.25.refs_9_) | copy-start | bytes 1572868
  124.7 15.0 %collective-permute-start.27 = (bf16[128,2048]{1,0:T(8,128)(2,1)}, bf16[128,2048]{1,0:T(8,128)(2,1)S(1)}, u32[]{:S(2)}, u32[]{:S(2)}) collective-permute-start(bf16[128,2048]{1,0:T(8,128)(2,1)} %get-tuple-element.77), channel_id=1, source_target_pairs={{0,8},{4,12},{8,0},{12,4},{1,9},{5,13},{9,1},{13,5},{2,10},{6,14},... | collective-permute-start | bytes 1572872 | tf_op jit(solution)/shard_map/ppermute | solution.py:175
  126.8 14.0 %copy-start.19 = (bf16[128,2048]{1,0:T(8,128)(2,1)S(1)}, bf16[128,2048]{1,0:T(8,128)(2,1)}, u32[]{:S(2)}) copy-start(bf16[128,2048]{1,0:T(8,128)(2,1)} %get-tuple-element.76) | copy-start | bytes 1572868
  126.8 14.0 %collective-permute-start.29 = (bf16[128,2048]{1,0:T(8,128)(2,1)S(1)}, bf16[128,2048]{1,0:T(8,128)(2,1)S(1)}, u32[]{:S(2)}, u32[]{:S(2)}) collective-permute-start(bf16[128,2048]{1,0:T(8,128)(2,1)S(1)} %add_convert_fusion.3), channel_id=1, source_target_pairs={{0,1},{1,2},{2,3},{3,0},{4,5},{5,6},{6,7},{7,4},{8,9},{9,10},{10,1... | collective-permute-start | bytes 1572872 | tf_op jit(solution)/shard_map/ppermute | solution.py:430
  139.3 14.9 %collective-permute-start.26 = (bf16[128,2048]{1,0:T(8,128)(2,1)}, bf16[128,2048]{1,0:T(8,128)(2,1)S(1)}, u32[]{:S(2)}, u32[]{:S(2)}) collective-permute-start(bf16[128,2048]{1,0:T(8,128)(2,1)} %get-tuple-element.73), channel_id=1, source_target_pairs={{0,8},{4,12},{8,0},{12,4},{1,9},{5,13},{9,1},{13,5},{2,10},{6,14},... | collective-permute-start | bytes 1572872 | tf_op jit(solution)/shard_map/ppermute | solution.py:175
  141.1 13.4 %copy-start.18 = (bf16[128,2048]{1,0:T(8,128)(2,1)S(1)}, bf16[128,2048]{1,0:T(8,128)(2,1)}, u32[]{:S(2)}) copy-start(bf16[128,2048]{1,0:T(8,128)(2,1)} %get-tuple-element.72) | copy-start | bytes 1572868
  141.1 13.4 %collective-permute-start.30 = (bf16[128,2048]{1,0:T(8,128)(2,1)S(1)}, bf16[128,2048]{1,0:T(8,128)(2,1)S(1)}, u32[]{:S(2)}, u32[]{:S(2)}) collective-permute-start(bf16[128,2048]{1,0:T(8,128)(2,1)S(1)} %add_convert_fusion.2), channel_id=1, source_target_pairs={{0,1},{1,2},{2,3},{3,0},{4,5},{5,6},{6,7},{7,4},{8,9},{9,10},{10,1... | collective-permute-start | bytes 1572872 | tf_op jit(solution)/shard_map/ppermute | solution.py:430
  153.5 14.2 %copy-start.14 = (bf16[128,2048]{1,0:T(8,128)(2,1)S(1)}, bf16[128,2048]{1,0:T(8,128)(2,1)}, u32[]{:S(2)}) copy-start(bf16[128,2048]{1,0:T(8,128)(2,1)} %get-tuple-element.69) | copy-start | bytes 1572868
  153.5 14.2 %copy-start.15 = (bf16[128,2048]{1,0:T(8,128)(2,1)S(1)}, bf16[128,2048]{1,0:T(8,128)(2,1)}, u32[]{:S(2)}) copy-start(bf16[128,2048]{1,0:T(8,128)(2,1)} %get-tuple-element.68) | copy-start | bytes 1572868
  153.5 11.5 %collective-permute-start.24 = (bf16[128,2048]{1,0:T(8,128)(2,1)}, bf16[128,2048]{1,0:T(8,128)(2,1)S(1)}, u32[]{:S(2)}, u32[]{:S(2)}) collective-permute-start(bf16[128,2048]{1,0:T(8,128)(2,1)} %get-tuple-element.70), channel_id=1, source_target_pairs={{0,8},{4,12},{8,0},{12,4},{1,9},{5,13},{9,1},{13,5},{2,10},{6,14},... | collective-permute-start | bytes 1572872 | tf_op jit(solution)/shard_map/ppermute | solution.py:175
  154.7 12.9 %collective-permute-start.31 = (bf16[128,2048]{1,0:T(8,128)(2,1)S(1)}, bf16[128,2048]{1,0:T(8,128)(2,1)S(1)}, u32[]{:S(2)}, u32[]{:S(2)}) collective-permute-start(bf16[128,2048]{1,0:T(8,128)(2,1)S(1)} %add_convert_fusion.1), channel_id=1, source_target_pairs={{0,1},{1,2},{2,3},{3,0},{4,5},{5,6},{6,7},{7,4},{8,9},{9,10},{10,1... | collective-permute-start | bytes 1572872 | tf_op jit(solution)/shard_map/ppermute | solution.py:430
  (7 other events, 25.1 us)

commit v4 on v3

--- a/solution.py
+++ b/solution.py
@@ -310,7 +310,7 @@
             pltpu.SemaphoreType.DMA((2 * (head_count + 2 + group_count),)),
             pltpu.SemaphoreType.DMA((3 * experts,)),
         ],
-        compiler_params=pltpu.CompilerParams(vmem_limit_bytes=60 * 2**20),
+        compiler_params=pltpu.CompilerParams(vmem_limit_bytes=61 * 2**20),
         cost_estimate=pl.CostEstimate(
             flops=flops, bytes_accessed=sum(2 * math.prod(w.shape) for w in weights), transcendentals=0
         ),
@@ -365,7 +365,7 @@
         for distance in ((1, head_count - 1), range(2, head_count - 1), ())[s]:
             piece = after(pieces[0], blocks[s], swapped[s])
             pieces[distance] = lax.ppermute(piece, "heads", ring_pairs(head_count, distance))
-        extra = (pieces, halves)[s - 1] if s else []
+        extra = pieces if s == 1 else []
         blocks[-1], across[-1], swapped[-1], projected, where, *extra = lax.optimization_barrier(
             (blocks[-1], across[-1], swapped[-1], projected, where, *extra)
         )
@@ -373,7 +373,7 @@
             halves = [jnp.concatenate(extra, axis=0)]
             if group_count == 2:
                 halves.append(lax.ppermute(halves[0], "groups", [(0, 1), (1, 0)]))
-    half = jnp.stack(extra, axis=0)
+    half = jnp.stack(halves, axis=0)
     projected = project(projected, head_count - 1)
     experts = experts + swapped
 

time: 169 us -> 171 us (1.012)
  starting transfers between devices: 40.7 us -> 44.8 us
  waiting for transfers between devices: 63.8 us -> 61.5 us
  local copies, waits for them, and re-layouts: 6.99 us -> 4.8 us
    ppermute x1, waiting for transfers between devices: 2.34 us -> 9.68 us  [on_device_dense(): halves.append(lax.ppermute(halves[0], 'groups', [(0, 1), (1, 0)]))]
    ppermute x3, waiting for transfers between devices: 19.1 us -> 13.1 us  [next_place(): return lax.ppermute(block, 'heads', ring_pairs(count, 1))]
    ppermute x12, starting transfers between devices: 15.8 us -> 18 us  [flip_row(): return lax.ppermute(block, 'ctx', partner_pairs(ctx_count, 2))]
    unnamed x50 -> x52, local copies, waits for them, and re-layouts: 4.67 us -> 3.01 us
  transfers between devices with their start and end apart: 32 -> 32, of which waited for: 14 -> 13; matrix products, arithmetic and copies ran while one was open for 7% -> 7% of each run, Pallas kernels for 28% -> 28%
where the time goes in v4:
time: 171 us
  waiting for transfers between devices  61.5 us (36%)
  Pallas kernels  47.4 us (28%)
  starting transfers between devices  44.8 us (26%)
  matrix products  6.99 us (4%)
  local copies, waits for them, and re-layouts  4.8 us (3%)
  other arithmetic  4.72 us (3%)
    pallas_call x4, Pallas kernels, run_chunk(): pl.pallas_call(functools.partial(chunk_kernel, head_count, turn), out_sha...  47.4 us
    ppermute x3, waiting for transfers between devices, on_device_dense(): lax.ppermute(piece, 'heads', ring_pairs(head_count, distance))  18.1 us
    ppermute x12, starting transfers between devices, flip_row(): return lax.ppermute(block, 'ctx', partner_pairs(ctx_count, 2))  18 us
    ppermute x3, waiting for transfers between devices, next_place(): return lax.ppermute(block, 'heads', ring_pairs(count, 1))  13.1 us
    ppermute x12, waiting for transfers between devices, flip_row(): return lax.ppermute(block, 'ctx', partner_pairs(ctx_count, 2))  12.1 us
    ppermute x1, waiting for transfers between devices, on_device_dense(): halves.append(lax.ppermute(halves[0], 'groups', [(0, 1), (1, 0)]))  9.68 us
    ppermute x3, starting transfers between devices, from_behind(): return lax.ppermute(block, axis, route)  6.01 us
    ppermute x3, starting transfers between devices, on_device_dense(): lax.ppermute(piece, 'heads', ring_pairs(head_count, distance))  5.42 us
  transfers between devices with their start and end apart: 32, of which 13 were waited for; matrix products, arithmetic and copies ran while one was open for 7% of the time, Pallas kernels for 28%

profile of v4, /device:TPU:0, one launch (start us, length us, event | category | flops | bytes accessed | tf_op | source)
XLA Modules:
  0.0 170.8 jit_solution(352376366217083565)
XLA Ops:
  0.5 2.6 %collective-permute-start = (bf16[128,2048]{1,0:T(8,128)(2,1)}, bf16[128,2048]{1,0:T(8,128)(2,1)}, u32[]{:S(2)}, u32[]{:S(2)}) collective-permute-start(bf16[128,2048]{1,0:T(8,128)(2,1)} %refs_8_.1), channel_id=1, source_target_pairs={{0,1},{1,2},{2,3},{3,0},{4,5},{5,6},{6,7},{7,4},{8,9},{9,10},{10,1... | collective-permute-start | bytes 1572872 | tf_op jit(solution)/shard_map/ppermute | solution.py:155
  3.1 1.5 collective-permute-start.1
  4.6 1.7 %copy.16 = bf16[2048,3,128]{0,2,1:T(8,128)(2,1)S(1)} copy(bf16[2048,3,128]{2,0,1:T(8,128)(2,1)} %param.13) | data formatting | bytes 3145728 | tf_op args[3]
  6.4 0.7 stack.52.place_ref
  7.8 10.2 %collective-permute-done.refs_8_ = bf16[128,2048]{1,0:T(8,128)(2,1)} collective-permute-done((bf16[128,2048]{1,0:T(8,128)(2,1)}, bf16[128,2048]{1,0:T(8,128)(2,1)}, u32[]{:S(2)}, u32[]{:S(2)}) %collective-permute-start) | collective-permute-done | bytes 524320 | tf_op jit(solution)/shard_map/ppermute | solution.py:155
  18.1 0.9 collective-permute-start.3
  18.9 1.5 collective-permute-start.4
  20.5 1.6 collective-permute-start.6
  22.1 2.2 %collective-permute-start.8 = (bf16[32,2048]{1,0:T(8,128)(2,1)S(1)}, bf16[32,2048]{1,0:T(8,128)(2,1)S(1)}, u32[]{:S(2)}, u32[]{:S(2)}) collective-permute-start(bf16[32,2048]{1,0:T(8,128)(2,1)S(1)} %constant_dynamic-slice_fusion), channel_id=1, source_target_pairs={{0,3},{1,0},{2,1},{3,2},{4,7},{5,4},{6,5},{7,6},{8,11},{9,8},{10,9... | collective-permute-start | bytes 393224 | tf_op jit(solution)/shard_map/ppermute | solution.py:367
  24.4 1.5 collective-permute-start.7
  25.9 1.6 fusion.6
  27.5 10.2 %collective-permute-done.6 = bf16[32,2048]{1,0:T(8,128)(2,1)S(1)} collective-permute-done((bf16[32,2048]{1,0:T(8,128)(2,1)S(1)}, bf16[32,2048]{1,0:T(8,128)(2,1)S(1)}, u32[]{:S(2)}, u32[]{:S(2)}) %collective-permute-start.6) | collective-permute-done | bytes 131104 | tf_op jit(solution)/shard_map/ppermute | solution.py:367
  37.7 2.3 %collective-permute-done.8 = bf16[32,2048]{1,0:T(8,128)(2,1)S(1)} collective-permute-done((bf16[32,2048]{1,0:T(8,128)(2,1)S(1)}, bf16[32,2048]{1,0:T(8,128)(2,1)S(1)}, u32[]{:S(2)}, u32[]{:S(2)}) %collective-permute-start.8) | collective-permute-done | bytes 131104 | tf_op jit(solution)/shard_map/ppermute | solution.py:367
  40.0 5.6 %collective-permute-done.7 = bf16[32,2048]{1,0:T(8,128)(2,1)S(1)} collective-permute-done((bf16[32,2048]{1,0:T(8,128)(2,1)S(1)}, bf16[32,2048]{1,0:T(8,128)(2,1)S(1)}, u32[]{:S(2)}, u32[]{:S(2)}) %collective-permute-start.7) | collective-permute-done | bytes 131104 | tf_op jit(solution)/shard_map/ppermute | solution.py:367
  45.8 1.6 collective-permute-start.22
  47.3 1.0 slice_bitcast_fusion.1
  48.4 1.6 collective-permute-start.10
  50.6 9.7 %collective-permute-done.22 = bf16[128,2048]{1,0:T(8,128)(2,1)} collective-permute-done((bf16[128,2048]{1,0:T(8,128)(2,1)S(1)}, bf16[128,2048]{1,0:T(8,128)(2,1)}, u32[]{:S(2)}, u32[]{:S(2)}) %collective-permute-start.22) | collective-permute-done | bytes 524320 | tf_op jit(solution)/shard_map/ppermute | solution.py:375
  60.3 1.1 pad_maximum_fusion
  61.4 2.9 %collective-permute-done.9.refs_8_ = bf16[128,2048]{1,0:T(8,128)(2,1)} collective-permute-done((bf16[128,2048]{1,0:T(8,128)(2,1)S(1)}, bf16[128,2048]{1,0:T(8,128)(2,1)}, u32[]{:S(2)}, u32[]{:S(2)}) %collective-permute-start.9) | collective-permute-done | bytes 524320 | tf_op jit(solution)/shard_map/ppermute | solution.py:155
  64.3 1.8 %fusion.4 = bf16[512,384]{1,0:T(8,128)(2,1)S(1)} fusion(bf16[512,384]{1,0:T(8,128)(2,1)S(1)} %fusion.5, s32[]{:T(128)S(6)} %select_n.75, bf16[128,2048]{1,0:T(8,128)(2,1)} %collective-permute-done.9.refs_8_, bf16[2048,384]{0,1:T(8,128)(2,1)S(1)} %bitcast.41), kind=kOutput, calls=%fused_computation.10 | convolution fusion | flops 201375744 | bytes 2195460 | tf_op jit(solution)/shard_map/dot_general | solution.py:344
  66.2 1.3 collective-permute-start.14
  67.8 2.4 %collective-permute-start.13 = (bf16[128,128]{1,0:T(8,128)(2,1)S(1)}, bf16[128,128]{1,0:T(8,128)(2,1)S(1)}, u32[]{:S(2)}, u32[]{:S(2)}) collective-permute-start(bf16[128,128]{1,0:T(8,128)(2,1)S(1)} %convolution_convert_fusion.4), channel_id=1, source_target_pairs={{0,12},{1,13},{2,14},{3,15},{16,28},{17,29},{18,30},{19,31}} | collective-permute-start | bytes 98312 | tf_op jit(solution)/shard_map/ppermute | solution.py:29
  70.2 2.3 %collective-permute-start.12 = (bf16[128,128]{1,0:T(8,128)(2,1)S(1)}, bf16[128,128]{1,0:T(8,128)(2,1)S(1)}, u32[]{:S(2)}, u32[]{:S(2)}) collective-permute-start(bf16[128,128]{1,0:T(8,128)(2,1)S(1)} %convolution_convert_fusion.4), channel_id=1, source_target_pairs={{0,8},{4,12},{1,9},{5,13},{2,10},{6,14},{3,11},{7,15},{16,24},{20,... | collective-permute-start | bytes 98312 | tf_op jit(solution)/shard_map/ppermute | solution.py:29
  74.0 1.0 collective-permute-start.23
  75.6 0.7 add_convert_fusion.4
  76.4 2.2 %collective-permute-start.16 = (bf16[544,128]{1,0:T(8,128)(2,1)S(1)}, bf16[544,128]{1,0:T(8,128)(2,1)S(1)}, u32[]{:S(2)}, u32[]{:S(2)}) collective-permute-start(bf16[544,128]{1,0:T(8,128)(2,1)S(1)} %pad_maximum_fusion.1.refs_0_), channel_id=1, source_target_pairs={{0,2},{1,3},{2,0},{3,1},{4,6},{5,7},{6,4},{7,5},{8,10},{9,11},{10,... | collective-permute-start | bytes 417800 | tf_op jit(solution)/shard_map/ppermute | solution.py:160
  78.5 1.6 collective-permute-start.17
  80.2 2.4 %collective-permute-start.18 = (bf16[544,128]{1,0:T(8,128)(2,1)S(1)}, bf16[544,128]{1,0:T(8,128)(2,1)S(1)}, u32[]{:S(2)}, u32[]{:S(2)}) collective-permute-start(bf16[544,128]{1,0:T(8,128)(2,1)S(1)} %pad_maximum_fusion.1.refs_0_), channel_id=1, source_target_pairs={{0,8},{4,12},{8,0},{12,4},{1,9},{5,13},{9,1},{13,5},{2,10},{6,14},... | collective-permute-start | bytes 417800 | tf_op jit(solution)/shard_map/ppermute | solution.py:175
  82.6 2.3 %collective-permute-done.15.refs_1_ = bf16[544,128]{1,0:T(8,128)(2,1)S(1)} collective-permute-done((bf16[544,128]{1,0:T(8,128)(2,1)S(1)}, bf16[544,128]{1,0:T(8,128)(2,1)S(1)}, u32[]{:S(2)}, u32[]{:S(2)}) %collective-permute-start.15) | collective-permute-done | bytes 139296 | tf_op jit(solution)/shard_map/ppermute | solution.py:160
  84.8 2.3 %collective-permute-start.19 = (bf16[544,128]{1,0:T(8,128)(2,1)S(1)}, bf16[544,128]{1,0:T(8,128)(2,1)S(1)}, u32[]{:S(2)}, u32[]{:S(2)}) collective-permute-start(bf16[544,128]{1,0:T(8,128)(2,1)S(1)} %collective-permute-done.15.refs_1_), channel_id=1, source_target_pairs={{0,8},{4,12},{8,0},{12,4},{1,9},{5,13},{9,1},{13,5},{2,10},{6,14},... | collective-permute-start | bytes 417800 | tf_op jit(solution)/shard_map/ppermute | solution.py:175
  87.1 2.7 %collective-permute-done.16.refs_2_ = bf16[544,128]{1,0:T(8,128)(2,1)S(1)} collective-permute-done((bf16[544,128]{1,0:T(8,128)(2,1)S(1)}, bf16[544,128]{1,0:T(8,128)(2,1)S(1)}, u32[]{:S(2)}, u32[]{:S(2)}) %collective-permute-start.16) | collective-permute-done | bytes 139296 | tf_op jit(solution)/shard_map/ppermute | solution.py:160
  89.8 2.4 %collective-permute-start.20 = (bf16[544,128]{1,0:T(8,128)(2,1)S(1)}, bf16[544,128]{1,0:T(8,128)(2,1)S(1)}, u32[]{:S(2)}, u32[]{:S(2)}) collective-permute-start(bf16[544,128]{1,0:T(8,128)(2,1)S(1)} %collective-permute-done.16.refs_2_), channel_id=1, source_target_pairs={{0,8},{4,12},{8,0},{12,4},{1,9},{5,13},{9,1},{13,5},{2,10},{6,14},... | collective-permute-start | bytes 417800 | tf_op jit(solution)/shard_map/ppermute | solution.py:175
  92.3 4.5 %collective-permute-done.20.refs_6_ = bf16[544,128]{1,0:T(8,128)(2,1)S(1)} collective-permute-done((bf16[544,128]{1,0:T(8,128)(2,1)S(1)}, bf16[544,128]{1,0:T(8,128)(2,1)S(1)}, u32[]{:S(2)}, u32[]{:S(2)}) %collective-permute-start.20) | collective-permute-done | bytes 139296 | tf_op jit(solution)/shard_map/ppermute | solution.py:175
  96.8 1.6 collective-permute-done.21.refs_7_
  98.3 1.7 %collective-permute-start.25 = (bf16[128,2048]{1,0:T(8,128)(2,1)}, bf16[128,2048]{1,0:T(8,128)(2,1)}, u32[]{:S(2)}, u32[]{:S(2)}) collective-permute-start(bf16[128,2048]{1,0:T(8,128)(2,1)} %collective-permute-done.9.refs_8_), channel_id=1, source_target_pairs={{0,8},{4,12},{8,0},{12,4},{1,9},{5,13},{9,1},{13,5},{2,10},{6,14},... | collective-permute-start | bytes 1572872 | tf_op jit(solution)/shard_map/ppermute | solution.py:175
  100.1 0.9 copy-done.2
  101.0 11.8 %chunk.7 = (bf16[128,2048]{1,0:T(8,128)(2,1)}, bf16[128,2048]{1,0:T(8,128)(2,1)}) custom-call(s32[10]{0:T(128)} %stack.52.place_ref, bf16[544,128]{1,0:T(8,128)(2,1)} %copy-done.3, bf16[544,128]{1,0:T(8,128)(2,1)} %copy-done.4, bf16[544,128]{1,0:T(8,128)(2,1)} %copy-done.5, bf16[544,128]{1,0:T(8,128)(2,1)} %copy-done.6, bf16[544,128]{1,0:T(8,128)(2,1)} %copy-done.7, ...), custom_call_target="tpu_custom_call" | custom-call | flops 5368709120 | bytes 18874368 | tf_op jit(solution)/shard_map/chunk/pallas_call | solution.py:296
  113.2 11.8 %chunk.6 = (bf16[128,2048]{1,0:T(8,128)(2,1)}, bf16[128,2048]{1,0:T(8,128)(2,1)}) custom-call(s32[10]{0:T(128)} %stack.52.place_ref, bf16[544,128]{1,0:T(8,128)(2,1)} %copy-done.3, bf16[544,128]{1,0:T(8,128)(2,1)} %copy-done.4, bf16[544,128]{1,0:T(8,128)(2,1)} %copy-done.5, bf16[544,128]{1,0:T(8,128)(2,1)} %copy-done.6, bf16[544,128]{1,0:T(8,128)(2,1)} %copy-done.7, ...), custom_call_target="tpu_custom_call" | custom-call | flops 5368709120 | bytes 18874368 | tf_op jit(solution)/shard_map/chunk/pallas_call | solution.py:296
  125.0 2.0 %collective-permute-start.27 = (bf16[128,2048]{1,0:T(8,128)(2,1)}, bf16[128,2048]{1,0:T(8,128)(2,1)S(1)}, u32[]{:S(2)}, u32[]{:S(2)}) collective-permute-start(bf16[128,2048]{1,0:T(8,128)(2,1)} %get-tuple-element.73), channel_id=1, source_target_pairs={{0,8},{4,12},{8,0},{12,4},{1,9},{5,13},{9,1},{13,5},{2,10},{6,14},... | collective-permute-start | bytes 1572872 | tf_op jit(solution)/shard_map/ppermute | solution.py:175
  127.8 11.8 %chunk.5 = (bf16[128,2048]{1,0:T(8,128)(2,1)}, bf16[128,2048]{1,0:T(8,128)(2,1)}) custom-call(s32[10]{0:T(128)} %stack.52.place_ref, bf16[544,128]{1,0:T(8,128)(2,1)} %copy-done.3, bf16[544,128]{1,0:T(8,128)(2,1)} %copy-done.4, bf16[544,128]{1,0:T(8,128)(2,1)} %copy-done.5, bf16[544,128]{1,0:T(8,128)(2,1)} %copy-done.6, bf16[544,128]{1,0:T(8,128)(2,1)} %copy-done.7, ...), custom_call_target="tpu_custom_call" | custom-call | flops 5368709120 | bytes 18874368 | tf_op jit(solution)/shard_map/chunk/pallas_call | solution.py:296
  140.8 1.4 add_convert_fusion.2
  142.8 12.0 %chunk.4 = (bf16[128,2048]{1,0:T(8,128)(2,1)}, bf16[128,2048]{1,0:T(8,128)(2,1)}, bf16[128,2048]{1,0:T(8,128)(2,1)}) custom-call(s32[10]{0:T(128)} %stack.52.place_ref, bf16[544,128]{1,0:T(8,128)(2,1)} %copy-done.3, bf16[544,128]{1,0:T(8,128)(2,1)} %copy-done.4, bf16[544,128]{1,0:T(8,128)(2,1)} %copy-done.5, bf16[544,128]{1,0:T(8,128)(2,1)} %copy-done.6, ...), custom_call_target="tpu_custom_call" | custom-call | flops 5368709120 | bytes 18874368 | tf_op jit(solution)/shard_map/chunk/pallas_call | solution.py:296
  154.8 1.8 %collective-permute-start.24 = (bf16[128,2048]{1,0:T(8,128)(2,1)}, bf16[128,2048]{1,0:T(8,128)(2,1)S(1)}, u32[]{:S(2)}, u32[]{:S(2)}) collective-permute-start(bf16[128,2048]{1,0:T(8,128)(2,1)} %get-tuple-element.66), channel_id=1, source_target_pairs={{0,8},{4,12},{8,0},{12,4},{1,9},{5,13},{9,1},{13,5},{2,10},{6,14},... | collective-permute-start | bytes 1572872 | tf_op jit(solution)/shard_map/ppermute | solution.py:175
  156.8 3.7 %collective-permute-start.31 = (bf16[128,2048]{1,0:T(8,128)(2,1)S(1)}, bf16[128,2048]{1,0:T(8,128)(2,1)S(1)}, u32[]{:S(2)}, u32[]{:S(2)}) collective-permute-start(bf16[128,2048]{1,0:T(8,128)(2,1)S(1)} %add_convert_fusion.1), channel_id=1, source_target_pairs={{0,1},{1,2},{2,3},{3,0},{4,5},{5,6},{6,7},{7,4},{8,9},{9,10},{10,1... | collective-permute-start | bytes 1572872 | tf_op jit(solution)/shard_map/ppermute | solution.py:430
  160.6 6.0 %collective-permute-done.24 = bf16[128,2048]{1,0:T(8,128)(2,1)S(1)} collective-permute-done((bf16[128,2048]{1,0:T(8,128)(2,1)}, bf16[128,2048]{1,0:T(8,128)(2,1)S(1)}, u32[]{:S(2)}, u32[]{:S(2)}) %collective-permute-start.24) | collective-permute-done | bytes 524320 | tf_op jit(solution)/shard_map/ppermute | solution.py:175
  166.6 3.0 %collective-permute-done.31 = bf16[128,2048]{1,0:T(8,128)(2,1)S(1)} collective-permute-done((bf16[128,2048]{1,0:T(8,128)(2,1)S(1)}, bf16[128,2048]{1,0:T(8,128)(2,1)S(1)}, u32[]{:S(2)}, u32[]{:S(2)}) %collective-permute-start.31) | collective-permute-done | bytes 524320 | tf_op jit(solution)/shard_map/ppermute | solution.py:430
  169.6 1.1 add_convert_fusion
  (102 shorter events, 7.5 us)
Async XLA Ops:
  0.0 20.5 %copy-start = (bf16[128,2048]{1,0:T(8,128)(2,1)S(1)}, bf16[128,2048]{1,0:T(8,128)(2,1)}, u32[]{:S(2)}) copy-start(bf16[128,2048]{1,0:T(8,128)(2,1)} %param.14) | copy-start | bytes 1572868
  0.0 18.0 %collective-permute-start.2 = (bf16[1,2048,768]{2,1,0:T(8,128)(2,1)}, bf16[1,2048,768]{2,1,0:T(8,128)(2,1)}, u32[]{:S(2)}, u32[]{:S(2)}) collective-permute-start(bf16[1,2048,768]{2,1,0:T(8,128)(2,1)} %refs_12_.7), channel_id=1, source_target_pairs={{0,4},{4,0},{8,12},{12,8},{1,5},{5,1},{9,13},{13,9},{2,6},{6,2},{1... | collective-permute-start | bytes 9437192 | tf_op jit(solution)/shard_map/ppermute | solution.py:179
  0.5 17.5 %collective-permute-start = (bf16[128,2048]{1,0:T(8,128)(2,1)}, bf16[128,2048]{1,0:T(8,128)(2,1)}, u32[]{:S(2)}, u32[]{:S(2)}) collective-permute-start(bf16[128,2048]{1,0:T(8,128)(2,1)} %refs_8_.1), channel_id=1, source_target_pairs={{0,1},{1,2},{2,3},{3,0},{4,5},{5,6},{6,7},{7,4},{8,9},{9,10},{10,1... | collective-permute-start | bytes 1572872 | tf_op jit(solution)/shard_map/ppermute | solution.py:155
  3.1 14.9 %collective-permute-start.1 = (bf16[128,2048]{1,0:T(8,128)(2,1)}, bf16[128,2048]{1,0:T(8,128)(2,1)S(1)}, u32[]{:S(2)}, u32[]{:S(2)}) collective-permute-start(bf16[128,2048]{1,0:T(8,128)(2,1)} %refs_8_.1), channel_id=1, source_target_pairs={{0,8},{4,12},{8,0},{12,4},{1,9},{5,13},{9,1},{13,5},{2,10},{6,14},... | collective-permute-start | bytes 1572872 | tf_op jit(solution)/shard_map/ppermute | solution.py:175
  7.1 38.5 %copy-start.22 = (f32[128,8]{0,1:T(8,128)S(1)}, f32[128,8]{0,1:T(8,128)}, u32[]{:S(2)}) copy-start(f32[128,8]{0,1:T(8,128)} %param.19) | copy-start | bytes 12292
  7.1 38.5 %copy-start.23 = (s32[128,8]{0,1:T(8,128)S(1)}, s32[128,8]{0,1:T(8,128)}, u32[]{:S(2)}) copy-start(s32[128,8]{0,1:T(8,128)} %param.18) | copy-start | bytes 12292
  18.0 27.7 %copy-start.13 = (bf16[128,2048]{1,0:T(8,128)(2,1)}, bf16[128,2048]{1,0:T(8,128)(2,1)S(1)}, u32[]{:S(2)}) copy-start(bf16[128,2048]{1,0:T(8,128)(2,1)S(1)} %collective-permute-done.1.refs_9_) | copy-start | bytes 1572868
  18.0 6.4 %collective-permute-start.5 = (bf16[1,2048,768]{2,1,0:T(8,128)(2,1)}, bf16[1,2048,768]{2,1,0:T(8,128)(2,1)}, u32[]{:S(2)}, u32[]{:S(2)}) collective-permute-start(bf16[1,2048,768]{2,1,0:T(8,128)(2,1)} %refs_13_.7), channel_id=1, source_target_pairs={{0,4},{4,0},{8,12},{12,8},{1,5},{5,1},{9,13},{13,9},{2,6},{6,2},{1... | collective-permute-start | bytes 9437192 | tf_op jit(solution)/shard_map/ppermute | solution.py:179
  18.1 22.0 %collective-permute-start.3 = (bf16[128,2048]{1,0:T(8,128)(2,1)}, bf16[128,2048]{1,0:T(8,128)(2,1)S(1)}, u32[]{:S(2)}, u32[]{:S(2)}) collective-permute-start(bf16[128,2048]{1,0:T(8,128)(2,1)} %collective-permute-done.refs_8_), channel_id=1, source_target_pairs={{0,1},{1,2},{2,3},{3,0},{4,5},{5,6},{6,7},{7,4},{8,9},{9,10},{10,1... | collective-permute-start | bytes 1572872 | tf_op jit(solution)/shard_map/ppermute | solution.py:155
  18.9 21.1 %collective-permute-start.4 = (bf16[128,2048]{1,0:T(8,128)(2,1)}, bf16[128,2048]{1,0:T(8,128)(2,1)}, u32[]{:S(2)}, u32[]{:S(2)}) collective-permute-start(bf16[128,2048]{1,0:T(8,128)(2,1)} %collective-permute-done.refs_8_), channel_id=1, source_target_pairs={{0,8},{4,12},{8,0},{12,4},{1,9},{5,13},{9,1},{13,5},{2,10},{6,14},... | collective-permute-start | bytes 1572872 | tf_op jit(solution)/shard_map/ppermute | solution.py:175
  20.5 17.2 %collective-permute-start.6 = (bf16[32,2048]{1,0:T(8,128)(2,1)S(1)}, bf16[32,2048]{1,0:T(8,128)(2,1)S(1)}, u32[]{:S(2)}, u32[]{:S(2)}) collective-permute-start(bf16[32,2048]{1,0:T(8,128)(2,1)S(1)} %constant_dynamic-slice_fusion), channel_id=1, source_target_pairs={{0,1},{1,2},{2,3},{3,0},{4,5},{5,6},{6,7},{7,4},{8,9},{9,10},{10,1... | collective-permute-start | bytes 393224 | tf_op jit(solution)/shard_map/ppermute | solution.py:367
  22.1 17.9 %collective-permute-start.8 = (bf16[32,2048]{1,0:T(8,128)(2,1)S(1)}, bf16[32,2048]{1,0:T(8,128)(2,1)S(1)}, u32[]{:S(2)}, u32[]{:S(2)}) collective-permute-start(bf16[32,2048]{1,0:T(8,128)(2,1)S(1)} %constant_dynamic-slice_fusion), channel_id=1, source_target_pairs={{0,3},{1,0},{2,1},{3,2},{4,7},{5,4},{6,5},{7,6},{8,11},{9,8},{10,9... | collective-permute-start | bytes 393224 | tf_op jit(solution)/shard_map/ppermute | solution.py:367
  24.4 21.3 %collective-permute-start.7 = (bf16[32,2048]{1,0:T(8,128)(2,1)S(1)}, bf16[32,2048]{1,0:T(8,128)(2,1)S(1)}, u32[]{:S(2)}, u32[]{:S(2)}) collective-permute-start(bf16[32,2048]{1,0:T(8,128)(2,1)S(1)} %constant_dynamic-slice_fusion), channel_id=1, source_target_pairs={{0,2},{1,3},{2,0},{3,1},{4,6},{5,7},{6,4},{7,5},{8,10},{9,11},{10,... | collective-permute-start | bytes 393224 | tf_op jit(solution)/shard_map/ppermute | solution.py:367
  40.0 21.4 %copy-start.12 = (bf16[128,2048]{1,0:T(8,128)(2,1)}, bf16[128,2048]{1,0:T(8,128)(2,1)S(1)}, u32[]{:S(2)}) copy-start(bf16[128,2048]{1,0:T(8,128)(2,1)S(1)} %collective-permute-done.3.refs_8_) | copy-start | bytes 1572868
  45.6 18.7 %collective-permute-start.11 = (bf16[1,768,2048]{2,1,0:T(8,128)(2,1)}, bf16[1,768,2048]{2,1,0:T(8,128)(2,1)}, u32[]{:S(2)}, u32[]{:S(2)}) collective-permute-start(bf16[1,768,2048]{2,1,0:T(8,128)(2,1)} %refs_14_.7), channel_id=1, source_target_pairs={{0,4},{4,0},{8,12},{12,8},{1,5},{5,1},{9,13},{13,9},{2,6},{6,2},{1... | collective-permute-start | bytes 9437192 | tf_op jit(solution)/shard_map/ppermute | solution.py:179
  45.8 14.5 %collective-permute-start.22 = (bf16[128,2048]{1,0:T(8,128)(2,1)S(1)}, bf16[128,2048]{1,0:T(8,128)(2,1)}, u32[]{:S(2)}, u32[]{:S(2)}) collective-permute-start(bf16[128,2048]{1,0:T(8,128)(2,1)S(1)} %constant_dynamic-update-slice_fusion), channel_id=1, source_target_pairs={{0,16},{16,0},{1,17},{17,1},{2,18},{18,2},{3,19},{19,3},{4,20},{20... | collective-permute-start | bytes 1572872 | tf_op jit(solution)/shard_map/ppermute | solution.py:375
  48.3 16.0 %collective-permute-start.9 = (bf16[128,2048]{1,0:T(8,128)(2,1)S(1)}, bf16[128,2048]{1,0:T(8,128)(2,1)}, u32[]{:S(2)}, u32[]{:S(2)}) collective-permute-start(bf16[128,2048]{1,0:T(8,128)(2,1)S(1)} %collective-permute-done.3.refs_8_), channel_id=1, source_target_pairs={{0,1},{1,2},{2,3},{3,0},{4,5},{5,6},{6,7},{7,4},{8,9},{9,10},{10,1... | collective-permute-start | bytes 1572872 | tf_op jit(solution)/shard_map/ppermute | solution.py:155
  48.4 15.9 %collective-permute-start.10 = (bf16[128,2048]{1,0:T(8,128)(2,1)S(1)}, bf16[128,2048]{1,0:T(8,128)(2,1)S(1)}, u32[]{:S(2)}, u32[]{:S(2)}) collective-permute-start(bf16[128,2048]{1,0:T(8,128)(2,1)S(1)} %collective-permute-done.3.refs_8_), channel_id=1, source_target_pairs={{0,8},{4,12},{8,0},{12,4},{1,9},{5,13},{9,1},{13,5},{2,10},{6,14},... | collective-permute-start | bytes 1572872 | tf_op jit(solution)/shard_map/ppermute | solution.py:175
  61.4 12.6 %copy-start.1 = (bf16[2,128,2048]{2,1,0:T(8,128)(2,1)}, bf16[2,128,2048]{2,1,0:T(8,128)(2,1)S(1)}, u32[]{:S(2)}) copy-start(bf16[2,128,2048]{2,1,0:T(8,128)(2,1)S(1)} %pad_maximum_fusion) | copy-start | bytes 3145732
  64.3 8.3 %copy-start.14 = (bf16[128,2048]{1,0:T(8,128)(2,1)}, bf16[128,2048]{1,0:T(8,128)(2,1)S(1)}, u32[]{:S(2)}) copy-start(bf16[128,2048]{1,0:T(8,128)(2,1)S(1)} %collective-permute-done.10.refs_9_) | copy-start | bytes 1572868
  66.2 6.3 %collective-permute-start.14 = (bf16[512,256]{1,0:T(8,128)(2,1)S(1)}, bf16[512,256]{1,0:T(8,128)(2,1)S(1)}, u32[]{:S(2)}, u32[]{:S(2)}) collective-permute-start(bf16[512,256]{1,0:T(8,128)(2,1)S(1)} %slice.47), channel_id=1, source_target_pairs={{0,4},{4,8},{8,12},{1,5},{5,9},{9,13},{2,6},{6,10},{10,14},{3,7},{... | collective-permute-start | bytes 786440 | tf_op jit(solution)/shard_map/ppermute | solution.py:29
  67.8 7.4 %collective-permute-start.13 = (bf16[128,128]{1,0:T(8,128)(2,1)S(1)}, bf16[128,128]{1,0:T(8,128)(2,1)S(1)}, u32[]{:S(2)}, u32[]{:S(2)}) collective-permute-start(bf16[128,128]{1,0:T(8,128)(2,1)S(1)} %convolution_convert_fusion.4), channel_id=1, source_target_pairs={{0,12},{1,13},{2,14},{3,15},{16,28},{17,29},{18,30},{19,31}} | collective-permute-start | bytes 98312 | tf_op jit(solution)/shard_map/ppermute | solution.py:29
  70.2 5.0 %collective-permute-start.12 = (bf16[128,128]{1,0:T(8,128)(2,1)S(1)}, bf16[128,128]{1,0:T(8,128)(2,1)S(1)}, u32[]{:S(2)}, u32[]{:S(2)}) collective-permute-start(bf16[128,128]{1,0:T(8,128)(2,1)S(1)} %convolution_convert_fusion.4), channel_id=1, source_target_pairs={{0,8},{4,12},{1,9},{5,13},{2,10},{6,14},{3,11},{7,15},{16,24},{20,... | collective-permute-start | bytes 98312 | tf_op jit(solution)/shard_map/ppermute | solution.py:29
  74.0 26.1 %collective-permute-start.23 = (bf16[2,128,2048]{2,1,0:T(8,128)(2,1)S(1)}, bf16[2,128,2048]{2,1,0:T(8,128)(2,1)S(1)}, u32[]{:S(2)}, u32[]{:S(2)}) collective-permute-start(bf16[2,128,2048]{2,1,0:T(8,128)(2,1)S(1)} %pad_maximum_fusion), channel_id=1, source_target_pairs={{0,4},{4,0},{8,12},{12,8},{1,5},{5,1},{9,13},{13,9},{2,6},{6,2},{1... | collective-permute-start | bytes 3145736 | tf_op jit(solution)/shard_map/ppermute | solution.py:179
  76.3 23.8 %copy-start.3 = (bf16[544,128]{1,0:T(8,128)(2,1)}, bf16[544,128]{1,0:T(8,128)(2,1)S(1)}, u32[]{:S(2)}) copy-start(bf16[544,128]{1,0:T(8,128)(2,1)S(1)} %pad_maximum_fusion.1.refs_0_) | copy-start | bytes 417796
  76.3 8.5 %collective-permute-start.15 = (bf16[544,128]{1,0:T(8,128)(2,1)S(1)}, bf16[544,128]{1,0:T(8,128)(2,1)S(1)}, u32[]{:S(2)}, u32[]{:S(2)}) collective-permute-start(bf16[544,128]{1,0:T(8,128)(2,1)S(1)} %pad_maximum_fusion.1.refs_0_), channel_id=1, source_target_pairs={{0,1},{1,2},{2,3},{3,0},{4,5},{5,6},{6,7},{7,4},{8,9},{9,10},{10,1... | collective-permute-start | bytes 417800 | tf_op jit(solution)/shard_map/ppermute | solution.py:160
  76.4 13.5 %collective-permute-start.16 = (bf16[544,128]{1,0:T(8,128)(2,1)S(1)}, bf16[544,128]{1,0:T(8,128)(2,1)S(1)}, u32[]{:S(2)}, u32[]{:S(2)}) collective-permute-start(bf16[544,128]{1,0:T(8,128)(2,1)S(1)} %pad_maximum_fusion.1.refs_0_), channel_id=1, source_target_pairs={{0,2},{1,3},{2,0},{3,1},{4,6},{5,7},{6,4},{7,5},{8,10},{9,11},{10,... | collective-permute-start | bytes 417800 | tf_op jit(solution)/shard_map/ppermute | solution.py:160
  78.5 13.6 %collective-permute-start.17 = (bf16[544,128]{1,0:T(8,128)(2,1)S(1)}, bf16[544,128]{1,0:T(8,128)(2,1)S(1)}, u32[]{:S(2)}, u32[]{:S(2)}) collective-permute-start(bf16[544,128]{1,0:T(8,128)(2,1)S(1)} %pad_maximum_fusion.1.refs_0_), channel_id=1, source_target_pairs={{0,3},{1,0},{2,1},{3,2},{4,7},{5,4},{6,5},{7,6},{8,11},{9,8},{10,9... | collective-permute-start | bytes 417800 | tf_op jit(solution)/shard_map/ppermute | solution.py:160
  80.2 12.1 %collective-permute-start.18 = (bf16[544,128]{1,0:T(8,128)(2,1)S(1)}, bf16[544,128]{1,0:T(8,128)(2,1)S(1)}, u32[]{:S(2)}, u32[]{:S(2)}) collective-permute-start(bf16[544,128]{1,0:T(8,128)(2,1)S(1)} %pad_maximum_fusion.1.refs_0_), channel_id=1, source_target_pairs={{0,8},{4,12},{8,0},{12,4},{1,9},{5,13},{9,1},{13,5},{2,10},{6,14},... | collective-permute-start | bytes 417800 | tf_op jit(solution)/shard_map/ppermute | solution.py:175
  84.8 15.3 %copy-start.4 = (bf16[544,128]{1,0:T(8,128)(2,1)}, bf16[544,128]{1,0:T(8,128)(2,1)S(1)}, u32[]{:S(2)}) copy-start(bf16[544,128]{1,0:T(8,128)(2,1)S(1)} %collective-permute-done.15.refs_1_) | copy-start | bytes 417796
  84.8 7.5 %collective-permute-start.19 = (bf16[544,128]{1,0:T(8,128)(2,1)S(1)}, bf16[544,128]{1,0:T(8,128)(2,1)S(1)}, u32[]{:S(2)}, u32[]{:S(2)}) collective-permute-start(bf16[544,128]{1,0:T(8,128)(2,1)S(1)} %collective-permute-done.15.refs_1_), channel_id=1, source_target_pairs={{0,8},{4,12},{8,0},{12,4},{1,9},{5,13},{9,1},{13,5},{2,10},{6,14},... | collective-permute-start | bytes 417800 | tf_op jit(solution)/shard_map/ppermute | solution.py:175
  89.8 10.3 %copy-start.5 = (bf16[544,128]{1,0:T(8,128)(2,1)}, bf16[544,128]{1,0:T(8,128)(2,1)S(1)}, u32[]{:S(2)}) copy-start(bf16[544,128]{1,0:T(8,128)(2,1)S(1)} %collective-permute-done.16.refs_2_) | copy-start | bytes 417796
  89.8 6.9 %collective-permute-start.20 = (bf16[544,128]{1,0:T(8,128)(2,1)S(1)}, bf16[544,128]{1,0:T(8,128)(2,1)S(1)}, u32[]{:S(2)}, u32[]{:S(2)}) collective-permute-start(bf16[544,128]{1,0:T(8,128)(2,1)S(1)} %collective-permute-done.16.refs_2_), channel_id=1, source_target_pairs={{0,8},{4,12},{8,0},{12,4},{1,9},{5,13},{9,1},{13,5},{2,10},{6,14},... | collective-permute-start | bytes 417800 | tf_op jit(solution)/shard_map/ppermute | solution.py:175
  92.2 7.9 %copy-start.6 = (bf16[544,128]{1,0:T(8,128)(2,1)}, bf16[544,128]{1,0:T(8,128)(2,1)S(1)}, u32[]{:S(2)}) copy-start(bf16[544,128]{1,0:T(8,128)(2,1)S(1)} %collective-permute-done.17.refs_3_) | copy-start | bytes 417796
  92.2 6.1 %collective-permute-start.21 = (bf16[544,128]{1,0:T(8,128)(2,1)S(1)}, bf16[544,128]{1,0:T(8,128)(2,1)S(1)}, u32[]{:S(2)}, u32[]{:S(2)}) collective-permute-start(bf16[544,128]{1,0:T(8,128)(2,1)S(1)} %collective-permute-done.17.refs_3_), channel_id=1, source_target_pairs={{0,8},{4,12},{8,0},{12,4},{1,9},{5,13},{9,1},{13,5},{2,10},{6,14},... | collective-permute-start | bytes 417800 | tf_op jit(solution)/shard_map/ppermute | solution.py:175
  98.3 14.9 %collective-permute-start.25 = (bf16[128,2048]{1,0:T(8,128)(2,1)}, bf16[128,2048]{1,0:T(8,128)(2,1)}, u32[]{:S(2)}, u32[]{:S(2)}) collective-permute-start(bf16[128,2048]{1,0:T(8,128)(2,1)} %collective-permute-done.9.refs_8_), channel_id=1, source_target_pairs={{0,8},{4,12},{8,0},{12,4},{1,9},{5,13},{9,1},{13,5},{2,10},{6,14},... | collective-permute-start | bytes 1572872 | tf_op jit(solution)/shard_map/ppermute | solution.py:175
  112.8 14.2 %copy-start.17 = (bf16[128,2048]{1,0:T(8,128)(2,1)S(1)}, bf16[128,2048]{1,0:T(8,128)(2,1)}, u32[]{:S(2)}) copy-start(bf16[128,2048]{1,0:T(8,128)(2,1)} %get-tuple-element.75) | copy-start | bytes 1572868
  112.9 14.2 %collective-permute-start.28 = (bf16[128,2048]{1,0:T(8,128)(2,1)}, bf16[128,2048]{1,0:T(8,128)(2,1)S(1)}, u32[]{:S(2)}, u32[]{:S(2)}) collective-permute-start(bf16[128,2048]{1,0:T(8,128)(2,1)} %get-tuple-element.76), channel_id=1, source_target_pairs={{0,8},{4,12},{8,0},{12,4},{1,9},{5,13},{9,1},{13,5},{2,10},{6,14},... | collective-permute-start | bytes 1572872 | tf_op jit(solution)/shard_map/ppermute | solution.py:175
  125.0 15.0 %collective-permute-start.27 = (bf16[128,2048]{1,0:T(8,128)(2,1)}, bf16[128,2048]{1,0:T(8,128)(2,1)S(1)}, u32[]{:S(2)}, u32[]{:S(2)}) collective-permute-start(bf16[128,2048]{1,0:T(8,128)(2,1)} %get-tuple-element.73), channel_id=1, source_target_pairs={{0,8},{4,12},{8,0},{12,4},{1,9},{5,13},{9,1},{13,5},{2,10},{6,14},... | collective-permute-start | bytes 1572872 | tf_op jit(solution)/shard_map/ppermute | solution.py:175
  127.2 13.6 %copy-start.19 = (bf16[128,2048]{1,0:T(8,128)(2,1)S(1)}, bf16[128,2048]{1,0:T(8,128)(2,1)}, u32[]{:S(2)}) copy-start(bf16[128,2048]{1,0:T(8,128)(2,1)} %get-tuple-element.72) | copy-start | bytes 1572868
  127.2 13.3 %collective-permute-start.29 = (bf16[128,2048]{1,0:T(8,128)(2,1)S(1)}, bf16[128,2048]{1,0:T(8,128)(2,1)}, u32[]{:S(2)}, u32[]{:S(2)}) collective-permute-start(bf16[128,2048]{1,0:T(8,128)(2,1)S(1)} %add_convert_fusion.3), channel_id=1, source_target_pairs={{0,1},{1,2},{2,3},{3,0},{4,5},{5,6},{6,7},{7,4},{8,9},{9,10},{10,1... | collective-permute-start | bytes 1572872 | tf_op jit(solution)/shard_map/ppermute | solution.py:430
  139.7 16.9 %collective-permute-start.26 = (bf16[128,2048]{1,0:T(8,128)(2,1)}, bf16[128,2048]{1,0:T(8,128)(2,1)S(1)}, u32[]{:S(2)}, u32[]{:S(2)}) collective-permute-start(bf16[128,2048]{1,0:T(8,128)(2,1)} %get-tuple-element.69), channel_id=1, source_target_pairs={{0,8},{4,12},{8,0},{12,4},{1,9},{5,13},{9,1},{13,5},{2,10},{6,14},... | collective-permute-start | bytes 1572872 | tf_op jit(solution)/shard_map/ppermute | solution.py:175
  142.3 14.3 %copy-start.18 = (bf16[128,2048]{1,0:T(8,128)(2,1)S(1)}, bf16[128,2048]{1,0:T(8,128)(2,1)}, u32[]{:S(2)}) copy-start(bf16[128,2048]{1,0:T(8,128)(2,1)} %get-tuple-element.68) | copy-start | bytes 1572868
  142.3 14.3 %collective-permute-start.30 = (bf16[128,2048]{1,0:T(8,128)(2,1)S(1)}, bf16[128,2048]{1,0:T(8,128)(2,1)S(1)}, u32[]{:S(2)}, u32[]{:S(2)}) collective-permute-start(bf16[128,2048]{1,0:T(8,128)(2,1)S(1)} %add_convert_fusion.2), channel_id=1, source_target_pairs={{0,1},{1,2},{2,3},{3,0},{4,5},{5,6},{6,7},{7,4},{8,9},{9,10},{10,1... | collective-permute-start | bytes 1572872 | tf_op jit(solution)/shard_map/ppermute | solution.py:430
  154.8 14.9 %copy-start.15 = (bf16[128,2048]{1,0:T(8,128)(2,1)S(1)}, bf16[128,2048]{1,0:T(8,128)(2,1)}, u32[]{:S(2)}) copy-start(bf16[128,2048]{1,0:T(8,128)(2,1)} %get-tuple-element.65) | copy-start | bytes 1572868
  154.8 14.9 %copy-start.16 = (bf16[128,2048]{1,0:T(8,128)(2,1)S(1)}, bf16[128,2048]{1,0:T(8,128)(2,1)}, u32[]{:S(2)}) copy-start(bf16[128,2048]{1,0:T(8,128)(2,1)} %get-tuple-element.64) | copy-start | bytes 1572868
  154.8 11.8 %collective-permute-start.24 = (bf16[128,2048]{1,0:T(8,128)(2,1)}, bf16[128,2048]{1,0:T(8,128)(2,1)S(1)}, u32[]{:S(2)}, u32[]{:S(2)}) collective-permute-start(bf16[128,2048]{1,0:T(8,128)(2,1)} %get-tuple-element.66), channel_id=1, source_target_pairs={{0,8},{4,12},{8,0},{12,4},{1,9},{5,13},{9,1},{13,5},{2,10},{6,14},... | collective-permute-start | bytes 1572872 | tf_op jit(solution)/shard_map/ppermute | solution.py:175
  156.8 12.8 %collective-permute-start.31 = (bf16[128,2048]{1,0:T(8,128)(2,1)S(1)}, bf16[128,2048]{1,0:T(8,128)(2,1)S(1)}, u32[]{:S(2)}, u32[]{:S(2)}) collective-permute-start(bf16[128,2048]{1,0:T(8,128)(2,1)S(1)} %add_convert_fusion.1), channel_id=1, source_target_pairs={{0,1},{1,2},{2,3},{3,0},{4,5},{5,6},{6,7},{7,4},{8,9},{9,10},{10,1... | collective-permute-start | bytes 1572872 | tf_op jit(solution)/shard_map/ppermute | solution.py:430
  (8 other events, 31.8 us)

commit v5 on v3

--- a/solution.py
+++ b/solution.py
@@ -310,7 +310,7 @@
             pltpu.SemaphoreType.DMA((2 * (head_count + 2 + group_count),)),
             pltpu.SemaphoreType.DMA((3 * experts,)),
         ],
-        compiler_params=pltpu.CompilerParams(vmem_limit_bytes=60 * 2**20),
+        compiler_params=pltpu.CompilerParams(vmem_limit_bytes=61 * 2**20),
         cost_estimate=pl.CostEstimate(
             flops=flops, bytes_accessed=sum(2 * math.prod(w.shape) for w in weights), transcendentals=0
         ),

time: 169 us -> 169 us (level)
  waiting for transfers between devices: 63.8 us -> 60.8 us
  starting transfers between devices: 40.7 us -> 43.2 us
  local copies, waits for them, and re-layouts: 6.99 us -> 4.72 us
    ppermute x3, waiting for transfers between devices: 19.1 us -> 21.7 us  [next_place(): return lax.ppermute(block, 'heads', ring_pairs(count, 1))]
    ppermute x1, waiting for transfers between devices: 2.34 us -> 0.01 us  [on_device_dense(): halves.append(lax.ppermute(halves[0], 'groups', [(0, 1), (1, 0)]))]
    unnamed x50 -> x52, local copies, waits for them, and re-layouts: 4.67 us -> 3.01 us
  transfers between devices with their start and end apart: 32 -> 32, of which waited for: 14 -> 12; matrix products, arithmetic and copies ran while one was open for 7% -> 7% of each run, Pallas kernels for 28% -> 28%
where the time goes in v5:
time: 169 us; the launch traced here: 168 us
  waiting for transfers between devices  60.8 us (36%)
  Pallas kernels  47.5 us (28%)
  starting transfers between devices  43.2 us (26%)
  matrix products  6.81 us (4%)
  local copies, waits for them, and re-layouts  4.72 us (3%)
  other arithmetic  4.72 us (3%)
    pallas_call x4, Pallas kernels, run_chunk(): pl.pallas_call(functools.partial(chunk_kernel, head_count, turn), out_sha...  47.5 us
    ppermute x3, waiting for transfers between devices, next_place(): return lax.ppermute(block, 'heads', ring_pairs(count, 1))  21.7 us
    ppermute x3, waiting for transfers between devices, on_device_dense(): lax.ppermute(piece, 'heads', ring_pairs(head_count, distance))  18.1 us
    ppermute x12, starting transfers between devices, flip_row(): return lax.ppermute(block, 'ctx', partner_pairs(ctx_count, 2))  17.4 us
    ppermute x12, waiting for transfers between devices, flip_row(): return lax.ppermute(block, 'ctx', partner_pairs(ctx_count, 2))  12.1 us
    ppermute x3, starting transfers between devices, from_behind(): return lax.ppermute(block, axis, route)  6.01 us
    ppermute x3, starting transfers between devices, on_device_dense(): lax.ppermute(piece, 'heads', ring_pairs(head_count, distance))  5.42 us
    ppermute x3, waiting for transfers between devices, gather_direct(): lax.ppermute(block, 'heads', ring_pairs(count, step))  5.36 us
  transfers between devices with their start and end apart: 32, of which 12 were waited for; matrix products, arithmetic and copies ran while one was open for 7% of the time, Pallas kernels for 28%

profile of v5, /device:TPU:0, one launch (start us, length us, event | category | flops | bytes accessed | tf_op | source)
XLA Modules:
  0.0 168.3 jit_solution(5652492577553346028)
XLA Ops:
  0.5 2.6 %collective-permute-start = (bf16[128,2048]{1,0:T(8,128)(2,1)}, bf16[128,2048]{1,0:T(8,128)(2,1)}, u32[]{:S(2)}, u32[]{:S(2)}) collective-permute-start(bf16[128,2048]{1,0:T(8,128)(2,1)} %refs_8_.1), channel_id=1, source_target_pairs={{0,1},{1,2},{2,3},{3,0},{4,5},{5,6},{6,7},{7,4},{8,9},{9,10},{10,1... | collective-permute-start | bytes 1572872 | tf_op jit(solution)/shard_map/ppermute | solution.py:155
  3.1 1.5 collective-permute-start.1
  4.6 1.7 %copy.16 = bf16[2048,3,128]{0,2,1:T(8,128)(2,1)S(1)} copy(bf16[2048,3,128]{2,0,1:T(8,128)(2,1)} %param.13) | data formatting | bytes 3145728 | tf_op args[3]
  6.4 0.6 stack.52.place_ref
  7.1 0.6 fusion.7
  7.7 10.3 %collective-permute-done.refs_8_ = bf16[128,2048]{1,0:T(8,128)(2,1)} collective-permute-done((bf16[128,2048]{1,0:T(8,128)(2,1)}, bf16[128,2048]{1,0:T(8,128)(2,1)}, u32[]{:S(2)}, u32[]{:S(2)}) %collective-permute-start) | collective-permute-done | bytes 524320 | tf_op jit(solution)/shard_map/ppermute | solution.py:155
  18.1 0.9 collective-permute-start.3
  18.9 1.5 collective-permute-start.4
  20.5 1.6 collective-permute-start.6
  22.1 2.2 %collective-permute-start.8 = (bf16[32,2048]{1,0:T(8,128)(2,1)S(1)}, bf16[32,2048]{1,0:T(8,128)(2,1)S(1)}, u32[]{:S(2)}, u32[]{:S(2)}) collective-permute-start(bf16[32,2048]{1,0:T(8,128)(2,1)S(1)} %constant_dynamic-slice_fusion), channel_id=1, source_target_pairs={{0,3},{1,0},{2,1},{3,2},{4,7},{5,4},{6,5},{7,6},{8,11},{9,8},{10,9... | collective-permute-start | bytes 393224 | tf_op jit(solution)/shard_map/ppermute | solution.py:367
  24.4 1.5 collective-permute-start.7
  25.9 1.6 fusion.6
  27.5 10.2 %collective-permute-done.6 = bf16[32,2048]{1,0:T(8,128)(2,1)S(1)} collective-permute-done((bf16[32,2048]{1,0:T(8,128)(2,1)S(1)}, bf16[32,2048]{1,0:T(8,128)(2,1)S(1)}, u32[]{:S(2)}, u32[]{:S(2)}) %collective-permute-start.6) | collective-permute-done | bytes 131104 | tf_op jit(solution)/shard_map/ppermute | solution.py:367
  37.7 2.3 %collective-permute-done.8 = bf16[32,2048]{1,0:T(8,128)(2,1)S(1)} collective-permute-done((bf16[32,2048]{1,0:T(8,128)(2,1)S(1)}, bf16[32,2048]{1,0:T(8,128)(2,1)S(1)}, u32[]{:S(2)}, u32[]{:S(2)}) %collective-permute-start.8) | collective-permute-done | bytes 131104 | tf_op jit(solution)/shard_map/ppermute | solution.py:367
  40.0 5.6 %collective-permute-done.7 = bf16[32,2048]{1,0:T(8,128)(2,1)S(1)} collective-permute-done((bf16[32,2048]{1,0:T(8,128)(2,1)S(1)}, bf16[32,2048]{1,0:T(8,128)(2,1)S(1)}, u32[]{:S(2)}, u32[]{:S(2)}) %collective-permute-start.7) | collective-permute-done | bytes 131104 | tf_op jit(solution)/shard_map/ppermute | solution.py:367
  45.8 1.6 collective-permute-start.10
  47.4 1.6 collective-permute-start.12
  49.0 1.0 slice_bitcast_fusion.1
  50.6 11.4 %collective-permute-done.9.refs_8_ = bf16[128,2048]{1,0:T(8,128)(2,1)} collective-permute-done((bf16[128,2048]{1,0:T(8,128)(2,1)S(1)}, bf16[128,2048]{1,0:T(8,128)(2,1)}, u32[]{:S(2)}, u32[]{:S(2)}) %collective-permute-start.9) | collective-permute-done | bytes 524320 | tf_op jit(solution)/shard_map/ppermute | solution.py:155
  62.0 1.7 fusion.4
  63.7 1.6 collective-permute-start.15
  65.6 2.4 %collective-permute-start.14 = (bf16[128,128]{1,0:T(8,128)(2,1)S(1)}, bf16[128,128]{1,0:T(8,128)(2,1)S(1)}, u32[]{:S(2)}, u32[]{:S(2)}) collective-permute-start(bf16[128,128]{1,0:T(8,128)(2,1)S(1)} %convolution_convert_fusion.4), channel_id=1, source_target_pairs={{0,12},{1,13},{2,14},{3,15},{16,28},{17,29},{18,30},{19,31}} | collective-permute-start | bytes 98312 | tf_op jit(solution)/shard_map/ppermute | solution.py:29
  68.0 2.0 %collective-permute-start.13 = (bf16[128,128]{1,0:T(8,128)(2,1)S(1)}, bf16[128,128]{1,0:T(8,128)(2,1)S(1)}, u32[]{:S(2)}, u32[]{:S(2)}) collective-permute-start(bf16[128,128]{1,0:T(8,128)(2,1)S(1)} %convolution_convert_fusion.4), channel_id=1, source_target_pairs={{0,8},{4,12},{1,9},{5,13},{2,10},{6,14},{3,11},{7,15},{16,24},{20,... | collective-permute-start | bytes 98312 | tf_op jit(solution)/shard_map/ppermute | solution.py:29
  70.0 1.1 pad_maximum_fusion
  73.3 0.7 add_convert_fusion.4
  74.1 2.6 %collective-permute-start.17 = (bf16[544,128]{1,0:T(8,128)(2,1)S(1)}, bf16[544,128]{1,0:T(8,128)(2,1)S(1)}, u32[]{:S(2)}, u32[]{:S(2)}) collective-permute-start(bf16[544,128]{1,0:T(8,128)(2,1)S(1)} %pad_maximum_fusion.1.refs_0_), channel_id=1, source_target_pairs={{0,2},{1,3},{2,0},{3,1},{4,6},{5,7},{6,4},{7,5},{8,10},{9,11},{10,... | collective-permute-start | bytes 417800 | tf_op jit(solution)/shard_map/ppermute | solution.py:160
  76.7 1.2 collective-permute-start.18
  77.9 2.1 %collective-permute-start.19 = (bf16[544,128]{1,0:T(8,128)(2,1)S(1)}, bf16[544,128]{1,0:T(8,128)(2,1)S(1)}, u32[]{:S(2)}, u32[]{:S(2)}) collective-permute-start(bf16[544,128]{1,0:T(8,128)(2,1)S(1)} %pad_maximum_fusion.1.refs_0_), channel_id=1, source_target_pairs={{0,8},{4,12},{8,0},{12,4},{1,9},{5,13},{9,1},{13,5},{2,10},{6,14},... | collective-permute-start | bytes 417800 | tf_op jit(solution)/shard_map/ppermute | solution.py:175
  80.0 2.5 %collective-permute-done.16.refs_1_ = bf16[544,128]{1,0:T(8,128)(2,1)S(1)} collective-permute-done((bf16[544,128]{1,0:T(8,128)(2,1)S(1)}, bf16[544,128]{1,0:T(8,128)(2,1)S(1)}, u32[]{:S(2)}, u32[]{:S(2)}) %collective-permute-start.16) | collective-permute-done | bytes 139296 | tf_op jit(solution)/shard_map/ppermute | solution.py:160
  82.5 2.1 %collective-permute-start.20 = (bf16[544,128]{1,0:T(8,128)(2,1)S(1)}, bf16[544,128]{1,0:T(8,128)(2,1)S(1)}, u32[]{:S(2)}, u32[]{:S(2)}) collective-permute-start(bf16[544,128]{1,0:T(8,128)(2,1)S(1)} %collective-permute-done.16.refs_1_), channel_id=1, source_target_pairs={{0,8},{4,12},{8,0},{12,4},{1,9},{5,13},{9,1},{13,5},{2,10},{6,14},... | collective-permute-start | bytes 417800 | tf_op jit(solution)/shard_map/ppermute | solution.py:175
  84.6 2.9 %collective-permute-done.17.refs_2_ = bf16[544,128]{1,0:T(8,128)(2,1)S(1)} collective-permute-done((bf16[544,128]{1,0:T(8,128)(2,1)S(1)}, bf16[544,128]{1,0:T(8,128)(2,1)S(1)}, u32[]{:S(2)}, u32[]{:S(2)}) %collective-permute-start.17) | collective-permute-done | bytes 139296 | tf_op jit(solution)/shard_map/ppermute | solution.py:160
  87.5 2.1 %collective-permute-start.21 = (bf16[544,128]{1,0:T(8,128)(2,1)S(1)}, bf16[544,128]{1,0:T(8,128)(2,1)S(1)}, u32[]{:S(2)}, u32[]{:S(2)}) collective-permute-start(bf16[544,128]{1,0:T(8,128)(2,1)S(1)} %collective-permute-done.17.refs_2_), channel_id=1, source_target_pairs={{0,8},{4,12},{8,0},{12,4},{1,9},{5,13},{9,1},{13,5},{2,10},{6,14},... | collective-permute-start | bytes 417800 | tf_op jit(solution)/shard_map/ppermute | solution.py:175
  89.8 4.5 %collective-permute-done.21.refs_6_ = bf16[544,128]{1,0:T(8,128)(2,1)S(1)} collective-permute-done((bf16[544,128]{1,0:T(8,128)(2,1)S(1)}, bf16[544,128]{1,0:T(8,128)(2,1)S(1)}, u32[]{:S(2)}, u32[]{:S(2)}) %collective-permute-start.21) | collective-permute-done | bytes 139296 | tf_op jit(solution)/shard_map/ppermute | solution.py:175
  94.2 1.6 collective-permute-done.22.refs_7_
  95.8 1.7 %collective-permute-start.25 = (bf16[128,2048]{1,0:T(8,128)(2,1)}, bf16[128,2048]{1,0:T(8,128)(2,1)S(1)}, u32[]{:S(2)}, u32[]{:S(2)}) collective-permute-start(bf16[128,2048]{1,0:T(8,128)(2,1)} %collective-permute-done.9.refs_8_), channel_id=1, source_target_pairs={{0,8},{4,12},{8,0},{12,4},{1,9},{5,13},{9,1},{13,5},{2,10},{6,14},... | collective-permute-start | bytes 1572872 | tf_op jit(solution)/shard_map/ppermute | solution.py:175
  97.6 0.9 copy-done.2
  98.5 11.8 %chunk.7 = (bf16[128,2048]{1,0:T(8,128)(2,1)}, bf16[128,2048]{1,0:T(8,128)(2,1)}) custom-call(s32[10]{0:T(128)} %stack.52.place_ref, bf16[544,128]{1,0:T(8,128)(2,1)} %copy-done.3, bf16[544,128]{1,0:T(8,128)(2,1)} %copy-done.4, bf16[544,128]{1,0:T(8,128)(2,1)} %copy-done.5, bf16[544,128]{1,0:T(8,128)(2,1)} %copy-done.6, bf16[544,128]{1,0:T(8,128)(2,1)} %copy-done.7, ...), custom_call_target="tpu_custom_call" | custom-call | flops 5368709120 | bytes 18874368 | tf_op jit(solution)/shard_map/chunk/pallas_call | solution.py:296
  110.7 11.8 %chunk.6 = (bf16[128,2048]{1,0:T(8,128)(2,1)}, bf16[128,2048]{1,0:T(8,128)(2,1)}) custom-call(s32[10]{0:T(128)} %stack.52.place_ref, bf16[544,128]{1,0:T(8,128)(2,1)} %copy-done.3, bf16[544,128]{1,0:T(8,128)(2,1)} %copy-done.4, bf16[544,128]{1,0:T(8,128)(2,1)} %copy-done.5, bf16[544,128]{1,0:T(8,128)(2,1)} %copy-done.6, bf16[544,128]{1,0:T(8,128)(2,1)} %copy-done.7, ...), custom_call_target="tpu_custom_call" | custom-call | flops 5368709120 | bytes 18874368 | tf_op jit(solution)/shard_map/chunk/pallas_call | solution.py:296
  122.6 2.0 %collective-permute-start.27 = (bf16[128,2048]{1,0:T(8,128)(2,1)}, bf16[128,2048]{1,0:T(8,128)(2,1)S(1)}, u32[]{:S(2)}, u32[]{:S(2)}) collective-permute-start(bf16[128,2048]{1,0:T(8,128)(2,1)} %get-tuple-element.77), channel_id=1, source_target_pairs={{0,8},{4,12},{8,0},{12,4},{1,9},{5,13},{9,1},{13,5},{2,10},{6,14},... | collective-permute-start | bytes 1572872 | tf_op jit(solution)/shard_map/ppermute | solution.py:175
  124.8 0.6 collective-permute-start.29
  125.4 11.8 %chunk.5 = (bf16[128,2048]{1,0:T(8,128)(2,1)}, bf16[128,2048]{1,0:T(8,128)(2,1)}) custom-call(s32[10]{0:T(128)} %stack.52.place_ref, bf16[544,128]{1,0:T(8,128)(2,1)} %copy-done.3, bf16[544,128]{1,0:T(8,128)(2,1)} %copy-done.4, bf16[544,128]{1,0:T(8,128)(2,1)} %copy-done.5, bf16[544,128]{1,0:T(8,128)(2,1)} %copy-done.6, bf16[544,128]{1,0:T(8,128)(2,1)} %copy-done.7, ...), custom_call_target="tpu_custom_call" | custom-call | flops 5368709120 | bytes 18874368 | tf_op jit(solution)/shard_map/chunk/pallas_call | solution.py:296
  138.4 1.4 add_convert_fusion.2
  140.3 12.0 %chunk.4 = (bf16[128,2048]{1,0:T(8,128)(2,1)}, bf16[128,2048]{1,0:T(8,128)(2,1)}, bf16[128,2048]{1,0:T(8,128)(2,1)}) custom-call(s32[10]{0:T(128)} %stack.52.place_ref, bf16[544,128]{1,0:T(8,128)(2,1)} %copy-done.3, bf16[544,128]{1,0:T(8,128)(2,1)} %copy-done.4, bf16[544,128]{1,0:T(8,128)(2,1)} %copy-done.5, bf16[544,128]{1,0:T(8,128)(2,1)} %copy-done.6, ...), custom_call_target="tpu_custom_call" | custom-call | flops 5368709120 | bytes 18874368 | tf_op jit(solution)/shard_map/chunk/pallas_call | solution.py:296
  152.3 1.8 %collective-permute-start.24 = (bf16[128,2048]{1,0:T(8,128)(2,1)}, bf16[128,2048]{1,0:T(8,128)(2,1)S(1)}, u32[]{:S(2)}, u32[]{:S(2)}) collective-permute-start(bf16[128,2048]{1,0:T(8,128)(2,1)} %get-tuple-element.70), channel_id=1, source_target_pairs={{0,8},{4,12},{8,0},{12,4},{1,9},{5,13},{9,1},{13,5},{2,10},{6,14},... | collective-permute-start | bytes 1572872 | tf_op jit(solution)/shard_map/ppermute | solution.py:175
  154.4 3.7 %collective-permute-start.31 = (bf16[128,2048]{1,0:T(8,128)(2,1)S(1)}, bf16[128,2048]{1,0:T(8,128)(2,1)S(1)}, u32[]{:S(2)}, u32[]{:S(2)}) collective-permute-start(bf16[128,2048]{1,0:T(8,128)(2,1)S(1)} %add_convert_fusion.1), channel_id=1, source_target_pairs={{0,1},{1,2},{2,3},{3,0},{4,5},{5,6},{6,7},{7,4},{8,9},{9,10},{10,1... | collective-permute-start | bytes 1572872 | tf_op jit(solution)/shard_map/ppermute | solution.py:430
  158.1 6.0 %collective-permute-done.24 = bf16[128,2048]{1,0:T(8,128)(2,1)S(1)} collective-permute-done((bf16[128,2048]{1,0:T(8,128)(2,1)}, bf16[128,2048]{1,0:T(8,128)(2,1)S(1)}, u32[]{:S(2)}, u32[]{:S(2)}) %collective-permute-start.24) | collective-permute-done | bytes 524320 | tf_op jit(solution)/shard_map/ppermute | solution.py:175
  164.1 3.0 %collective-permute-done.31 = bf16[128,2048]{1,0:T(8,128)(2,1)S(1)} collective-permute-done((bf16[128,2048]{1,0:T(8,128)(2,1)S(1)}, bf16[128,2048]{1,0:T(8,128)(2,1)S(1)}, u32[]{:S(2)}, u32[]{:S(2)}) %collective-permute-start.31) | collective-permute-done | bytes 524320 | tf_op jit(solution)/shard_map/ppermute | solution.py:430
  167.2 1.1 add_convert_fusion
  (102 shorter events, 6.3 us)
Async XLA Ops:
  0.0 20.5 %copy-start = (bf16[128,2048]{1,0:T(8,128)(2,1)S(1)}, bf16[128,2048]{1,0:T(8,128)(2,1)}, u32[]{:S(2)}) copy-start(bf16[128,2048]{1,0:T(8,128)(2,1)} %param.14) | copy-start | bytes 1572868
  0.0 18.0 %collective-permute-start.2 = (bf16[1,2048,768]{2,1,0:T(8,128)(2,1)}, bf16[1,2048,768]{2,1,0:T(8,128)(2,1)}, u32[]{:S(2)}, u32[]{:S(2)}) collective-permute-start(bf16[1,2048,768]{2,1,0:T(8,128)(2,1)} %refs_12_.7), channel_id=1, source_target_pairs={{0,4},{4,0},{8,12},{12,8},{1,5},{5,1},{9,13},{13,9},{2,6},{6,2},{1... | collective-permute-start | bytes 9437192 | tf_op jit(solution)/shard_map/ppermute | solution.py:179
  0.5 17.5 %collective-permute-start = (bf16[128,2048]{1,0:T(8,128)(2,1)}, bf16[128,2048]{1,0:T(8,128)(2,1)}, u32[]{:S(2)}, u32[]{:S(2)}) collective-permute-start(bf16[128,2048]{1,0:T(8,128)(2,1)} %refs_8_.1), channel_id=1, source_target_pairs={{0,1},{1,2},{2,3},{3,0},{4,5},{5,6},{6,7},{7,4},{8,9},{9,10},{10,1... | collective-permute-start | bytes 1572872 | tf_op jit(solution)/shard_map/ppermute | solution.py:155
  3.1 14.9 %collective-permute-start.1 = (bf16[128,2048]{1,0:T(8,128)(2,1)}, bf16[128,2048]{1,0:T(8,128)(2,1)S(1)}, u32[]{:S(2)}, u32[]{:S(2)}) collective-permute-start(bf16[128,2048]{1,0:T(8,128)(2,1)} %refs_8_.1), channel_id=1, source_target_pairs={{0,8},{4,12},{8,0},{12,4},{1,9},{5,13},{9,1},{13,5},{2,10},{6,14},... | collective-permute-start | bytes 1572872 | tf_op jit(solution)/shard_map/ppermute | solution.py:175
  7.0 38.6 %copy-start.22 = (f32[128,8]{0,1:T(8,128)S(1)}, f32[128,8]{0,1:T(8,128)}, u32[]{:S(2)}) copy-start(f32[128,8]{0,1:T(8,128)} %param.19) | copy-start | bytes 12292
  7.1 38.6 %copy-start.23 = (s32[128,8]{0,1:T(8,128)S(1)}, s32[128,8]{0,1:T(8,128)}, u32[]{:S(2)}) copy-start(s32[128,8]{0,1:T(8,128)} %param.18) | copy-start | bytes 12292
  18.0 27.8 %copy-start.13 = (bf16[128,2048]{1,0:T(8,128)(2,1)}, bf16[128,2048]{1,0:T(8,128)(2,1)S(1)}, u32[]{:S(2)}) copy-start(bf16[128,2048]{1,0:T(8,128)(2,1)S(1)} %collective-permute-done.1.refs_9_) | copy-start | bytes 1572868
  18.0 6.4 %collective-permute-start.5 = (bf16[1,2048,768]{2,1,0:T(8,128)(2,1)}, bf16[1,2048,768]{2,1,0:T(8,128)(2,1)}, u32[]{:S(2)}, u32[]{:S(2)}) collective-permute-start(bf16[1,2048,768]{2,1,0:T(8,128)(2,1)} %refs_13_.7), channel_id=1, source_target_pairs={{0,4},{4,0},{8,12},{12,8},{1,5},{5,1},{9,13},{13,9},{2,6},{6,2},{1... | collective-permute-start | bytes 9437192 | tf_op jit(solution)/shard_map/ppermute | solution.py:179
  18.1 22.0 %collective-permute-start.3 = (bf16[128,2048]{1,0:T(8,128)(2,1)}, bf16[128,2048]{1,0:T(8,128)(2,1)S(1)}, u32[]{:S(2)}, u32[]{:S(2)}) collective-permute-start(bf16[128,2048]{1,0:T(8,128)(2,1)} %collective-permute-done.refs_8_), channel_id=1, source_target_pairs={{0,1},{1,2},{2,3},{3,0},{4,5},{5,6},{6,7},{7,4},{8,9},{9,10},{10,1... | collective-permute-start | bytes 1572872 | tf_op jit(solution)/shard_map/ppermute | solution.py:155
  18.9 21.1 %collective-permute-start.4 = (bf16[128,2048]{1,0:T(8,128)(2,1)}, bf16[128,2048]{1,0:T(8,128)(2,1)}, u32[]{:S(2)}, u32[]{:S(2)}) collective-permute-start(bf16[128,2048]{1,0:T(8,128)(2,1)} %collective-permute-done.refs_8_), channel_id=1, source_target_pairs={{0,8},{4,12},{8,0},{12,4},{1,9},{5,13},{9,1},{13,5},{2,10},{6,14},... | collective-permute-start | bytes 1572872 | tf_op jit(solution)/shard_map/ppermute | solution.py:175
  20.5 17.2 %collective-permute-start.6 = (bf16[32,2048]{1,0:T(8,128)(2,1)S(1)}, bf16[32,2048]{1,0:T(8,128)(2,1)S(1)}, u32[]{:S(2)}, u32[]{:S(2)}) collective-permute-start(bf16[32,2048]{1,0:T(8,128)(2,1)S(1)} %constant_dynamic-slice_fusion), channel_id=1, source_target_pairs={{0,1},{1,2},{2,3},{3,0},{4,5},{5,6},{6,7},{7,4},{8,9},{9,10},{10,1... | collective-permute-start | bytes 393224 | tf_op jit(solution)/shard_map/ppermute | solution.py:367
  22.1 17.9 %collective-permute-start.8 = (bf16[32,2048]{1,0:T(8,128)(2,1)S(1)}, bf16[32,2048]{1,0:T(8,128)(2,1)S(1)}, u32[]{:S(2)}, u32[]{:S(2)}) collective-permute-start(bf16[32,2048]{1,0:T(8,128)(2,1)S(1)} %constant_dynamic-slice_fusion), channel_id=1, source_target_pairs={{0,3},{1,0},{2,1},{3,2},{4,7},{5,4},{6,5},{7,6},{8,11},{9,8},{10,9... | collective-permute-start | bytes 393224 | tf_op jit(solution)/shard_map/ppermute | solution.py:367
  24.4 21.3 %collective-permute-start.7 = (bf16[32,2048]{1,0:T(8,128)(2,1)S(1)}, bf16[32,2048]{1,0:T(8,128)(2,1)S(1)}, u32[]{:S(2)}, u32[]{:S(2)}) collective-permute-start(bf16[32,2048]{1,0:T(8,128)(2,1)S(1)} %constant_dynamic-slice_fusion), channel_id=1, source_target_pairs={{0,2},{1,3},{2,0},{3,1},{4,6},{5,7},{6,4},{7,5},{8,10},{9,11},{10,... | collective-permute-start | bytes 393224 | tf_op jit(solution)/shard_map/ppermute | solution.py:367
  40.0 23.6 %copy-start.12 = (bf16[128,2048]{1,0:T(8,128)(2,1)}, bf16[128,2048]{1,0:T(8,128)(2,1)S(1)}, u32[]{:S(2)}) copy-start(bf16[128,2048]{1,0:T(8,128)(2,1)S(1)} %collective-permute-done.3.refs_8_) | copy-start | bytes 1572868
  45.6 16.3 %collective-permute-start.11 = (bf16[1,768,2048]{2,1,0:T(8,128)(2,1)}, bf16[1,768,2048]{2,1,0:T(8,128)(2,1)}, u32[]{:S(2)}, u32[]{:S(2)}) collective-permute-start(bf16[1,768,2048]{2,1,0:T(8,128)(2,1)} %refs_14_.7), channel_id=1, source_target_pairs={{0,4},{4,0},{8,12},{12,8},{1,5},{5,1},{9,13},{13,9},{2,6},{6,2},{1... | collective-permute-start | bytes 9437192 | tf_op jit(solution)/shard_map/ppermute | solution.py:179
  45.7 16.3 %collective-permute-start.9 = (bf16[128,2048]{1,0:T(8,128)(2,1)S(1)}, bf16[128,2048]{1,0:T(8,128)(2,1)}, u32[]{:S(2)}, u32[]{:S(2)}) collective-permute-start(bf16[128,2048]{1,0:T(8,128)(2,1)S(1)} %collective-permute-done.3.refs_8_), channel_id=1, source_target_pairs={{0,1},{1,2},{2,3},{3,0},{4,5},{5,6},{6,7},{7,4},{8,9},{9,10},{10,1... | collective-permute-start | bytes 1572872 | tf_op jit(solution)/shard_map/ppermute | solution.py:155
  45.8 16.2 %collective-permute-start.10 = (bf16[128,2048]{1,0:T(8,128)(2,1)S(1)}, bf16[128,2048]{1,0:T(8,128)(2,1)}, u32[]{:S(2)}, u32[]{:S(2)}) collective-permute-start(bf16[128,2048]{1,0:T(8,128)(2,1)S(1)} %collective-permute-done.3.refs_8_), channel_id=1, source_target_pairs={{0,8},{4,12},{8,0},{12,4},{1,9},{5,13},{9,1},{13,5},{2,10},{6,14},... | collective-permute-start | bytes 1572872 | tf_op jit(solution)/shard_map/ppermute | solution.py:175
  47.4 14.6 %collective-permute-start.12 = (bf16[128,2048]{1,0:T(8,128)(2,1)S(1)}, bf16[128,2048]{1,0:T(8,128)(2,1)}, u32[]{:S(2)}, u32[]{:S(2)}) collective-permute-start(bf16[128,2048]{1,0:T(8,128)(2,1)S(1)} %constant_dynamic-update-slice_fusion), channel_id=1, source_target_pairs={{0,16},{16,0},{1,17},{17,1},{2,18},{18,2},{3,19},{19,3},{4,20},{20... | collective-permute-start | bytes 1572872 | tf_op jit(solution)/shard_map/ppermute | solution.py:375
  63.7 7.4 %collective-permute-start.15 = (bf16[512,256]{1,0:T(8,128)(2,1)S(1)}, bf16[512,256]{1,0:T(8,128)(2,1)S(1)}, u32[]{:S(2)}, u32[]{:S(2)}) collective-permute-start(bf16[512,256]{1,0:T(8,128)(2,1)S(1)} %slice.47), channel_id=1, source_target_pairs={{0,4},{4,8},{8,12},{1,5},{5,9},{9,13},{2,6},{6,10},{10,14},{3,7},{... | collective-permute-start | bytes 786440 | tf_op jit(solution)/shard_map/ppermute | solution.py:29
  65.6 7.3 %collective-permute-start.14 = (bf16[128,128]{1,0:T(8,128)(2,1)S(1)}, bf16[128,128]{1,0:T(8,128)(2,1)S(1)}, u32[]{:S(2)}, u32[]{:S(2)}) collective-permute-start(bf16[128,128]{1,0:T(8,128)(2,1)S(1)} %convolution_convert_fusion.4), channel_id=1, source_target_pairs={{0,12},{1,13},{2,14},{3,15},{16,28},{17,29},{18,30},{19,31}} | collective-permute-start | bytes 98312 | tf_op jit(solution)/shard_map/ppermute | solution.py:29
  68.0 4.9 %collective-permute-start.13 = (bf16[128,128]{1,0:T(8,128)(2,1)S(1)}, bf16[128,128]{1,0:T(8,128)(2,1)S(1)}, u32[]{:S(2)}, u32[]{:S(2)}) collective-permute-start(bf16[128,128]{1,0:T(8,128)(2,1)S(1)} %convolution_convert_fusion.4), channel_id=1, source_target_pairs={{0,8},{4,12},{1,9},{5,13},{2,10},{6,14},{3,11},{7,15},{16,24},{20,... | collective-permute-start | bytes 98312 | tf_op jit(solution)/shard_map/ppermute | solution.py:29
  72.6 25.0 %collective-permute-start.23 = (bf16[2,128,2048]{2,1,0:T(8,128)(2,1)S(1)}, bf16[2,128,2048]{2,1,0:T(8,128)(2,1)S(1)}, u32[]{:S(2)}, u32[]{:S(2)}) collective-permute-start(bf16[2,128,2048]{2,1,0:T(8,128)(2,1)S(1)} %pad_maximum_fusion), channel_id=1, source_target_pairs={{0,4},{4,0},{8,12},{12,8},{1,5},{5,1},{9,13},{13,9},{2,6},{6,2},{1... | collective-permute-start | bytes 3145736 | tf_op jit(solution)/shard_map/ppermute | solution.py:179
  74.0 23.6 %copy-start.3 = (bf16[544,128]{1,0:T(8,128)(2,1)}, bf16[544,128]{1,0:T(8,128)(2,1)S(1)}, u32[]{:S(2)}) copy-start(bf16[544,128]{1,0:T(8,128)(2,1)S(1)} %pad_maximum_fusion.1.refs_0_) | copy-start | bytes 417796
  74.0 8.5 %collective-permute-start.16 = (bf16[544,128]{1,0:T(8,128)(2,1)S(1)}, bf16[544,128]{1,0:T(8,128)(2,1)S(1)}, u32[]{:S(2)}, u32[]{:S(2)}) collective-permute-start(bf16[544,128]{1,0:T(8,128)(2,1)S(1)} %pad_maximum_fusion.1.refs_0_), channel_id=1, source_target_pairs={{0,1},{1,2},{2,3},{3,0},{4,5},{5,6},{6,7},{7,4},{8,9},{9,10},{10,1... | collective-permute-start | bytes 417800 | tf_op jit(solution)/shard_map/ppermute | solution.py:160
  74.1 13.4 %collective-permute-start.17 = (bf16[544,128]{1,0:T(8,128)(2,1)S(1)}, bf16[544,128]{1,0:T(8,128)(2,1)S(1)}, u32[]{:S(2)}, u32[]{:S(2)}) collective-permute-start(bf16[544,128]{1,0:T(8,128)(2,1)S(1)} %pad_maximum_fusion.1.refs_0_), channel_id=1, source_target_pairs={{0,2},{1,3},{2,0},{3,1},{4,6},{5,7},{6,4},{7,5},{8,10},{9,11},{10,... | collective-permute-start | bytes 417800 | tf_op jit(solution)/shard_map/ppermute | solution.py:160
  76.7 12.9 %collective-permute-start.18 = (bf16[544,128]{1,0:T(8,128)(2,1)S(1)}, bf16[544,128]{1,0:T(8,128)(2,1)S(1)}, u32[]{:S(2)}, u32[]{:S(2)}) collective-permute-start(bf16[544,128]{1,0:T(8,128)(2,1)S(1)} %pad_maximum_fusion.1.refs_0_), channel_id=1, source_target_pairs={{0,3},{1,0},{2,1},{3,2},{4,7},{5,4},{6,5},{7,6},{8,11},{9,8},{10,9... | collective-permute-start | bytes 417800 | tf_op jit(solution)/shard_map/ppermute | solution.py:160
  77.9 11.9 %collective-permute-start.19 = (bf16[544,128]{1,0:T(8,128)(2,1)S(1)}, bf16[544,128]{1,0:T(8,128)(2,1)S(1)}, u32[]{:S(2)}, u32[]{:S(2)}) collective-permute-start(bf16[544,128]{1,0:T(8,128)(2,1)S(1)} %pad_maximum_fusion.1.refs_0_), channel_id=1, source_target_pairs={{0,8},{4,12},{8,0},{12,4},{1,9},{5,13},{9,1},{13,5},{2,10},{6,14},... | collective-permute-start | bytes 417800 | tf_op jit(solution)/shard_map/ppermute | solution.py:175
  82.5 15.1 %copy-start.4 = (bf16[544,128]{1,0:T(8,128)(2,1)}, bf16[544,128]{1,0:T(8,128)(2,1)S(1)}, u32[]{:S(2)}) copy-start(bf16[544,128]{1,0:T(8,128)(2,1)S(1)} %collective-permute-done.16.refs_1_) | copy-start | bytes 417796
  82.5 7.3 %collective-permute-start.20 = (bf16[544,128]{1,0:T(8,128)(2,1)S(1)}, bf16[544,128]{1,0:T(8,128)(2,1)S(1)}, u32[]{:S(2)}, u32[]{:S(2)}) collective-permute-start(bf16[544,128]{1,0:T(8,128)(2,1)S(1)} %collective-permute-done.16.refs_1_), channel_id=1, source_target_pairs={{0,8},{4,12},{8,0},{12,4},{1,9},{5,13},{9,1},{13,5},{2,10},{6,14},... | collective-permute-start | bytes 417800 | tf_op jit(solution)/shard_map/ppermute | solution.py:175
  87.5 10.1 %copy-start.5 = (bf16[544,128]{1,0:T(8,128)(2,1)}, bf16[544,128]{1,0:T(8,128)(2,1)S(1)}, u32[]{:S(2)}) copy-start(bf16[544,128]{1,0:T(8,128)(2,1)S(1)} %collective-permute-done.17.refs_2_) | copy-start | bytes 417796
  87.5 6.7 %collective-permute-start.21 = (bf16[544,128]{1,0:T(8,128)(2,1)S(1)}, bf16[544,128]{1,0:T(8,128)(2,1)S(1)}, u32[]{:S(2)}, u32[]{:S(2)}) collective-permute-start(bf16[544,128]{1,0:T(8,128)(2,1)S(1)} %collective-permute-done.17.refs_2_), channel_id=1, source_target_pairs={{0,8},{4,12},{8,0},{12,4},{1,9},{5,13},{9,1},{13,5},{2,10},{6,14},... | collective-permute-start | bytes 417800 | tf_op jit(solution)/shard_map/ppermute | solution.py:175
  89.7 7.9 %copy-start.6 = (bf16[544,128]{1,0:T(8,128)(2,1)}, bf16[544,128]{1,0:T(8,128)(2,1)S(1)}, u32[]{:S(2)}) copy-start(bf16[544,128]{1,0:T(8,128)(2,1)S(1)} %collective-permute-done.18.refs_3_) | copy-start | bytes 417796
  89.7 6.1 %collective-permute-start.22 = (bf16[544,128]{1,0:T(8,128)(2,1)S(1)}, bf16[544,128]{1,0:T(8,128)(2,1)S(1)}, u32[]{:S(2)}, u32[]{:S(2)}) collective-permute-start(bf16[544,128]{1,0:T(8,128)(2,1)S(1)} %collective-permute-done.18.refs_3_), channel_id=1, source_target_pairs={{0,8},{4,12},{8,0},{12,4},{1,9},{5,13},{9,1},{13,5},{2,10},{6,14},... | collective-permute-start | bytes 417800 | tf_op jit(solution)/shard_map/ppermute | solution.py:175
  89.8 7.8 %copy-start.7 = (bf16[544,128]{1,0:T(8,128)(2,1)}, bf16[544,128]{1,0:T(8,128)(2,1)S(1)}, u32[]{:S(2)}) copy-start(bf16[544,128]{1,0:T(8,128)(2,1)S(1)} %collective-permute-done.19.refs_4_) | copy-start | bytes 417796
  95.8 14.9 %collective-permute-start.25 = (bf16[128,2048]{1,0:T(8,128)(2,1)}, bf16[128,2048]{1,0:T(8,128)(2,1)S(1)}, u32[]{:S(2)}, u32[]{:S(2)}) collective-permute-start(bf16[128,2048]{1,0:T(8,128)(2,1)} %collective-permute-done.9.refs_8_), channel_id=1, source_target_pairs={{0,8},{4,12},{8,0},{12,4},{1,9},{5,13},{9,1},{13,5},{2,10},{6,14},... | collective-permute-start | bytes 1572872 | tf_op jit(solution)/shard_map/ppermute | solution.py:175
  110.3 14.3 %copy-start.17 = (bf16[128,2048]{1,0:T(8,128)(2,1)S(1)}, bf16[128,2048]{1,0:T(8,128)(2,1)}, u32[]{:S(2)}) copy-start(bf16[128,2048]{1,0:T(8,128)(2,1)} %get-tuple-element.79) | copy-start | bytes 1572868
  110.4 14.3 %collective-permute-start.28 = (bf16[128,2048]{1,0:T(8,128)(2,1)}, bf16[128,2048]{1,0:T(8,128)(2,1)S(1)}, u32[]{:S(2)}, u32[]{:S(2)}) collective-permute-start(bf16[128,2048]{1,0:T(8,128)(2,1)} %get-tuple-element.80), channel_id=1, source_target_pairs={{0,8},{4,12},{8,0},{12,4},{1,9},{5,13},{9,1},{13,5},{2,10},{6,14},... | collective-permute-start | bytes 1572872 | tf_op jit(solution)/shard_map/ppermute | solution.py:175
  110.7 11.9 %copy-start.16 = (bf16[128,2048]{1,0:T(8,128)(2,1)}, bf16[128,2048]{1,0:T(8,128)(2,1)S(1)}, u32[]{:S(2)}) copy-start(bf16[128,2048]{1,0:T(8,128)(2,1)S(1)} %collective-permute-done.25.refs_9_) | copy-start | bytes 1572868
  122.6 15.0 %collective-permute-start.27 = (bf16[128,2048]{1,0:T(8,128)(2,1)}, bf16[128,2048]{1,0:T(8,128)(2,1)S(1)}, u32[]{:S(2)}, u32[]{:S(2)}) collective-permute-start(bf16[128,2048]{1,0:T(8,128)(2,1)} %get-tuple-element.77), channel_id=1, source_target_pairs={{0,8},{4,12},{8,0},{12,4},{1,9},{5,13},{9,1},{13,5},{2,10},{6,14},... | collective-permute-start | bytes 1572872 | tf_op jit(solution)/shard_map/ppermute | solution.py:175
  124.7 13.6 %copy-start.19 = (bf16[128,2048]{1,0:T(8,128)(2,1)S(1)}, bf16[128,2048]{1,0:T(8,128)(2,1)}, u32[]{:S(2)}) copy-start(bf16[128,2048]{1,0:T(8,128)(2,1)} %get-tuple-element.76) | copy-start | bytes 1572868
  124.8 13.3 %collective-permute-start.29 = (bf16[128,2048]{1,0:T(8,128)(2,1)S(1)}, bf16[128,2048]{1,0:T(8,128)(2,1)}, u32[]{:S(2)}, u32[]{:S(2)}) collective-permute-start(bf16[128,2048]{1,0:T(8,128)(2,1)S(1)} %add_convert_fusion.3), channel_id=1, source_target_pairs={{0,1},{1,2},{2,3},{3,0},{4,5},{5,6},{6,7},{7,4},{8,9},{9,10},{10,1... | collective-permute-start | bytes 1572872 | tf_op jit(solution)/shard_map/ppermute | solution.py:430
  137.2 16.9 %collective-permute-start.26 = (bf16[128,2048]{1,0:T(8,128)(2,1)}, bf16[128,2048]{1,0:T(8,128)(2,1)S(1)}, u32[]{:S(2)}, u32[]{:S(2)}) collective-permute-start(bf16[128,2048]{1,0:T(8,128)(2,1)} %get-tuple-element.73), channel_id=1, source_target_pairs={{0,8},{4,12},{8,0},{12,4},{1,9},{5,13},{9,1},{13,5},{2,10},{6,14},... | collective-permute-start | bytes 1572872 | tf_op jit(solution)/shard_map/ppermute | solution.py:175
  139.8 14.3 %copy-start.18 = (bf16[128,2048]{1,0:T(8,128)(2,1)S(1)}, bf16[128,2048]{1,0:T(8,128)(2,1)}, u32[]{:S(2)}) copy-start(bf16[128,2048]{1,0:T(8,128)(2,1)} %get-tuple-element.72) | copy-start | bytes 1572868
  139.8 14.3 %collective-permute-start.30 = (bf16[128,2048]{1,0:T(8,128)(2,1)S(1)}, bf16[128,2048]{1,0:T(8,128)(2,1)S(1)}, u32[]{:S(2)}, u32[]{:S(2)}) collective-permute-start(bf16[128,2048]{1,0:T(8,128)(2,1)S(1)} %add_convert_fusion.2), channel_id=1, source_target_pairs={{0,1},{1,2},{2,3},{3,0},{4,5},{5,6},{6,7},{7,4},{8,9},{9,10},{10,1... | collective-permute-start | bytes 1572872 | tf_op jit(solution)/shard_map/ppermute | solution.py:430
  152.3 14.9 %copy-start.14 = (bf16[128,2048]{1,0:T(8,128)(2,1)S(1)}, bf16[128,2048]{1,0:T(8,128)(2,1)}, u32[]{:S(2)}) copy-start(bf16[128,2048]{1,0:T(8,128)(2,1)} %get-tuple-element.69) | copy-start | bytes 1572868
  152.3 14.9 %copy-start.15 = (bf16[128,2048]{1,0:T(8,128)(2,1)S(1)}, bf16[128,2048]{1,0:T(8,128)(2,1)}, u32[]{:S(2)}) copy-start(bf16[128,2048]{1,0:T(8,128)(2,1)} %get-tuple-element.68) | copy-start | bytes 1572868
  152.3 11.8 %collective-permute-start.24 = (bf16[128,2048]{1,0:T(8,128)(2,1)}, bf16[128,2048]{1,0:T(8,128)(2,1)S(1)}, u32[]{:S(2)}, u32[]{:S(2)}) collective-permute-start(bf16[128,2048]{1,0:T(8,128)(2,1)} %get-tuple-element.70), channel_id=1, source_target_pairs={{0,8},{4,12},{8,0},{12,4},{1,9},{5,13},{9,1},{13,5},{2,10},{6,14},... | collective-permute-start | bytes 1572872 | tf_op jit(solution)/shard_map/ppermute | solution.py:175
  154.4 12.8 %collective-permute-start.31 = (bf16[128,2048]{1,0:T(8,128)(2,1)S(1)}, bf16[128,2048]{1,0:T(8,128)(2,1)S(1)}, u32[]{:S(2)}, u32[]{:S(2)}) collective-permute-start(bf16[128,2048]{1,0:T(8,128)(2,1)S(1)} %add_convert_fusion.1), channel_id=1, source_target_pairs={{0,1},{1,2},{2,3},{3,0},{4,5},{5,6},{6,7},{7,4},{8,9},{9,10},{10,1... | collective-permute-start | bytes 1572872 | tf_op jit(solution)/shard_map/ppermute | solution.py:430
  (8 other events, 24.4 us)
